TPU v7x, 256 devices: a whole 4x4x8 slice. The times are simulated.
256 devices in a mesh: gx: 8 (over x, y_lo), gy: 8 (over z), gz: 4 (over y_hi, core).
Axes of the slice: x: 4, y: 4 (y_hi: 2, y_lo: 2; y = y_hi * 2 + y_lo), z: 8, core: 2. Of those that a mesh axis runs over, the one named last changes fastest.
Arguments:
- layer_input: bfloat16 [512, 8192], P(('gy', 'gz'), 'gx'), may hold values from -3 to 3
- out_grad: bfloat16 [512, 8192], P(('gy', 'gz'), 'gx'), may hold values from -1.5 to 1.5
- gate_pre: bfloat16 [512, 29568], P('gx', ('gy', 'gz')), may hold values from -8 to 8
- up_pre: bfloat16 [512, 29568], P('gx', ('gy', 'gz')), may hold values from -6 to 6
- gate_weight: bfloat16 [8192, 29568], P('gx', ('gy', 'gz')), may hold values from -0.0625 to 0.0625
- up_weight: bfloat16 [8192, 29568], P('gx', ('gy', 'gz')), may hold values from -0.0625 to 0.0625
- down_weight: bfloat16 [29568, 8192], P(('gy', 'gz'), 'gx'), may hold values from -0.03125 to 0.03125
Outputs:
- input_grad: bfloat16 [512, 8192], P(('gy', 'gz'), 'gx')
- gate_wgrad: bfloat16 [8192, 29568], P('gx', ('gy', 'gz'))
- up_wgrad: bfloat16 [8192, 29568], P('gx', ('gy', 'gz'))
- down_wgrad: bfloat16 [29568, 8192], P(('gy', 'gz'), 'gx')
All inputs are finite; a program needn't handle non-finite values.
Results may differ from a plain program's by a relative error of at most 0.0054.
Values may be sent and summed in bfloat16 or wider, within the bound.
No kernel may reach another device: no remote copies, remote signals or barrier semaphores. Data moves between devices by JAX's collectives and lax.ppermute only.
A program may use at most 64 MiB of HBM per device.

v0:
```python
import jax
import jax.numpy as jnp
from jax import lax
from jax.sharding import PartitionSpec as P

BY_FEATURE = (((1,), (1,)), ((), ()))
BY_TOKEN = (((0,), (0,)), ((), ()))


def swiglu_back(hidden_grad, gate_pre, up_pre):
    gate = gate_pre.astype(jnp.float32)
    up_value = up_pre.astype(jnp.float32)
    sigmoid_gate = jax.nn.sigmoid(gate)
    activated = gate * sigmoid_gate
    hidden = (activated * up_value).astype(jnp.bfloat16)
    gate_grad = (
        hidden_grad * up_value * sigmoid_gate * (1.0 + gate * (1.0 - sigmoid_gate))
    ).astype(jnp.bfloat16)
    up_grad = (hidden_grad * activated).astype(jnp.bfloat16)
    return (gate_grad, up_grad, hidden)


def input_term(gate_grad, up_grad, gate_weight, up_weight):
    first = lax.dot_general(gate_grad, gate_weight, BY_FEATURE, preferred_element_type=jnp.float32)
    return first + lax.dot_general(
        up_grad, up_weight, BY_FEATURE, preferred_element_type=jnp.float32
    )


def body(layer_input, out_grad, gate_pre, up_pre, gate_weight, up_weight, down_weight):
    input_cols, grad_cols = (
        lax.all_gather(layer_input, ("gy", "gz"), axis=0, tiled=True),
        lax.all_gather(out_grad, ("gy", "gz"), axis=0, tiled=True),
    )
    partial_hidden = lax.dot_general(
        grad_cols, down_weight, BY_FEATURE, preferred_element_type=jnp.float32
    )
    hidden_grad = lax.psum(partial_hidden, "gx")
    gate_all, up_all = (
        lax.all_gather(gate_pre, "gx", axis=0, tiled=True),
        lax.all_gather(up_pre, "gx", axis=0, tiled=True),
    )
    gate_grad, up_grad, hidden = swiglu_back(hidden_grad, gate_all, up_all)
    gate_sum = lax.dot_general(input_cols, gate_grad, BY_TOKEN, preferred_element_type=jnp.float32)
    up_sum = lax.dot_general(input_cols, up_grad, BY_TOKEN, preferred_element_type=jnp.float32)
    down_sum = lax.dot_general(hidden, grad_cols, BY_TOKEN, preferred_element_type=jnp.float32)
    partial_input = input_term(gate_grad, up_grad, gate_weight, up_weight)
    input_sum = lax.psum_scatter(partial_input, ("gy", "gz"), scatter_dimension=0, tiled=True)
    return (
        input_sum.astype(jnp.bfloat16),
        gate_sum.astype(jnp.bfloat16),
        up_sum.astype(jnp.bfloat16),
        down_sum.astype(jnp.bfloat16),
    )


def solution(mesh):
    return jax.shard_map(
        body,
        mesh=mesh,
        in_specs=(
            P(("gy", "gz"), "gx"),
            P(("gy", "gz"), "gx"),
            P("gx", ("gy", "gz")),
            P("gx", ("gy", "gz")),
            P("gx", ("gy", "gz")),
            P("gx", ("gy", "gz")),
            P(("gy", "gz"), "gx"),
        ),
        out_specs=(
            P(("gy", "gz"), "gx"),
            P("gx", ("gy", "gz")),
            P("gx", ("gy", "gz")),
            P(("gy", "gz"), "gx"),
        ),
        check_vma=False,
    )
```

profile of v0, /device:TPU:8, one launch (start us, length us, event | category | flops | bytes accessed | tf_op | source)
XLA Modules:
  0.0 431.6 jit_solution(12275365256739942077)
XLA Ops:
  7.2 0.0 copy-start
  7.2 0.0 all-gather.3.cloned.1.call-start
  7.2 0.7 all-gather.3.cloned.1.call-update
  7.9 0.0 all-reduce.2.cloned.1.call-start
  8.0 82.4 %all-gather.3.cloned.1.call-done = bf16[512,1024]{1,0:T(8,128)(2,1)} async-done(((bf16[16,1024]{1,0:T(8,128)(2,1)}), bf16[512,1024]{1,0:T(8,128)(2,1)}) %all-gather.3.cloned.1.call-update) | async-done | bytes 1048592 | tf_op jit(solution)/shard_map/all_gather | solution.py:33
  90.3 4.3 fusion.10
  94.6 0.0 all-reduce.2.cloned.1.call-update
  94.6 0.0 copy-start.6
  94.6 0.0 all-gather.5.cloned.1.call-start
  94.7 0.7 all-gather.5.cloned.1.call-update
  95.4 0.0 reduce-scatter.2.cloned.1.call-start
  95.4 0.1 copy-done.5
  95.5 44.6 %all_gather.14 = bf16[512,924]{1,0:T(8,128)(2,1)S(1)} all-gather(bf16[64,924]{1,0:T(8,128)(2,1)S(1)} %copy-done.5), channel_id=1, replica_groups=mesh['gx'=8,'gy'=8,'gz'=4] {'gx'}, dimensions={0}, use_global_device_ids=true | all-gather | bytes 1064448 | tf_op jit(solution)/shard_map/all_gather | solution.py:40
  140.1 1.3 copy.14
  141.4 38.3 %all_gather.13 = bf16[512,924]{1,0:T(8,128)(2,1)S(1)} all-gather(bf16[64,924]{1,0:T(8,128)(2,1)S(1)} %copy-done.6), channel_id=1, replica_groups=mesh['gx'=8,'gy'=8,'gz'=4] {'gx'}, dimensions={0}, use_global_device_ids=true | all-gather | bytes 1064448 | tf_op jit(solution)/shard_map/all_gather | solution.py:41
  179.7 1.3 copy.13
  181.0 41.0 %all-reduce.2.cloned.1.call-done = f32[512,924]{0,1:T(8,128)} async-done(((f32[512,924]{0,1:T(8,128)}), f32[512,924]{0,1:T(8,128)}) %all-reduce.2.cloned.1.call-update) | async-done | bytes 1892368 | tf_op jit(solution)/shard_map/psum | solution.py:38
  222.0 2.8 fusion.2
  224.8 0.0 copy-done
  224.8 0.0 copy-start.1
  224.9 0.0 copy-start.7
  224.9 1.3 fusion.11
  226.2 0.5 copy-done.3
  226.7 0.6 copy-done.7
  227.2 2.7 convolution_add_fusion
  229.9 0.0 reduce-scatter.2.cloned.1.call-update
  229.9 4.4 %convolution_convert_fusion = bf16[924,1024]{1,0:T(8,128)(2,1)} fusion(bf16[512,1024]{1,0:T(8,128)(2,1)} %all-gather.3.cloned.1.call-done, bf16[512,924]{0,1:T(8,128)(2,1)} %copy.13, bf16[512,924]{0,1:T(8,128)(2,1)} %copy.14), kind=kOutput, calls=%fused_computation.16 | convolution fusion | flops 973615104 | bytes 4833280 | tf_op jit(solution)/shard_map/dot_general | solution.py:46
  234.3 68.6 %all-gather.5.cloned.1.call-done = bf16[512,1024]{1,0:T(8,128)(2,1)} async-done(((bf16[16,1024]{1,0:T(8,128)(2,1)}), bf16[512,1024]{1,0:T(8,128)(2,1)}) %all-gather.5.cloned.1.call-update) | async-done | bytes 1048592 | tf_op jit(solution)/shard_map/all_gather | solution.py:32
  302.9 3.8 convert_bitcast_fusion.1
  306.7 2.5 convert_bitcast_fusion
  309.2 114.4 %reduce-scatter.2.cloned.1.call-done = f32[16,1024]{1,0:T(8,128)} async-done(((f32[512,1024]{1,0:T(8,128)}), f32[16,1024]{1,0:T(8,128)}) %reduce-scatter.2.cloned.1.call-update) | async-done | bytes 65552 | tf_op jit(solution)/shard_map/reduce_scatter | solution.py:48
  423.6 1.5 convert_element_type.37
  (10 shorter events, 0.0 us)
Async XLA Ops:
  7.2 217.7 %copy-start = (bf16[1024,924]{0,1:T(8,128)(2,1)S(1)}, bf16[1024,924]{0,1:T(8,128)(2,1)}, u32[]{:S(2)}) copy-start(bf16[1024,924]{0,1:T(8,128)(2,1)} %param.11) | copy-start | bytes 5677060
  7.2 83.1 %all-gather.3.cloned.1.call-start = ((), (), s32[]{:S(2)}) async-start(), calls=%async_computation.1 | async-start | bytes 1081344 | tf_op jit(solution)/shard_map/all_gather | solution.py:33
  7.9 214.1 %all-reduce.2.cloned.1.call-start = ((), (), s32[]{:S(2)}) async-start(), calls=%async_computation.2 | async-start | bytes 3801088 | tf_op jit(solution)/shard_map/psum | solution.py:38
  94.6 0.9 copy-start.5
  94.6 46.7 %copy-start.6 = (bf16[64,924]{1,0:T(8,128)(2,1)S(1)}, bf16[64,924]{1,0:T(8,128)(2,1)}, u32[]{:S(2)}) copy-start(bf16[64,924]{1,0:T(8,128)(2,1)} %param.10) | copy-start | bytes 354820
  94.6 208.3 %all-gather.5.cloned.1.call-start = ((), (), s32[]{:S(2)}) async-start(), calls=%async_computation.4 | async-start | bytes 1081344 | tf_op jit(solution)/shard_map/all_gather | solution.py:32
  95.4 328.2 %reduce-scatter.2.cloned.1.call-start = ((), (), s32[]{:S(2)}) async-start(), calls=%async_computation.3 | async-start | bytes 2162688 | tf_op jit(solution)/shard_map/reduce_scatter | solution.py:48
  224.8 1.3 copy-start.1
  224.8 1.8 copy-start.3
  224.9 2.4 copy-start.7
  302.9 3.8 copy-start.2
  302.9 3.8 copy-start.4
  302.9 3.8 copy-start.8
Sparse Core Ops, SparseCore 0:
  10.8 79.4 all-gather.2
  94.8 127.1 all-reduce.1
  225.2 77.7 all-gather.4
  307.5 116.0 reduce-scatter.1
where the time goes:
time: 433 us; the launch traced here: 432 us
  waiting for transfers between devices  308 us (71%)
  blocking collectives  82.9 us (19%)
  matrix products  18.8 us (4%)
  between operations  13.8 us (3%)
    reduce_scatter x1, waiting for transfers between devices, body(): lax.psum_scatter(partial_input, ('gy', 'gz'), scatter_dimension=0, tiled=...  114 us
    all_gather x1, waiting for transfers between devices, body(): lax.all_gather(out_grad, ('gy', 'gz'), axis=0, tiled=True)  82.4 us
    all_gather x1, waiting for transfers between devices, body(): lax.all_gather(layer_input, ('gy', 'gz'), axis=0, tiled=True)  68.6 us
    all_gather x1, blocking collectives, body(): lax.all_gather(gate_pre, 'gx', axis=0, tiled=True)  44.6 us
    psum x1, waiting for transfers between devices, body(): hidden_grad = lax.psum(partial_hidden, 'gx')  41 us
    all_gather x1, blocking collectives, body(): lax.all_gather(up_pre, 'gx', axis=0, tiled=True)  38.3 us
  transfers between devices with their start and end apart: 4, of which 4 were waited for; matrix products, arithmetic and copies ran while one was open for 5% of the time, Pallas kernels for 0%

commit v1 on v0

v1 whole, which is shorter than its diff:
```python
import jax
import jax.numpy as jnp
from jax import lax
from jax.experimental import pallas as pl
from jax.experimental.pallas import tpu as pltpu
from jax.sharding import PartitionSpec as P

F32 = jnp.float32
BF16 = jnp.bfloat16
BY_FEATURE = (((1,), (1,)), ((), ()))
BY_TOKEN = (((0,), (0,)), ((), ()))
ROWS = 16
NZ = 8

OWN = ((0, 0), (0, 1), (4, 0), (4, 1))
PREV = ((-1, 0), (-1, 1), (3, 0), (3, 1))
NEXT = ((1, 0), (1, 1), (5, 0), (5, 1))
PREV2 = ((-2, 0), (-2, 1))
NEXT2 = ((2, 0), (2, 1))
ORDER = OWN + PREV + NEXT + PREV2 + NEXT2


def gy_shift(step):
    return [(i, (i + step) % NZ) for i in range(NZ)]


def place_shift(step, flip):
    return [
        (z * 4 + g, ((z + step) % NZ) * 4 + (g ^ (2 * flip))) for z in range(NZ) for g in range(4)
    ]


OTHER_CORE = [(i, i ^ 1) for i in range(4)]
OTHER_Y = [(i, i ^ 2) for i in range(4)]


def place():
    gz = lax.axis_index("gz")
    return lax.axis_index("gy"), gz // 2, gz % 2


def row_of(here, there, core):
    z, y, _ = here
    step, flip = there
    block = lax.rem(z + step + NZ, NZ) * 4 + (y + flip - 2 * y * flip) * 2 + core
    return pl.multiple_of(block * ROWS, ROWS)


def gather_core(x):
    same_z = lax.ppermute(x, "gz", OTHER_Y)
    far = lax.ppermute(x, "gy", gy_shift(4))
    far_y = lax.ppermute(x, ("gy", "gz"), place_shift(4, 1))
    near = jnp.concatenate([x, same_z], axis=0)
    four = jnp.concatenate([near, far, far_y], axis=0)
    prev = lax.ppermute(four, "gy", gy_shift(1))
    following = lax.ppermute(four, "gy", gy_shift(-1))
    prev2 = lax.ppermute(near, "gy", gy_shift(2))
    following2 = lax.ppermute(near, "gy", gy_shift(-2))
    mine = jnp.concatenate([four, prev, following, prev2, following2], axis=0)
    other = lax.ppermute(mine, "gz", OTHER_CORE)
    return mine, other


def place_kernel(mine_ref, other_ref, out_ref):
    here = place()
    core = here[2]
    for k, there in enumerate(ORDER):
        rows = pl.ds(k * ROWS, ROWS)
        out_ref[pl.ds(row_of(here, there, core), ROWS), :] = mine_ref[rows, :]
        out_ref[pl.ds(row_of(here, there, 1 - core), ROWS), :] = other_ref[rows, :]


def place_rows(mine, other):
    rows, cols = mine.shape
    return pl.pallas_call(
        place_kernel,
        out_shape=jax.ShapeDtypeStruct((2 * rows, cols), mine.dtype),
        in_specs=[pl.BlockSpec(memory_space=pltpu.VMEM)] * 2,
        out_specs=pl.BlockSpec(memory_space=pltpu.VMEM),
        compiler_params=pltpu.CompilerParams(vmem_limit_bytes=16 * 2**20),
    )(mine, other)


def send_kernel(part_ref, out_ref):
    here = place()
    for k, there in enumerate(ORDER):
        out_ref[pl.ds(k * ROWS, ROWS), :] = part_ref[
            pl.ds(row_of(here, there, 1 - here[2]), ROWS), :
        ].astype(BF16)


def fold_kernel(part_ref, recv_ref, own_ref, prev_ref, next_ref, prev2_ref, next2_ref):
    here = place()
    k = 0
    for group, ref in (
        (OWN, own_ref),
        (PREV, prev_ref),
        (NEXT, next_ref),
        (PREV2, prev2_ref),
        (NEXT2, next2_ref),
    ):
        for j, there in enumerate(group):
            total = part_ref[pl.ds(row_of(here, there, here[2]), ROWS), :] + recv_ref[
                pl.ds(k * ROWS, ROWS), :
            ].astype(F32)
            ref[pl.ds(j * ROWS, ROWS), :] = total.astype(ref.dtype)
            k += 1


def scatter_rows(part):
    rows, cols = part.shape
    vmem = pl.BlockSpec(memory_space=pltpu.VMEM)
    params = pltpu.CompilerParams(vmem_limit_bytes=16 * 2**20)
    send = pl.pallas_call(
        send_kernel,
        out_shape=jax.ShapeDtypeStruct((rows // 2, cols), BF16),
        in_specs=[vmem],
        out_specs=vmem,
        compiler_params=params,
    )(part)
    recv = lax.ppermute(send, "gz", OTHER_CORE)
    own, prev, following, prev2, following2 = pl.pallas_call(
        fold_kernel,
        out_shape=(
            jax.ShapeDtypeStruct((64, cols), F32),
            jax.ShapeDtypeStruct((64, cols), BF16),
            jax.ShapeDtypeStruct((64, cols), BF16),
            jax.ShapeDtypeStruct((32, cols), BF16),
            jax.ShapeDtypeStruct((32, cols), BF16),
        ),
        in_specs=[vmem] * 2,
        out_specs=(vmem,) * 5,
        compiler_params=params,
    )(part, recv)
    from_next = lax.ppermute(prev, "gy", gy_shift(-1))
    from_prev = lax.ppermute(following, "gy", gy_shift(1))
    from_next2 = lax.ppermute(prev2, "gy", gy_shift(-2))
    from_prev2 = lax.ppermute(following2, "gy", gy_shift(2))
    total = own + from_next.astype(F32) + from_prev.astype(F32)
    near = total[:32] + from_next2.astype(F32) + from_prev2.astype(F32)
    far = total[32:].astype(BF16)
    got = (
        lax.ppermute(near[16:].astype(BF16), "gz", OTHER_Y),
        lax.ppermute(far[:16], "gy", gy_shift(4)),
        lax.ppermute(far[16:], ("gy", "gz"), place_shift(4, 1)),
    )
    return near[:16] + got[0].astype(F32) + got[1].astype(F32) + got[2].astype(F32)


def body(layer_input, out_grad, gate_pre, up_pre, gate_weight, up_weight, down_weight):
    pre = lax.all_gather(jnp.stack([gate_pre, up_pre]), "gx", axis=0)
    grad_cols = place_rows(*gather_core(out_grad))
    part = lax.dot_general(grad_cols, down_weight, BY_FEATURE, preferred_element_type=F32)
    tokens, units = part.shape
    block = tokens // 8
    parts = lax.all_to_all(part.astype(BF16).reshape(8, block, units), "gx", 0, 0)
    mine = jnp.sum(parts.astype(F32), axis=0).astype(BF16)
    hidden_grad = lax.all_to_all(jnp.broadcast_to(mine[None], (8, block, units)), "gx", 0, 0)
    hidden_grad = hidden_grad.reshape(tokens, units).astype(F32)
    gate = pre[:, 0].reshape(tokens, units).astype(F32)
    up_value = pre[:, 1].reshape(tokens, units).astype(F32)
    sigmoid_gate = jax.nn.sigmoid(gate)
    activated = gate * sigmoid_gate
    hidden = (activated * up_value).astype(BF16)
    gate_grad = (
        hidden_grad * up_value * sigmoid_gate * (1.0 + gate * (1.0 - sigmoid_gate))
    ).astype(BF16)
    up_grad = (hidden_grad * activated).astype(BF16)
    part_in = lax.dot_general(gate_grad, gate_weight, BY_FEATURE, preferred_element_type=F32)
    part_in = part_in + lax.dot_general(
        up_grad, up_weight, BY_FEATURE, preferred_element_type=F32
    )
    input_sum = scatter_rows(part_in)
    input_cols = place_rows(*gather_core(layer_input))
    gate_sum = lax.dot_general(input_cols, gate_grad, BY_TOKEN, preferred_element_type=F32)
    up_sum = lax.dot_general(input_cols, up_grad, BY_TOKEN, preferred_element_type=F32)
    down_sum = lax.dot_general(hidden, grad_cols, BY_TOKEN, preferred_element_type=F32)
    return (
        input_sum.astype(BF16),
        gate_sum.astype(BF16),
        up_sum.astype(BF16),
        down_sum.astype(BF16),
    )


def solution(mesh):
    tokens = P(("gy", "gz"), "gx")
    hidden = P("gx", ("gy", "gz"))
    return jax.shard_map(
        body,
        mesh=mesh,
        in_specs=(tokens, tokens, hidden, hidden, hidden, hidden, tokens),
        out_specs=(tokens, hidden, hidden, tokens),
        check_vma=False,
    )
```

time: 433 us -> 150 us (0.35)
  waiting for transfers between devices: 308 us -> 41.7 us
  blocking collectives: 82.9 us -> 0 us
  starting transfers between devices: 0.16 us -> 58.8 us
  local copies, waits for them, and re-layouts: 3.79 us -> 11.9 us
  matrix products: 18.8 us -> 12.1 us
    all_gather x2 -> x1, waiting for transfers between devices: 151 us -> 0.02 us  [body(): pre = lax.all_gather(jnp.stack([gate_pre, up_pre]), 'gx', axis=0)]
    reduce_scatter x1 -> x0, waiting for transfers between devices: 114 us -> none  [body(): lax.psum_scatter(partial_input, ('gy', 'gz'), scatter_dimension=0, tiled=...]
    all_gather x2 -> x0, blocking collectives: 82.9 us -> none  [the longest x1 44.6 us: body(): lax.all_gather(gate_pre, 'gx', axis=0, tiled=True)]
    ppermute x0 -> x24, starting transfers between devices: none -> 45.9 us  [the longest x2 11.1 us: gather_core(): far = lax.ppermute(x, 'gy', gy_shift(4))]
    psum x1 -> x0, waiting for transfers between devices: 41 us -> none  [body(): hidden_grad = lax.psum(partial_hidden, 'gx')]
    ppermute x0 -> x24, waiting for transfers between devices: none -> 39.9 us  [the longest x2 14.5 us: gather_core(): same_z = lax.ppermute(x, 'gz', OTHER_Y)]
    all_to_all x0 -> x2, starting transfers between devices: none -> 12.9 us  [the longest x1 6.74 us: body(): lax.all_to_all(jnp.broadcast_to(mine[None], (8, block, units)), 'gx', 0, 0)]
    dot_general x5, matrix products: 14.6 us -> 9.94 us  [the longest x1 2.5 us: body(): lax.dot_general(hidden, grad_cols, BY_TOKEN, preferred_element_type=F32)]
  transfers between devices with their start and end apart: 4 -> 27, of which waited for: 4 -> 13; matrix products, arithmetic and copies ran while one was open for 5% -> 20% of each run, Pallas kernels for 0% -> 1%
where the time goes in v1:
time: 150 us; the launch traced here: 148 us
  starting transfers between devices  58.8 us (39%)
  waiting for transfers between devices  41.7 us (28%)
  between operations  14.3 us (10%)
  matrix products  12.1 us (8%)
  local copies, waits for them, and re-layouts  11.9 us (8%)
  other arithmetic  7.66 us (5%)
  Pallas kernels  1.5 us (1%)
    ppermute x2, waiting for transfers between devices, gather_core(): same_z = lax.ppermute(x, 'gz', OTHER_Y)  14.5 us
    ppermute x2, starting transfers between devices, gather_core(): far = lax.ppermute(x, 'gy', gy_shift(4))  11.1 us
    ppermute x2, waiting for transfers between devices, gather_core(): far_y = lax.ppermute(x, ('gy', 'gz'), place_shift(4, 1))  7.18 us
    all_to_all x1, starting transfers between devices, body(): lax.all_to_all(jnp.broadcast_to(mine[None], (8, block, units)), 'gx', 0, 0)  6.74 us
    all_to_all x1, starting transfers between devices, body(): lax.all_to_all(part.astype(BF16).reshape(8, block, units), 'gx', 0, 0)  6.14 us
    ppermute x2, waiting for transfers between devices, gather_core(): prev2 = lax.ppermute(near, 'gy', gy_shift(2))  5.25 us
    ppermute x2, starting transfers between devices, gather_core(): prev2 = lax.ppermute(near, 'gy', gy_shift(2))  5.22 us
    ppermute x2, starting transfers between devices, gather_core(): far_y = lax.ppermute(x, ('gy', 'gz'), place_shift(4, 1))  4.63 us
  transfers between devices with their start and end apart: 27, of which 13 were waited for; matrix products, arithmetic and copies ran while one was open for 20% of the time, Pallas kernels for 1%

profile of v1, /device:TPU:8, one launch (start us, length us, event | category | flops | bytes accessed | tf_op | source)
XLA Modules:
  0.0 148.0 jit_solution(794997140387202376)
XLA Ops:
  7.2 1.8 %pad_maximum_fusion = bf16[2,64,924]{2,1,0:T(8,128)(2,1)} fusion(bf16[1,64,924]{2,1,0:T(8,128)(2,1)} %bitcast.31, bf16[1,64,924]{2,1,0:T(8,128)(2,1)} %bitcast.32), kind=kLoop, calls=%fused_computation.20 | loop fusion | flops 118272 | bytes 473088 | tf_op jit(solution)/shard_map/stack | solution.py:151
  9.1 7.3 %collective-permute-start.1 = (bf16[16,1024]{1,0:T(8,128)(2,1)}, bf16[16,1024]{1,0:T(8,128)(2,1)S(1)}, u32[]{:S(2)}, u32[]{:S(2)}) collective-permute-start(bf16[16,1024]{1,0:T(8,128)(2,1)} %param.8), channel_id=1, source_target_pairs={{0,16},{4,20},{8,24},{12,28},{16,0},{20,4},{24,8},{28,12},{1,17},{... | collective-permute-start | bytes 98312 | tf_op jit(solution)/shard_map/ppermute | solution.py:51
  16.4 2.3 %collective-permute-start = (bf16[16,1024]{1,0:T(8,128)(2,1)}, bf16[16,1024]{1,0:T(8,128)(2,1)S(1)}, u32[]{:S(2)}, u32[]{:S(2)}) collective-permute-start(bf16[16,1024]{1,0:T(8,128)(2,1)} %param.8), channel_id=1, source_target_pairs={{0,2},{1,3},{2,0},{3,1},{4,6},{5,7},{6,4},{7,5},{8,10},{9,11},{10,... | collective-permute-start | bytes 98312 | tf_op jit(solution)/shard_map/ppermute | solution.py:50
  20.2 1.8 %collective-permute-done = bf16[16,1024]{1,0:T(8,128)(2,1)S(1)} collective-permute-done((bf16[16,1024]{1,0:T(8,128)(2,1)}, bf16[16,1024]{1,0:T(8,128)(2,1)S(1)}, u32[]{:S(2)}, u32[]{:S(2)}) %collective-permute-start) | collective-permute-done | bytes 32800 | tf_op jit(solution)/shard_map/ppermute | solution.py:50
  22.0 7.2 %collective-permute-done.2 = bf16[16,1024]{1,0:T(8,128)(2,1)S(1)} collective-permute-done((bf16[16,1024]{1,0:T(8,128)(2,1)}, bf16[16,1024]{1,0:T(8,128)(2,1)S(1)}, u32[]{:S(2)}, u32[]{:S(2)}) %collective-permute-start.2) | collective-permute-done | bytes 32800 | tf_op jit(solution)/shard_map/ppermute | solution.py:52
  30.2 2.2 %collective-permute-start.4 = (bf16[64,1024]{1,0:T(8,128)(2,1)S(1)}, bf16[64,1024]{1,0:T(8,128)(2,1)S(1)}, u32[]{:S(2)}, u32[]{:S(2)}) collective-permute-start(bf16[64,1024]{1,0:T(8,128)(2,1)S(1)} %get-tuple-element.39), channel_id=1, source_target_pairs={{0,28},{4,0},{8,4},{12,8},{16,12},{20,16},{24,20},{28,24},{1,29},{... | collective-permute-start | bytes 393224 | tf_op jit(solution)/shard_map/ppermute | solution.py:56
  32.5 2.9 %collective-permute-start.5 = (bf16[32,1024]{1,0:T(8,128)(2,1)S(1)}, bf16[32,1024]{1,0:T(8,128)(2,1)S(1)}, u32[]{:S(2)}, u32[]{:S(2)}) collective-permute-start(bf16[32,1024]{1,0:T(8,128)(2,1)S(1)} %get-tuple-element.33), channel_id=1, source_target_pairs={{0,8},{4,12},{8,16},{12,20},{16,24},{20,28},{24,0},{28,4},{1,9},{5... | collective-permute-start | bytes 196616 | tf_op jit(solution)/shard_map/ppermute | solution.py:57
  36.8 2.1 %collective-permute-done.5 = bf16[32,1024]{1,0:T(8,128)(2,1)S(1)} collective-permute-done((bf16[32,1024]{1,0:T(8,128)(2,1)S(1)}, bf16[32,1024]{1,0:T(8,128)(2,1)S(1)}, u32[]{:S(2)}, u32[]{:S(2)}) %collective-permute-start.5) | collective-permute-done | bytes 65568 | tf_op jit(solution)/shard_map/ppermute | solution.py:57
  39.0 1.9 %collective-permute-done.7.other_ref = bf16[256,1024]{1,0:T(8,128)(2,1)S(1)} collective-permute-done((bf16[256,1024]{1,0:T(8,128)(2,1)S(1)}, bf16[256,1024]{1,0:T(8,128)(2,1)S(1)}, u32[]{:S(2)}, u32[]{:S(2)}) %collective-permute-start.7) | collective-permute-done | bytes 524320 | tf_op jit(solution)/shard_map/ppermute | solution.py:60
  41.0 2.1 %convolution_convert_fusion.3 = bf16[512,924]{0,1:T(8,128)(2,1)} fusion(bf16[512,1024]{1,0:T(8,128)(2,1)S(1)} %shard_map.102, bf16[924,1024]{1,0:T(8,128)(2,1)S(1)} %copy-done.5), kind=kOutput, calls=%fused_computation.19 | convolution fusion | flops 969357312 | bytes 3887104 | tf_op jit(solution)/shard_map/dot_general | solution.py:153
  43.2 2.3 %copy.12 = bf16[512,924]{1,0:T(8,128)(2,1)} copy(bf16[512,924]{0,1:T(8,128)(2,1)} %convolution_convert_fusion.3) | data formatting | bytes 1892352 | tf_op jit(solution)/shard_map/convert_element_type | solution.py:156
  45.4 6.1 %all-to-all-start = ((bf16[8,64,924]{2,1,0:T(8,128)(2,1)}), bf16[8,64,924]{2,1,0:T(8,128)(2,1)}, u32[]{:S(2)}, u32[]{:S(2)}) async-start(bf16[8,64,924]{2,1,0:T(8,128)(2,1)} %bitcast.28), calls=%async_computation | async-start | bytes 2097152 | tf_op jit(solution)/shard_map/all_to_all | solution.py:156
  51.6 3.8 %collective-permute-start.17 = (bf16[16,1024]{1,0:T(8,128)(2,1)S(1)}, bf16[16,1024]{1,0:T(8,128)(2,1)S(1)}, u32[]{:S(2)}, u32[]{:S(2)}) collective-permute-start(bf16[16,1024]{1,0:T(8,128)(2,1)S(1)} %copy-done.2), channel_id=1, source_target_pairs={{0,16},{4,20},{8,24},{12,28},{16,0},{20,4},{24,8},{28,12},{1,17},{... | collective-permute-start | bytes 98312 | tf_op jit(solution)/shard_map/ppermute | solution.py:51
  56.6 3.9 %collective-permute-start.18 = (bf16[16,1024]{1,0:T(8,128)(2,1)S(1)}, bf16[16,1024]{1,0:T(8,128)(2,1)S(1)}, u32[]{:S(2)}, u32[]{:S(2)}) collective-permute-start(bf16[16,1024]{1,0:T(8,128)(2,1)S(1)} %copy-done.2), channel_id=1, source_target_pairs={{0,18},{1,19},{2,16},{3,17},{4,22},{5,23},{6,20},{7,21},{8,26},{9,... | collective-permute-start | bytes 98312 | tf_op jit(solution)/shard_map/ppermute | solution.py:52
  61.1 12.7 %collective-permute-done.16 = bf16[16,1024]{1,0:T(8,128)(2,1)S(1)} collective-permute-done((bf16[16,1024]{1,0:T(8,128)(2,1)S(1)}, bf16[16,1024]{1,0:T(8,128)(2,1)S(1)}, u32[]{:S(2)}, u32[]{:S(2)}) %collective-permute-start.16) | collective-permute-done | bytes 32800 | tf_op jit(solution)/shard_map/ppermute | solution.py:50
  77.1 2.1 %reduce_sum.12 = bf16[64,924]{1,0:T(8,128)(2,1)} reduce(bf16[8,64,924]{2,1,0:T(8,128)(2,1)} %all-to-all-done, bf16[]{:T(256)} %constant.1.clone.1), dimensions={0}, to_apply=%region_0.0 | reduce | flops 413952 | bytes 1064450 | tf_op jit(solution)/shard_map/reduce_sum | solution.py:157
  79.2 2.0 %broadcast_in_dim.2 = bf16[8,64,924]{2,1,0:T(8,128)(2,1)} broadcast(bf16[64,924]{1,0:T(8,128)(2,1)} %reduce_sum.12), dimensions={1,2} | broadcast | bytes 1064448 | tf_op jit(solution)/shard_map/broadcast_in_dim | solution.py:158
  81.2 6.7 %all-to-all-start.1 = ((bf16[8,64,924]{2,1,0:T(8,128)(2,1)}), bf16[8,64,924]{2,1,0:T(8,128)(2,1)}, u32[]{:S(2)}, u32[]{:S(2)}) async-start(bf16[8,64,924]{2,1,0:T(8,128)(2,1)} %broadcast_in_dim.2), calls=%async_computation.1 | async-start | bytes 2097152 | tf_op jit(solution)/shard_map/all_to_all | solution.py:158
  87.9 1.9 %collective-permute-start.20 = (bf16[64,1024]{1,0:T(8,128)(2,1)}, bf16[64,1024]{1,0:T(8,128)(2,1)S(1)}, u32[]{:S(2)}, u32[]{:S(2)}) collective-permute-start(bf16[64,1024]{1,0:T(8,128)(2,1)} %get-tuple-element.29), channel_id=1, source_target_pairs={{0,28},{4,0},{8,4},{12,8},{16,12},{20,16},{24,20},{28,24},{1,29},{... | collective-permute-start | bytes 393224 | tf_op jit(solution)/shard_map/ppermute | solution.py:56
  90.4 2.3 %collective-permute-start.21 = (bf16[32,1024]{1,0:T(8,128)(2,1)S(1)}, bf16[32,1024]{1,0:T(8,128)(2,1)S(1)}, u32[]{:S(2)}, u32[]{:S(2)}) collective-permute-start(bf16[32,1024]{1,0:T(8,128)(2,1)S(1)} %copy-done.4), channel_id=1, source_target_pairs={{0,8},{4,12},{8,16},{12,20},{16,24},{20,28},{24,0},{28,4},{1,9},{5... | collective-permute-start | bytes 196616 | tf_op jit(solution)/shard_map/ppermute | solution.py:57
  94.3 3.2 %collective-permute-done.21 = bf16[32,1024]{1,0:T(8,128)(2,1)S(1)} collective-permute-done((bf16[32,1024]{1,0:T(8,128)(2,1)S(1)}, bf16[32,1024]{1,0:T(8,128)(2,1)S(1)}, u32[]{:S(2)}, u32[]{:S(2)}) %collective-permute-start.21) | collective-permute-done | bytes 65568 | tf_op jit(solution)/shard_map/ppermute | solution.py:57
  97.7 3.1 %fusion.15 = (bf16[8,1,64,924]{3,2,1,0:T(8,128)(2,1)}, bf16[8,1,64,924]{3,2,1,0:T(8,128)(2,1)}) fusion(bf16[8,2,64,924]{3,2,1,0:T(8,128)(2,1)} %bitcast.30), kind=kLoop, calls=%fused_computation.58 | loop fusion | bytes 3784704 | tf_op jit(solution)/shard_map/slice | solution.py:160
  102.5 3.0 %fusion = (bf16[512,924]{1,0:T(8,128)(2,1)S(1)}, bf16[512,924]{1,0:T(8,128)(2,1)S(1)}, f32[512,924]{1,0:T(8,128)S(1)}) fusion(bf16[8,64,924]{2,1,0:T(8,128)(2,1)} %all-to-all-done.1, bf16[8,1,64,924]{3,2,1,0:T(8,128)(2,1)} %get-tuple-element.18, bf16[8,1,64,924]{3,2,1,0:T(8,128)(2,1)} %get-tuple-element.19), kind=kLoop, calls=%fused_computation.6 | loop fusion | flops 7569408 | bytes 6623232 | tf_op jit(solution)/shard_map/convert_element_type | solution.py:168
  109.8 2.5 %convolution_convert_fusion = bf16[924,1024]{1,0:T(8,128)(2,1)} fusion(bf16[512,1024]{1,0:T(8,128)(2,1)S(1)} %shard_map.102, f32[512,924]{1,0:T(8,128)S(1)} %get-tuple-element.20, bf16[512,924]{1,0:T(8,128)(2,1)S(1)} %bitcast.29), kind=kOutput, calls=%fused_computation.15 | convolution fusion | flops 971249664 | bytes 5779456 | tf_op jit(solution)/shard_map/dot_general | solution.py:177
  112.4 2.0 %collective-permute-start.9 = (bf16[64,1024]{1,0:T(8,128)(2,1)S(1)}, bf16[64,1024]{1,0:T(8,128)(2,1)S(1)}, u32[]{:S(2)}, u32[]{:S(2)}) collective-permute-start(bf16[64,1024]{1,0:T(8,128)(2,1)S(1)} %get-tuple-element.10), channel_id=1, source_target_pairs={{0,28},{4,0},{8,4},{12,8},{16,12},{20,16},{24,20},{28,24},{1,29},{... | collective-permute-start | bytes 393224 | tf_op jit(solution)/shard_map/ppermute | solution.py:135
  114.6 2.5 %convolution_convert_fusion.1 = bf16[1024,924]{0,1:T(8,128)(2,1)} fusion(bf16[512,1024]{1,0:T(8,128)(2,1)S(1)} %shard_map.105, bf16[512,924]{1,0:T(8,128)(2,1)S(1)} %get-tuple-element.16), kind=kOutput, calls=%fused_computation.16 | convolution fusion | flops 969830400 | bytes 3887104 | tf_op jit(solution)/shard_map/dot_general | solution.py:176
  121.2 1.9 %collective-permute-done.11 = bf16[32,1024]{1,0:T(8,128)(2,1)S(1)} collective-permute-done((bf16[32,1024]{1,0:T(8,128)(2,1)S(1)}, bf16[32,1024]{1,0:T(8,128)(2,1)S(1)}, u32[]{:S(2)}, u32[]{:S(2)}) %collective-permute-start.11) | collective-permute-done | bytes 65568 | tf_op jit(solution)/shard_map/ppermute | solution.py:137
  123.1 2.5 %collective-permute-done.12 = bf16[32,1024]{1,0:T(8,128)(2,1)S(1)} collective-permute-done((bf16[32,1024]{1,0:T(8,128)(2,1)S(1)}, bf16[32,1024]{1,0:T(8,128)(2,1)S(1)}, u32[]{:S(2)}, u32[]{:S(2)}) %collective-permute-start.12) | collective-permute-done | bytes 65568 | tf_op jit(solution)/shard_map/ppermute | solution.py:138
  126.9 3.3 %collective-permute-start.14 = (bf16[16,1024]{1,0:T(8,128)(2,1)S(1)}, bf16[16,1024]{1,0:T(8,128)(2,1)S(1)}, u32[]{:S(2)}, u32[]{:S(2)}) collective-permute-start(bf16[16,1024]{1,0:T(8,128)(2,1)S(1)} %get-tuple-element.21), channel_id=1, source_target_pairs={{0,16},{4,20},{8,24},{12,28},{16,0},{20,4},{24,8},{28,12},{1,17},{... | collective-permute-start | bytes 98312 | tf_op jit(solution)/shard_map/ppermute | solution.py:144
  130.2 4.4 %collective-permute-start.15 = (bf16[16,1024]{1,0:T(8,128)(2,1)S(1)}, bf16[16,1024]{1,0:T(8,128)(2,1)S(1)}, u32[]{:S(2)}, u32[]{:S(2)}) collective-permute-start(bf16[16,1024]{1,0:T(8,128)(2,1)S(1)} %get-tuple-element.22), channel_id=1, source_target_pairs={{0,18},{1,19},{2,16},{3,17},{4,22},{5,23},{6,20},{7,21},{8,26},{9,... | collective-permute-start | bytes 98312 | tf_op jit(solution)/shard_map/ppermute | solution.py:145
  134.6 2.5 %convolution_convert_fusion.2 = bf16[1024,924]{0,1:T(8,128)(2,1)} fusion(bf16[512,1024]{1,0:T(8,128)(2,1)S(1)} %shard_map.105, bf16[512,924]{1,0:T(8,128)(2,1)S(1)} %get-tuple-element.17), kind=kOutput, calls=%fused_computation.17 | convolution fusion | flops 969830400 | bytes 3887104 | tf_op jit(solution)/shard_map/dot_general | solution.py:175
  137.1 3.4 %collective-permute-done.15 = bf16[16,1024]{1,0:T(8,128)(2,1)S(1)} collective-permute-done((bf16[16,1024]{1,0:T(8,128)(2,1)S(1)}, bf16[16,1024]{1,0:T(8,128)(2,1)S(1)}, u32[]{:S(2)}, u32[]{:S(2)}) %collective-permute-start.15) | collective-permute-done | bytes 32800 | tf_op jit(solution)/shard_map/ppermute | solution.py:145
  (74 shorter events, 24.1 us)
Async XLA Ops:
  7.2 98.4 %copy-start = (bf16[1024,924]{0,1:T(8,128)(2,1)S(1)}, bf16[1024,924]{0,1:T(8,128)(2,1)}, u32[]{:S(2)}) copy-start(bf16[1024,924]{0,1:T(8,128)(2,1)} %param.11) | copy-start | bytes 5677060
  7.2 90.5 %all-gather.3.cloned.1.call-start = ((), (), s32[]{:S(2)}) async-start(), calls=%async_computation.2 | async-start | bytes 2359296 | tf_op jit(solution)/shard_map/all_gather | solution.py:151
  9.1 31.9 %copy-start.5 = (bf16[924,1024]{1,0:T(8,128)(2,1)S(1)}, bf16[924,1024]{1,0:T(8,128)(2,1)}, u32[]{:S(2)}) copy-start(bf16[924,1024]{1,0:T(8,128)(2,1)} %param.13) | copy-start | bytes 5677060
  9.1 12.9 %collective-permute-start.1 = (bf16[16,1024]{1,0:T(8,128)(2,1)}, bf16[16,1024]{1,0:T(8,128)(2,1)S(1)}, u32[]{:S(2)}, u32[]{:S(2)}) collective-permute-start(bf16[16,1024]{1,0:T(8,128)(2,1)} %param.8), channel_id=1, source_target_pairs={{0,16},{4,20},{8,24},{12,28},{16,0},{20,4},{24,8},{28,12},{1,17},{... | collective-permute-start | bytes 98312 | tf_op jit(solution)/shard_map/ppermute | solution.py:51
  16.4 5.6 %collective-permute-start = (bf16[16,1024]{1,0:T(8,128)(2,1)}, bf16[16,1024]{1,0:T(8,128)(2,1)S(1)}, u32[]{:S(2)}, u32[]{:S(2)}) collective-permute-start(bf16[16,1024]{1,0:T(8,128)(2,1)} %param.8), channel_id=1, source_target_pairs={{0,2},{1,3},{2,0},{3,1},{4,6},{5,7},{6,4},{7,5},{8,10},{9,11},{10,... | collective-permute-start | bytes 98312 | tf_op jit(solution)/shard_map/ppermute | solution.py:50
  18.7 10.5 %collective-permute-start.2 = (bf16[16,1024]{1,0:T(8,128)(2,1)}, bf16[16,1024]{1,0:T(8,128)(2,1)S(1)}, u32[]{:S(2)}, u32[]{:S(2)}) collective-permute-start(bf16[16,1024]{1,0:T(8,128)(2,1)} %param.8), channel_id=1, source_target_pairs={{0,18},{1,19},{2,16},{3,17},{4,22},{5,23},{6,20},{7,21},{8,26},{9,... | collective-permute-start | bytes 98312 | tf_op jit(solution)/shard_map/ppermute | solution.py:52
  29.2 7.6 %collective-permute-start.3 = (bf16[64,1024]{1,0:T(8,128)(2,1)S(1)}, bf16[64,1024]{1,0:T(8,128)(2,1)S(1)}, u32[]{:S(2)}, u32[]{:S(2)}) collective-permute-start(bf16[64,1024]{1,0:T(8,128)(2,1)S(1)} %get-tuple-element.39), channel_id=1, source_target_pairs={{0,4},{4,8},{8,12},{12,16},{16,20},{20,24},{24,28},{28,0},{1,5},{5... | collective-permute-start | bytes 393224 | tf_op jit(solution)/shard_map/ppermute | solution.py:55
  30.2 6.6 %collective-permute-start.4 = (bf16[64,1024]{1,0:T(8,128)(2,1)S(1)}, bf16[64,1024]{1,0:T(8,128)(2,1)S(1)}, u32[]{:S(2)}, u32[]{:S(2)}) collective-permute-start(bf16[64,1024]{1,0:T(8,128)(2,1)S(1)} %get-tuple-element.39), channel_id=1, source_target_pairs={{0,28},{4,0},{8,4},{12,8},{16,12},{20,16},{24,20},{28,24},{1,29},{... | collective-permute-start | bytes 393224 | tf_op jit(solution)/shard_map/ppermute | solution.py:56
  32.5 6.5 %collective-permute-start.6 = (bf16[32,1024]{1,0:T(8,128)(2,1)S(1)}, bf16[32,1024]{1,0:T(8,128)(2,1)S(1)}, u32[]{:S(2)}, u32[]{:S(2)}) collective-permute-start(bf16[32,1024]{1,0:T(8,128)(2,1)S(1)} %get-tuple-element.33), channel_id=1, source_target_pairs={{0,24},{4,28},{8,0},{12,4},{16,8},{20,12},{24,16},{28,20},{1,25},{... | collective-permute-start | bytes 196616 | tf_op jit(solution)/shard_map/ppermute | solution.py:58
  32.5 6.5 %collective-permute-start.5 = (bf16[32,1024]{1,0:T(8,128)(2,1)S(1)}, bf16[32,1024]{1,0:T(8,128)(2,1)S(1)}, u32[]{:S(2)}, u32[]{:S(2)}) collective-permute-start(bf16[32,1024]{1,0:T(8,128)(2,1)S(1)} %get-tuple-element.33), channel_id=1, source_target_pairs={{0,8},{4,12},{8,16},{12,20},{16,24},{20,28},{24,0},{28,4},{1,9},{5... | collective-permute-start | bytes 196616 | tf_op jit(solution)/shard_map/ppermute | solution.py:57
  38.9 2.0 %collective-permute-start.7 = (bf16[256,1024]{1,0:T(8,128)(2,1)S(1)}, bf16[256,1024]{1,0:T(8,128)(2,1)S(1)}, u32[]{:S(2)}, u32[]{:S(2)}) collective-permute-start(bf16[256,1024]{1,0:T(8,128)(2,1)S(1)} %constant_dynamic-update-slice_fusion.6.mine_ref), channel_id=1, source_target_pairs={{0,1},{1,0},{2,3},{3,2},{4,5},{5,4},{6,7},{7,6},{8,9},{9,8},{10,11... | collective-permute-start | bytes 1572872 | tf_op jit(solution)/shard_map/ppermute | solution.py:60
  43.1 8.4 %copy-start.2 = (bf16[16,1024]{1,0:T(8,128)(2,1)S(1)}, bf16[16,1024]{1,0:T(8,128)(2,1)}, u32[]{:S(2)}) copy-start(bf16[16,1024]{1,0:T(8,128)(2,1)} %param.7) | copy-start | bytes 98308
  45.4 31.6 %all-to-all-start = ((bf16[8,64,924]{2,1,0:T(8,128)(2,1)}), bf16[8,64,924]{2,1,0:T(8,128)(2,1)}, u32[]{:S(2)}, u32[]{:S(2)}) async-start(bf16[8,64,924]{2,1,0:T(8,128)(2,1)} %bitcast.28), calls=%async_computation | async-start | bytes 2097152 | tf_op jit(solution)/shard_map/all_to_all | solution.py:156
  51.6 22.9 %collective-permute-start.17 = (bf16[16,1024]{1,0:T(8,128)(2,1)S(1)}, bf16[16,1024]{1,0:T(8,128)(2,1)S(1)}, u32[]{:S(2)}, u32[]{:S(2)}) collective-permute-start(bf16[16,1024]{1,0:T(8,128)(2,1)S(1)} %copy-done.2), channel_id=1, source_target_pairs={{0,16},{4,20},{8,24},{12,28},{16,0},{20,4},{24,8},{28,12},{1,17},{... | collective-permute-start | bytes 98312 | tf_op jit(solution)/shard_map/ppermute | solution.py:51
  55.4 18.4 %collective-permute-start.16 = (bf16[16,1024]{1,0:T(8,128)(2,1)S(1)}, bf16[16,1024]{1,0:T(8,128)(2,1)S(1)}, u32[]{:S(2)}, u32[]{:S(2)}) collective-permute-start(bf16[16,1024]{1,0:T(8,128)(2,1)S(1)} %copy-done.2), channel_id=1, source_target_pairs={{0,2},{1,3},{2,0},{3,1},{4,6},{5,7},{6,4},{7,5},{8,10},{9,11},{10,... | collective-permute-start | bytes 98312 | tf_op jit(solution)/shard_map/ppermute | solution.py:50
  56.6 18.5 %collective-permute-start.18 = (bf16[16,1024]{1,0:T(8,128)(2,1)S(1)}, bf16[16,1024]{1,0:T(8,128)(2,1)S(1)}, u32[]{:S(2)}, u32[]{:S(2)}) collective-permute-start(bf16[16,1024]{1,0:T(8,128)(2,1)S(1)} %copy-done.2), channel_id=1, source_target_pairs={{0,18},{1,19},{2,16},{3,17},{4,22},{5,23},{6,20},{7,21},{8,26},{9,... | collective-permute-start | bytes 98312 | tf_op jit(solution)/shard_map/ppermute | solution.py:52
  75.7 14.1 %copy-start.4 = (bf16[32,1024]{1,0:T(8,128)(2,1)S(1)}, bf16[32,1024]{1,0:T(8,128)(2,1)}, u32[]{:S(2)}) copy-start(bf16[32,1024]{1,0:T(8,128)(2,1)} %copy-done.3) | copy-start | bytes 196612
  75.7 17.0 %collective-permute-start.19 = (bf16[64,1024]{1,0:T(8,128)(2,1)}, bf16[64,1024]{1,0:T(8,128)(2,1)}, u32[]{:S(2)}, u32[]{:S(2)}) collective-permute-start(bf16[64,1024]{1,0:T(8,128)(2,1)} %get-tuple-element.29), channel_id=1, source_target_pairs={{0,4},{4,8},{8,12},{12,16},{16,20},{20,24},{24,28},{28,0},{1,5},{5... | collective-permute-start | bytes 393224 | tf_op jit(solution)/shard_map/ppermute | solution.py:55
  81.2 21.3 %all-to-all-start.1 = ((bf16[8,64,924]{2,1,0:T(8,128)(2,1)}), bf16[8,64,924]{2,1,0:T(8,128)(2,1)}, u32[]{:S(2)}, u32[]{:S(2)}) async-start(bf16[8,64,924]{2,1,0:T(8,128)(2,1)} %broadcast_in_dim.2), calls=%async_computation.1 | async-start | bytes 2097152 | tf_op jit(solution)/shard_map/all_to_all | solution.py:158
  87.9 6.4 %collective-permute-start.20 = (bf16[64,1024]{1,0:T(8,128)(2,1)}, bf16[64,1024]{1,0:T(8,128)(2,1)S(1)}, u32[]{:S(2)}, u32[]{:S(2)}) collective-permute-start(bf16[64,1024]{1,0:T(8,128)(2,1)} %get-tuple-element.29), channel_id=1, source_target_pairs={{0,28},{4,0},{8,4},{12,8},{16,12},{20,16},{24,20},{28,24},{1,29},{... | collective-permute-start | bytes 393224 | tf_op jit(solution)/shard_map/ppermute | solution.py:56
  89.8 7.7 %collective-permute-start.22 = (bf16[32,1024]{1,0:T(8,128)(2,1)S(1)}, bf16[32,1024]{1,0:T(8,128)(2,1)S(1)}, u32[]{:S(2)}, u32[]{:S(2)}) collective-permute-start(bf16[32,1024]{1,0:T(8,128)(2,1)S(1)} %copy-done.4), channel_id=1, source_target_pairs={{0,24},{4,28},{8,0},{12,4},{16,8},{20,12},{24,16},{28,20},{1,25},{... | collective-permute-start | bytes 196616 | tf_op jit(solution)/shard_map/ppermute | solution.py:58
  90.4 7.1 %collective-permute-start.21 = (bf16[32,1024]{1,0:T(8,128)(2,1)S(1)}, bf16[32,1024]{1,0:T(8,128)(2,1)S(1)}, u32[]{:S(2)}, u32[]{:S(2)}) collective-permute-start(bf16[32,1024]{1,0:T(8,128)(2,1)S(1)} %copy-done.4), channel_id=1, source_target_pairs={{0,8},{4,12},{8,16},{12,20},{16,24},{20,28},{24,0},{28,4},{1,9},{5... | collective-permute-start | bytes 196616 | tf_op jit(solution)/shard_map/ppermute | solution.py:57
  97.5 11.0 %collective-permute-start.23 = (bf16[256,1024]{1,0:T(8,128)(2,1)S(1)}, bf16[256,1024]{1,0:T(8,128)(2,1)}, u32[]{:S(2)}, u32[]{:S(2)}) collective-permute-start(bf16[256,1024]{1,0:T(8,128)(2,1)S(1)} %constant_dynamic-update-slice_fusion.20.mine_ref), channel_id=1, source_target_pairs={{0,1},{1,0},{2,3},{3,2},{4,5},{5,4},{6,7},{7,6},{8,9},{9,8},{10,11... | collective-permute-start | bytes 1572872 | tf_op jit(solution)/shard_map/ppermute | solution.py:60
  105.5 1.5 %copy-start.6 = (bf16[1024,924]{0,1:T(8,128)(2,1)S(1)}, bf16[1024,924]{0,1:T(8,128)(2,1)}, u32[]{:S(2)}) copy-start(bf16[1024,924]{0,1:T(8,128)(2,1)} %param.12) | copy-start | bytes 5677060
  108.5 3.9 %collective-permute-start.8 = (bf16[256,1024]{1,0:T(8,128)(2,1)S(1)}, bf16[256,1024]{1,0:T(8,128)(2,1)S(1)}, u32[]{:S(2)}, u32[]{:S(2)}) collective-permute-start(bf16[256,1024]{1,0:T(8,128)(2,1)S(1)} %shard_map.103), channel_id=1, source_target_pairs={{0,1},{1,0},{2,3},{3,2},{4,5},{5,4},{6,7},{7,6},{8,9},{9,8},{10,11... | collective-permute-start | bytes 1572872 | tf_op jit(solution)/shard_map/ppermute | solution.py:121
  112.4 7.5 %collective-permute-start.9 = (bf16[64,1024]{1,0:T(8,128)(2,1)S(1)}, bf16[64,1024]{1,0:T(8,128)(2,1)S(1)}, u32[]{:S(2)}, u32[]{:S(2)}) collective-permute-start(bf16[64,1024]{1,0:T(8,128)(2,1)S(1)} %get-tuple-element.10), channel_id=1, source_target_pairs={{0,28},{4,0},{8,4},{12,8},{16,12},{20,16},{24,20},{28,24},{1,29},{... | collective-permute-start | bytes 393224 | tf_op jit(solution)/shard_map/ppermute | solution.py:135
  114.4 6.7 %collective-permute-start.10 = (bf16[64,1024]{1,0:T(8,128)(2,1)S(1)}, bf16[64,1024]{1,0:T(8,128)(2,1)S(1)}, u32[]{:S(2)}, u32[]{:S(2)}) collective-permute-start(bf16[64,1024]{1,0:T(8,128)(2,1)S(1)} %get-tuple-element.11), channel_id=1, source_target_pairs={{0,4},{4,8},{8,12},{12,16},{16,20},{20,24},{24,28},{28,0},{1,5},{5... | collective-permute-start | bytes 393224 | tf_op jit(solution)/shard_map/ppermute | solution.py:136
  117.0 6.1 %collective-permute-start.11 = (bf16[32,1024]{1,0:T(8,128)(2,1)S(1)}, bf16[32,1024]{1,0:T(8,128)(2,1)S(1)}, u32[]{:S(2)}, u32[]{:S(2)}) collective-permute-start(bf16[32,1024]{1,0:T(8,128)(2,1)S(1)} %get-tuple-element.12), channel_id=1, source_target_pairs={{0,24},{4,28},{8,0},{12,4},{16,8},{20,12},{24,16},{28,20},{1,25},{... | collective-permute-start | bytes 196616 | tf_op jit(solution)/shard_map/ppermute | solution.py:137
  118.7 6.9 %collective-permute-start.12 = (bf16[32,1024]{1,0:T(8,128)(2,1)S(1)}, bf16[32,1024]{1,0:T(8,128)(2,1)S(1)}, u32[]{:S(2)}, u32[]{:S(2)}) collective-permute-start(bf16[32,1024]{1,0:T(8,128)(2,1)S(1)} %get-tuple-element.13), channel_id=1, source_target_pairs={{0,8},{4,12},{8,16},{12,20},{16,24},{20,28},{24,0},{28,4},{1,9},{5... | collective-permute-start | bytes 196616 | tf_op jit(solution)/shard_map/ppermute | solution.py:138
  125.6 11.4 %collective-permute-start.13 = (bf16[16,1024]{1,0:T(8,128)(2,1)S(1)}, bf16[16,1024]{1,0:T(8,128)(2,1)S(1)}, u32[]{:S(2)}, u32[]{:S(2)}) collective-permute-start(bf16[16,1024]{1,0:T(8,128)(2,1)S(1)} %slice.51), channel_id=1, source_target_pairs={{0,2},{1,3},{2,0},{3,1},{4,6},{5,7},{6,4},{7,5},{8,10},{9,11},{10,... | collective-permute-start | bytes 98312 | tf_op jit(solution)/shard_map/ppermute | solution.py:143
  126.9 10.1 %collective-permute-start.14 = (bf16[16,1024]{1,0:T(8,128)(2,1)S(1)}, bf16[16,1024]{1,0:T(8,128)(2,1)S(1)}, u32[]{:S(2)}, u32[]{:S(2)}) collective-permute-start(bf16[16,1024]{1,0:T(8,128)(2,1)S(1)} %get-tuple-element.21), channel_id=1, source_target_pairs={{0,16},{4,20},{8,24},{12,28},{16,0},{20,4},{24,8},{28,12},{1,17},{... | collective-permute-start | bytes 98312 | tf_op jit(solution)/shard_map/ppermute | solution.py:144
  130.2 10.2 %collective-permute-start.15 = (bf16[16,1024]{1,0:T(8,128)(2,1)S(1)}, bf16[16,1024]{1,0:T(8,128)(2,1)S(1)}, u32[]{:S(2)}, u32[]{:S(2)}) collective-permute-start(bf16[16,1024]{1,0:T(8,128)(2,1)S(1)} %get-tuple-element.22), channel_id=1, source_target_pairs={{0,18},{1,19},{2,16},{3,17},{4,22},{5,23},{6,20},{7,21},{8,26},{9,... | collective-permute-start | bytes 98312 | tf_op jit(solution)/shard_map/ppermute | solution.py:145
  (2 other events, 2.7 us)
Sparse Core Ops, SparseCore 0:
  10.4 68.9 all-gather.2

commit v2 on v0

v2 whole, which is shorter than its diff:
```python
import jax
import jax.numpy as jnp
from jax import lax
from jax.experimental import pallas as pl
from jax.experimental.pallas import tpu as pltpu
from jax.sharding import PartitionSpec as P

F32 = jnp.float32
BF16 = jnp.bfloat16
BY_FEATURE = (((1,), (1,)), ((), ()))
BY_TOKEN = (((0,), (0,)), ((), ()))
ROWS = 16
NZ = 8

OWN = ((0, 0), (0, 1), (4, 0), (4, 1))
PREV = ((-1, 0), (-1, 1), (3, 0), (3, 1))
NEXT = ((1, 0), (1, 1), (5, 0), (5, 1))
PREV2 = ((-2, 0), (-2, 1))
NEXT2 = ((2, 0), (2, 1))
ORDER = OWN + PREV + NEXT + PREV2 + NEXT2


def gy_shift(step):
    return [(i, (i + step) % NZ) for i in range(NZ)]


def place_shift(step, flip):
    return [
        (z * 4 + g, ((z + step) % NZ) * 4 + (g ^ (2 * flip))) for z in range(NZ) for g in range(4)
    ]


OTHER_CORE = [(i, i ^ 1) for i in range(4)]
OTHER_Y = [(i, i ^ 2) for i in range(4)]
SAME_CORE = [[2 * k + core for k in range(16)] for core in range(2)]

ANY = pl.BlockSpec(memory_space=pl.ANY)
VMEM = pl.BlockSpec(memory_space=pltpu.VMEM)


def params(mib):
    return pltpu.CompilerParams(vmem_limit_bytes=mib * 2**20)


def row_of(there, second):
    z, y = lax.axis_index("gy"), lax.axis_index("gz") // 2
    step, flip = there
    block = lax.rem(z + step + NZ, NZ) * 4 + second * 2 + (y + flip - 2 * y * flip)
    return pl.multiple_of(block * ROWS, ROWS)


def far_places(x):
    return (
        lax.ppermute(x, ("gy", "gz"), place_shift(4, 1)),
        lax.ppermute(x, "gy", gy_shift(4)),
        lax.ppermute(x, "gz", OTHER_Y),
    )


def near_places(near, four):
    return (
        lax.ppermute(near, "gy", gy_shift(2)),
        lax.ppermute(near, "gy", gy_shift(-2)),
        lax.ppermute(four, "gy", gy_shift(1)),
        lax.ppermute(four, "gy", gy_shift(-1)),
    )


def swap_core(x):
    return lax.ppermute(x, "gz", OTHER_CORE)


def pair_kernel(x_ref, y_ref, out_ref, sems):
    copies = [
        pltpu.make_async_copy(ref, out_ref.at[pl.ds(k * ROWS, ROWS)], sems.at[k])
        for k, ref in enumerate((x_ref, y_ref))
    ]
    for copy in copies:
        copy.start()
    for copy in copies:
        copy.wait()


def pair(x, y):
    rows, cols = x.shape
    return pl.pallas_call(
        pair_kernel,
        out_shape=jax.ShapeDtypeStruct((2 * rows, cols), x.dtype),
        in_specs=[ANY] * 2,
        out_specs=VMEM,
        scratch_shapes=[pltpu.SemaphoreType.DMA((2,))],
        compiler_params=params(4),
    )(x, y)


def pack_kernel(x_ref, y_ref, far_ref, far_y_ref, _, *outs):
    for j in range(2):
        near_ref, four_ref = outs[2 * j : 2 * j + 2]
        for k, ref in enumerate((x_ref, y_ref, far_ref, far_y_ref)):
            rows = pl.ds(k * ROWS, ROWS)
            block = ref[j * ROWS : (j + 1) * ROWS, :]
            four_ref[rows, :] = block
            if k < 2:
                near_ref[rows, :] = block


def pack(x, far, earlier):
    far_y, far_z, same_z = far
    rows, cols = x.shape
    near = jax.ShapeDtypeStruct((rows, cols), x.dtype)
    four = jax.ShapeDtypeStruct((2 * rows, cols), x.dtype)
    return pl.pallas_call(
        pack_kernel,
        out_shape=(near, four, near, four),
        in_specs=[VMEM] * 4 + [ANY],
        out_specs=(VMEM,) * 4,
        compiler_params=params(4),
    )(x, same_z, far_z, far_y, earlier)


def merge_kernel(four_ref, prev_ref, next_ref, prev2_ref, next2_ref, *refs):
    out_ref = refs[-1]
    k = 0
    for ref in (four_ref, prev_ref, next_ref, prev2_ref, next2_ref):
        out_ref[pl.ds(k, ref.shape[0]), :] = ref[...]
        k += ref.shape[0]


def merge(four, got, earlier):
    prev2, next2, prev, following = got
    return pl.pallas_call(
        merge_kernel,
        out_shape=jax.ShapeDtypeStruct((16 * ROWS, four.shape[1]), four.dtype),
        in_specs=[VMEM] * 5 + [ANY] * len(earlier),
        out_specs=VMEM,
        compiler_params=params(4),
    )(four, prev, following, prev2, next2, *earlier)


def place_kernel(mine_ref, other_ref, out_ref):
    for k, there in enumerate(ORDER):
        rows = pl.ds(k * ROWS, ROWS)
        out_ref[pl.ds(row_of(there, 0), ROWS), :] = mine_ref[rows, :]
        out_ref[pl.ds(row_of(there, 1), ROWS), :] = other_ref[rows, :]


def place_rows(mine, other):
    rows, cols = mine.shape
    return pl.pallas_call(
        place_kernel,
        out_shape=jax.ShapeDtypeStruct((2 * rows, cols), mine.dtype),
        in_specs=[VMEM] * 2,
        out_specs=VMEM,
        compiler_params=params(8),
    )(mine, other)


def hidden_kernel(mine_ref, other_ref, weight_ref, _, cols_ref, out_ref):
    place_kernel(mine_ref, other_ref, cols_ref)
    part = lax.dot_general(
        cols_ref[...], weight_ref[...], BY_FEATURE, preferred_element_type=F32
    )
    out_ref[...] = part.astype(BF16).reshape(out_ref.shape)


def hidden_part(mine, other, weight, earlier):
    rows, cols = mine.shape
    return pl.pallas_call(
        hidden_kernel,
        out_shape=(
            jax.ShapeDtypeStruct((2 * rows, cols), BF16),
            jax.ShapeDtypeStruct((8, rows // 4, weight.shape[0]), BF16),
        ),
        in_specs=[VMEM, VMEM, VMEM, ANY],
        out_specs=(VMEM, VMEM),
        compiler_params=params(16),
    )(mine, other, weight, earlier)


def own_core_first(x):
    core = lax.axis_index("gz") % 2
    blocks = [x[k * ROWS : (k + 1) * ROWS, :] for k in range(4)]
    own = [jnp.where(core == 0, blocks[2 * y], blocks[2 * y + 1]) for y in range(2)]
    second = [jnp.where(core == 0, blocks[2 * y + 1], blocks[2 * y]) for y in range(2)]
    return jnp.concatenate(own + second, axis=0)


def local_hidden_kernel(gate_ref, up_ref, out_ref):
    gate = gate_ref[...].astype(F32)
    up_value = up_ref[...].astype(F32)
    out_ref[...] = own_core_first(gate * jax.nn.sigmoid(gate) * up_value).astype(BF16)


def local_hidden(gate, up):
    return pl.pallas_call(
        local_hidden_kernel,
        out_shape=jax.ShapeDtypeStruct(gate.shape, BF16),
        in_specs=[VMEM, VMEM],
        out_specs=VMEM,
        compiler_params=params(4),
    )(gate, up)


def sum_kernel(parts_ref, gate_ref, up_ref, _, out_ref):
    hidden_grad = parts_ref[0].astype(F32)
    for k in range(1, parts_ref.shape[0]):
        hidden_grad = hidden_grad + parts_ref[k].astype(F32)
    gate = own_core_first(gate_ref[...].astype(F32))
    up_value = own_core_first(up_ref[...].astype(F32))
    sigmoid_gate = jax.nn.sigmoid(gate)
    activated = gate * sigmoid_gate
    gate_grad = hidden_grad * up_value * sigmoid_gate * (1.0 + gate * (1.0 - sigmoid_gate))
    gate_grad = gate_grad.astype(BF16)
    up_grad = (hidden_grad * activated).astype(BF16)
    for k in range(out_ref.shape[0]):
        out_ref[k, 0] = gate_grad
        out_ref[k, 1] = up_grad


def grad_copies(parts, gate, up, earlier):
    blocks, rows, units = parts.shape
    return pl.pallas_call(
        sum_kernel,
        out_shape=jax.ShapeDtypeStruct((blocks, 2, rows, units), BF16),
        in_specs=[VMEM] * 3 + [ANY],
        out_specs=VMEM,
        compiler_params=params(8),
    )(parts, gate, up, earlier)


def stack_kernel(x_ref, y_ref, out_ref):
    rows = x_ref.shape[0]
    out_ref[:rows, :] = x_ref[...]
    out_ref[rows:, :] = y_ref[...]


def stack(x, y):
    rows, cols = x.shape
    return pl.pallas_call(
        stack_kernel,
        out_shape=jax.ShapeDtypeStruct((2 * rows, cols), x.dtype),
        in_specs=[VMEM] * 2,
        out_specs=VMEM,
        compiler_params=params(4),
    )(x, y)


def order_kernel(*refs):
    pieces, out_ref = refs[:4], refs[4]
    me = lax.axis_index("gx")
    rows = pieces[0].shape[0] // 2
    for step, ref in zip((0, 2, 6, 4), pieces):
        block = lax.rem(me + 8 - step, 8)
        for k in range(2):
            there = block + k * (1 - 2 * lax.rem(block, 2))
            out_ref[pl.ds(pl.multiple_of(there * rows, rows), rows), :] = ref[
                k * rows : (k + 1) * rows, :
            ]


def same_pair(x):
    return stack(x, lax.ppermute(x, "gx", [(i, i ^ 1) for i in range(8)]))


def along_x(pair):
    return [pair] + [
        lax.ppermute(pair, "gx", [(i, (i + step) % 8) for i in range(8)]) for step in (2, 6, 4)
    ]


def in_order(pieces):
    rows, units = pieces[0].shape
    return pl.pallas_call(
        order_kernel,
        out_shape=jax.ShapeDtypeStruct((4 * rows, units), pieces[0].dtype),
        in_specs=[VMEM] * 4,
        out_specs=VMEM,
        compiler_params=params(8),
    )(*pieces)


def last_sum_kernel(parts_ref, out_ref):
    total = parts_ref[0].astype(F32)
    for k in range(1, parts_ref.shape[0]):
        total = total + parts_ref[k].astype(F32)
    out_ref[...] = total.astype(BF16)


def last_sum(parts):
    return pl.pallas_call(
        last_sum_kernel,
        out_shape=jax.ShapeDtypeStruct(parts.shape[1:], BF16),
        in_specs=[VMEM],
        out_specs=VMEM,
        compiler_params=params(4),
    )(parts)


def input_kernel(grads_ref, gw_ref, uw_ref, send_ref, keep_ref):
    blocks, _, rows, units = grads_ref.shape
    half = rows // 2
    for k, ref in enumerate((send_ref, keep_ref)):
        part = pl.ds((1 - k) * half, half)
        gate_grad = grads_ref[:, 0, part, :].reshape(blocks * half, units)
        up_grad = grads_ref[:, 1, part, :].reshape(blocks * half, units)
        ref[...] = jnp.dot(gate_grad, gw_ref[...], preferred_element_type=F32) + jnp.dot(
            up_grad, uw_ref[...], preferred_element_type=F32
        )


def input_parts(grads, gate_weight, up_weight):
    blocks, _, rows, _ = grads.shape
    half = jax.ShapeDtypeStruct((blocks * rows // 2, gate_weight.shape[1]), F32)
    return pl.pallas_call(
        input_kernel,
        out_shape=(half, half),
        in_specs=[VMEM] * 3,
        out_specs=(VMEM, VMEM),
        compiler_params=params(16),
    )(grads, gate_weight, up_weight)


def body(layer_input, out_grad, gate_pre, up_pre, gate_weight, up_weight, down_weight):
    both = pair(out_grad, layer_input)
    far = far_places(both)
    hidden_pair = same_pair(local_hidden(gate_pre, up_pre))
    near, four, near_in, four_in = pack(both, far, hidden_pair)
    pieces = along_x(hidden_pair)
    mine = merge(four, near_places(near, four), pieces[1:])
    hidden = in_order(pieces)
    grad_cols, part = hidden_part(mine, swap_core(mine), down_weight, hidden)
    parts = lax.all_to_all(part, "gx", 0, 0)
    mine_in = merge(four_in, near_places(near_in, four_in), [])
    grads = lax.all_to_all(grad_copies(parts, gate_pre, up_pre, mine_in), "gx", 0, 0)
    send, keep = input_parts(grads, gate_weight.T, up_weight.T)
    total = (keep + swap_core(send)).astype(BF16).reshape(16, ROWS, -1)
    totals = lax.all_to_all(total, ("gy", "gz"), 0, 0, axis_index_groups=SAME_CORE)
    input_sum = last_sum(totals)
    gate_grad, up_grad = grads[:, 0].reshape(512, -1), grads[:, 1].reshape(512, -1)
    input_cols = place_rows(mine_in, swap_core(mine_in))
    gate_sum = lax.dot_general(input_cols, gate_grad, BY_TOKEN, preferred_element_type=F32)
    up_sum = lax.dot_general(input_cols, up_grad, BY_TOKEN, preferred_element_type=F32)
    down_sum = lax.dot_general(hidden, grad_cols, BY_TOKEN, preferred_element_type=F32)
    return (
        input_sum,
        gate_sum.astype(BF16),
        up_sum.astype(BF16),
        down_sum.astype(BF16),
    )


def solution(mesh):
    tokens = P(("gy", "gz"), "gx")
    hidden = P("gx", ("gy", "gz"))
    return jax.shard_map(
        body,
        mesh=mesh,
        in_specs=(tokens, tokens, hidden, hidden, hidden, hidden, tokens),
        out_specs=(tokens, hidden, hidden, tokens),
        check_vma=False,
    )
```

time: 433 us -> 131 us (0.30)
  waiting for transfers between devices: 308 us -> 32 us
  blocking collectives: 82.9 us -> 29.6 us
  starting transfers between devices: 0.16 us -> 44.8 us
  between operations: 13.8 us -> 0.81 us
  matrix products: 18.8 us -> 8.58 us
  Pallas kernels: 0 us -> 7.16 us
    all_gather x2 -> x0, waiting for transfers between devices: 151 us -> none  [the longest x1 82.4 us: body(): lax.all_gather(out_grad, ('gy', 'gz'), axis=0, tiled=True)]
    reduce_scatter x1 -> x0, waiting for transfers between devices: 114 us -> none  [body(): lax.psum_scatter(partial_input, ('gy', 'gz'), scatter_dimension=0, tiled=...]
    all_gather x2 -> x0, blocking collectives: 82.9 us -> none  [the longest x1 44.6 us: body(): lax.all_gather(gate_pre, 'gx', axis=0, tiled=True)]
    psum x1 -> x0, waiting for transfers between devices: 41 us -> none  [body(): hidden_grad = lax.psum(partial_hidden, 'gx')]
    ppermute x0 -> x18, starting transfers between devices: none -> 32.7 us  [the longest x2 7.29 us: near_places(): lax.ppermute(near, 'gy', gy_shift(-2))]
    all_to_all x0 -> x1, blocking collectives: none -> 29.6 us  [body(): lax.all_to_all(grad_copies(parts, gate_pre, up_pre, mine_in), 'gx', 0, 0)]
    ppermute x0 -> x18, waiting for transfers between devices: none -> 18.3 us  [the longest x1 5.53 us: far_places(): lax.ppermute(x, ('gy', 'gz'), place_shift(4, 1))]
    all_to_all x0 -> x2, waiting for transfers between devices: none -> 13.7 us  [the longest x1 9.66 us: body(): lax.all_to_all(total, ('gy', 'gz'), 0, 0, axis_index_groups=SAME_CORE)]
  transfers between devices with their start and end apart: 4 -> 20, of which waited for: 4 -> 9; matrix products, arithmetic and copies ran while one was open for 5% -> 7% of each run, Pallas kernels for 0% -> 0%
where the time goes in v2:
time: 131 us; the launch traced here: 130 us
  starting transfers between devices  44.8 us (34%)
  waiting for transfers between devices  32 us (24%)
  blocking collectives  29.6 us (23%)
  matrix products  8.58 us (7%)
  Pallas kernels  7.16 us (5%)
  local copies, waits for them, and re-layouts  6.52 us (5%)
    all_to_all x1, blocking collectives, body(): lax.all_to_all(grad_copies(parts, gate_pre, up_pre, mine_in), 'gx', 0, 0)  29.6 us
    all_to_all x1, waiting for transfers between devices, body(): lax.all_to_all(total, ('gy', 'gz'), 0, 0, axis_index_groups=SAME_CORE)  9.66 us
    ppermute x2, starting transfers between devices, near_places(): lax.ppermute(near, 'gy', gy_shift(-2))  7.29 us
    ppermute x1, starting transfers between devices, far_places(): lax.ppermute(x, 'gy', gy_shift(4))  7.19 us
    all_to_all x1, starting transfers between devices, body(): parts = lax.all_to_all(part, 'gx', 0, 0)  7.12 us
    unnamed x28, local copies, waits for them, and re-layouts  6.35 us
    ppermute x2, starting transfers between devices, near_places(): lax.ppermute(four, 'gy', gy_shift(-1))  5.86 us
    ppermute x1, waiting for transfers between devices, far_places(): lax.ppermute(x, ('gy', 'gz'), place_shift(4, 1))  5.53 us
  transfers between devices with their start and end apart: 20, of which 9 were waited for; matrix products, arithmetic and copies ran while one was open for 7% of the time, Pallas kernels for 0%

profile of v2, /device:TPU:8, one launch (start us, length us, event | category | flops | bytes accessed | tf_op | source)
XLA Modules:
  0.0 130.3 jit_solution(11929311762042130351)
XLA Ops:
  2.5 2.3 %collective-permute-start.3 = (bf16[64,924]{1,0:T(8,128)(2,1)S(1)}, bf16[64,924]{1,0:T(8,128)(2,1)S(1)}, u32[]{:S(2)}, u32[]{:S(2)}) collective-permute-start(bf16[64,924]{1,0:T(8,128)(2,1)S(1)} %shard_map.103.x_ref), channel_id=1, source_target_pairs={{0,32},{32,0},{64,96},{96,64},{128,160},{160,128},{192,224},{224,1... | collective-permute-start | bytes 354824 | tf_op jit(solution)/shard_map/ppermute | solution.py:262
  6.4 0.9 collective-permute-start
  7.3 7.2 %collective-permute-start.1 = (bf16[32,1024]{1,0:T(8,128)(2,1)S(1)}, bf16[32,1024]{1,0:T(8,128)(2,1)S(1)}, u32[]{:S(2)}, u32[]{:S(2)}) collective-permute-start(bf16[32,1024]{1,0:T(8,128)(2,1)S(1)} %shard_map.102.x_ref), channel_id=1, source_target_pairs={{0,16},{4,20},{8,24},{12,28},{16,0},{20,4},{24,8},{28,12},{1,17},{... | collective-permute-start | bytes 196616 | tf_op jit(solution)/shard_map/ppermute | solution.py:55
  15.4 1.1 collective-permute-start.8
  16.5 2.2 %collective-permute-start.9 = (bf16[128,924]{1,0:T(8,128)(2,1)S(1)}, bf16[128,924]{1,0:T(8,128)(2,1)S(1)}, u32[]{:S(2)}, u32[]{:S(2)}) collective-permute-start(bf16[128,924]{1,0:T(8,128)(2,1)S(1)} %shard_map.104._.refs_0_), channel_id=1, source_target_pairs={{0,192},{32,224},{64,0},{96,32},{128,64},{160,96},{192,128},{224,1... | collective-permute-start | bytes 709640 | tf_op jit(solution)/shard_map/ppermute | solution.py:267
  18.7 1.3 %collective-permute-start.10 = (bf16[128,924]{1,0:T(8,128)(2,1)S(1)}, bf16[128,924]{1,0:T(8,128)(2,1)S(1)}, u32[]{:S(2)}, u32[]{:S(2)}) collective-permute-start(bf16[128,924]{1,0:T(8,128)(2,1)S(1)} %shard_map.104._.refs_0_), channel_id=1, source_target_pairs={{0,128},{32,160},{64,192},{96,224},{128,0},{160,32},{192,64},{224,... | collective-permute-start | bytes 709640 | tf_op jit(solution)/shard_map/ppermute | solution.py:267
  20.1 5.5 %collective-permute-done.2.far_y_ref = bf16[32,1024]{1,0:T(8,128)(2,1)S(1)} collective-permute-done((bf16[32,1024]{1,0:T(8,128)(2,1)S(1)}, bf16[32,1024]{1,0:T(8,128)(2,1)S(1)}, u32[]{:S(2)}, u32[]{:S(2)}) %collective-permute-start.2) | collective-permute-done | bytes 65568 | tf_op jit(solution)/shard_map/ppermute | solution.py:54
  25.6 1.1 collective-permute-start.6
  26.7 3.2 %collective-permute-start.7 = (bf16[32,1024]{1,0:T(8,128)(2,1)S(1)}, bf16[32,1024]{1,0:T(8,128)(2,1)S(1)}, u32[]{:S(2)}, u32[]{:S(2)}) collective-permute-start(bf16[32,1024]{1,0:T(8,128)(2,1)S(1)} %get-tuple-element.13), channel_id=1, source_target_pairs={{0,24},{4,28},{8,0},{12,4},{16,8},{20,12},{24,16},{28,20},{1,25},{... | collective-permute-start | bytes 196616 | tf_op jit(solution)/shard_map/ppermute | solution.py:63
  29.8 2.3 %collective-permute-done.6.prev2_ref = bf16[32,1024]{1,0:T(8,128)(2,1)S(1)} collective-permute-done((bf16[32,1024]{1,0:T(8,128)(2,1)S(1)}, bf16[32,1024]{1,0:T(8,128)(2,1)S(1)}, u32[]{:S(2)}, u32[]{:S(2)}) %collective-permute-start.6) | collective-permute-done | bytes 65568 | tf_op jit(solution)/shard_map/ppermute | solution.py:62
  32.2 1.8 %collective-permute-start.4 = (bf16[64,1024]{1,0:T(8,128)(2,1)S(1)}, bf16[64,1024]{1,0:T(8,128)(2,1)S(1)}, u32[]{:S(2)}, u32[]{:S(2)}) collective-permute-start(bf16[64,1024]{1,0:T(8,128)(2,1)S(1)} %get-tuple-element.12.four_ref), channel_id=1, source_target_pairs={{0,4},{4,8},{8,12},{12,16},{16,20},{20,24},{24,28},{28,0},{1,5},{5... | collective-permute-start | bytes 393224 | tf_op jit(solution)/shard_map/ppermute | solution.py:64
  33.9 2.4 %collective-permute-start.5 = (bf16[64,1024]{1,0:T(8,128)(2,1)S(1)}, bf16[64,1024]{1,0:T(8,128)(2,1)S(1)}, u32[]{:S(2)}, u32[]{:S(2)}) collective-permute-start(bf16[64,1024]{1,0:T(8,128)(2,1)S(1)} %get-tuple-element.12.four_ref), channel_id=1, source_target_pairs={{0,28},{4,0},{8,4},{12,8},{16,12},{20,16},{24,20},{28,24},{1,29},{... | collective-permute-start | bytes 393224 | tf_op jit(solution)/shard_map/ppermute | solution.py:65
  36.3 2.0 %collective-permute-done.4.prev_ref = bf16[64,1024]{1,0:T(8,128)(2,1)S(1)} collective-permute-done((bf16[64,1024]{1,0:T(8,128)(2,1)S(1)}, bf16[64,1024]{1,0:T(8,128)(2,1)S(1)}, u32[]{:S(2)}, u32[]{:S(2)}) %collective-permute-start.4) | collective-permute-done | bytes 131104 | tf_op jit(solution)/shard_map/ppermute | solution.py:64
  39.2 1.8 %collective-permute-done.11.other_ref = bf16[256,1024]{1,0:T(8,128)(2,1)S(1)} collective-permute-done((bf16[256,1024]{1,0:T(8,128)(2,1)S(1)}, bf16[256,1024]{1,0:T(8,128)(2,1)S(1)}, u32[]{:S(2)}, u32[]{:S(2)}) %collective-permute-start.11) | collective-permute-done | bytes 524320 | tf_op jit(solution)/shard_map/ppermute | solution.py:70
  41.0 2.3 %shard_map.108 = (bf16[512,1024]{1,0:T(8,128)(2,1)S(1)}, bf16[8,64,924]{2,1,0:T(8,128)(2,1)}) custom-call(bf16[256,1024]{1,0:T(8,128)(2,1)S(1)} %shard_map.106.mine_ref, bf16[256,1024]{1,0:T(8,128)(2,1)S(1)} %collective-permute-done.11.other_ref, bf16[924,1024]{1,0:T(8,128)(2,1)S(1)} %copy-done.4, bf16[512,924]{1,0:T(8,128)(2,1)S(1)} %shard_map.107._), custom_call_target="tpu_custom_call" | custom-call | tf_op jit(solution)/shard_map/pallas_call | solution.py:168
  43.3 1.0 copy-done.13
  44.3 7.1 %all-to-all-start = ((bf16[8,64,924]{2,1,0:T(8,128)(2,1)}), bf16[8,64,924]{2,1,0:T(8,128)(2,1)S(1)}, u32[]{:S(2)}, u32[]{:S(2)}) async-start(bf16[8,64,924]{2,1,0:T(8,128)(2,1)} %get-tuple-element.14), calls=%async_computation | async-start | bytes 2097152 | tf_op jit(solution)/shard_map/all_to_all | solution.py:332
  51.5 3.5 %collective-permute-start.13 = (bf16[64,1024]{1,0:T(8,128)(2,1)S(1)}, bf16[64,1024]{1,0:T(8,128)(2,1)S(1)}, u32[]{:S(2)}, u32[]{:S(2)}) collective-permute-start(bf16[64,1024]{1,0:T(8,128)(2,1)S(1)} %get-tuple-element.15.four_ref), channel_id=1, source_target_pairs={{0,28},{4,0},{8,4},{12,8},{16,12},{20,16},{24,20},{28,24},{1,29},{... | collective-permute-start | bytes 393224 | tf_op jit(solution)/shard_map/ppermute | solution.py:65
  55.0 4.1 %collective-permute-start.15 = (bf16[32,1024]{1,0:T(8,128)(2,1)S(1)}, bf16[32,1024]{1,0:T(8,128)(2,1)S(1)}, u32[]{:S(2)}, u32[]{:S(2)}) collective-permute-start(bf16[32,1024]{1,0:T(8,128)(2,1)S(1)} %get-tuple-element.16), channel_id=1, source_target_pairs={{0,24},{4,28},{8,0},{12,4},{16,8},{20,12},{24,16},{28,20},{1,25},{... | collective-permute-start | bytes 196616 | tf_op jit(solution)/shard_map/ppermute | solution.py:63
  59.1 3.1 %collective-permute-done.14.prev2_ref = bf16[32,1024]{1,0:T(8,128)(2,1)S(1)} collective-permute-done((bf16[32,1024]{1,0:T(8,128)(2,1)S(1)}, bf16[32,1024]{1,0:T(8,128)(2,1)S(1)}, u32[]{:S(2)}, u32[]{:S(2)}) %collective-permute-start.14) | collective-permute-done | bytes 65568 | tf_op jit(solution)/shard_map/ppermute | solution.py:62
  62.2 4.1 %all-to-all-done.parts_ref = bf16[8,64,924]{2,1,0:T(8,128)(2,1)S(1)} async-done(((bf16[8,64,924]{2,1,0:T(8,128)(2,1)}), bf16[8,64,924]{2,1,0:T(8,128)(2,1)S(1)}, u32[]{:S(2)}, u32[]{:S(2)}) %all-to-all-start) | async-done | bytes 946208 | tf_op jit(solution)/shard_map/all_to_all | solution.py:332
  66.7 29.6 %all_to_all.15.grads_ref = bf16[8,2,64,924]{3,2,1,0:T(8,128)(2,1)S(1)} all-to-all(bf16[8,2,64,924]{3,2,1,0:T(8,128)(2,1)S(1)} %shard_map.110), channel_id=1, replica_groups=mesh['gx'=8,'gy'=8,'gz'=4] {'gx'}, dimensions={0} | all-to-all | bytes 3784704 | tf_op jit(solution)/shard_map/all_to_all | solution.py:334
  96.3 2.3 %shard_map.111 = (f32[256,1024]{1,0:T(8,128)S(1)}, f32[256,1024]{1,0:T(8,128)S(1)}) custom-call(bf16[8,2,64,924]{3,2,1,0:T(8,128)(2,1)S(1)} %all_to_all.15.grads_ref, bf16[924,1024]{1,0:T(8,128)(2,1)S(1)} %bitcast.11, bf16[924,1024]{1,0:T(8,128)(2,1)S(1)} %bitcast.12), custom_call_target="tpu_custom_call" | custom-call | tf_op jit(solution)/shard_map/pallas_call | solution.py:314
  99.2 2.9 %collective-permute-done.17.other_ref = bf16[256,1024]{1,0:T(8,128)(2,1)S(1)} collective-permute-done((bf16[256,1024]{1,0:T(8,128)(2,1)S(1)}, bf16[256,1024]{1,0:T(8,128)(2,1)S(1)}, u32[]{:S(2)}, u32[]{:S(2)}) %collective-permute-start.17) | collective-permute-done | bytes 524320 | tf_op jit(solution)/shard_map/ppermute | solution.py:70
  102.2 1.0 copy-done.5
  104.1 5.0 %all-to-all-start.2 = ((bf16[16,16,1024]{2,1,0:T(8,128)(2,1)}), bf16[16,16,1024]{2,1,0:T(8,128)(2,1)}, u32[]{:S(2)}, u32[]{:S(2)}) async-start(bf16[16,16,1024]{2,1,0:T(8,128)(2,1)} %bitcast.13), calls=%async_computation.2 | async-start | bytes 1048576 | tf_op jit(solution)/shard_map/all_to_all | solution.py:337
  109.1 3.7 %convolution_convert_fusion = bf16[924,1024]{1,0:T(8,128)(2,1)} fusion(bf16[512,924]{1,0:T(8,128)(2,1)S(1)} %copy-done.1, bf16[512,1024]{1,0:T(8,128)(2,1)} %copy-done.13), kind=kOutput, calls=%fused_computation | convolution fusion | flops 969830400 | bytes 3887104 | tf_op jit(solution)/shard_map/dot_general | solution.py:343
  113.0 1.0 copy-done.6
  114.0 2.5 %convolution_convert_fusion.2 = bf16[1024,924]{0,1:T(8,128)(2,1)} fusion(bf16[512,1024]{1,0:T(8,128)(2,1)S(1)} %copy-done.6, bf16[512,924]{1,0:T(8,128)(2,1)S(1)} %bitcast.15), kind=kOutput, calls=%fused_computation.2 | convolution fusion | flops 969830400 | bytes 3887104 | tf_op jit(solution)/shard_map/dot_general | solution.py:341
  116.5 2.5 %convolution_convert_fusion.1 = bf16[1024,924]{0,1:T(8,128)(2,1)} fusion(bf16[512,1024]{1,0:T(8,128)(2,1)S(1)} %copy-done.6, bf16[512,924]{1,0:T(8,128)(2,1)S(1)} %bitcast.14), kind=kOutput, calls=%fused_computation.1 | convolution fusion | flops 969830400 | bytes 3887104 | tf_op jit(solution)/shard_map/dot_general | solution.py:342
  118.9 9.7 %all-to-all-done.2.parts_ref = bf16[16,16,1024]{2,1,0:T(8,128)(2,1)} async-done(((bf16[16,16,1024]{2,1,0:T(8,128)(2,1)}), bf16[16,16,1024]{2,1,0:T(8,128)(2,1)}, u32[]{:S(2)}, u32[]{:S(2)}) %all-to-all-start.2) | async-done | bytes 524320 | tf_op jit(solution)/shard_map/all_to_all | solution.py:337
  128.6 1.7 %shard_map.112 = bf16[16,1024]{1,0:T(8,128)(2,1)} custom-call(bf16[16,16,1024]{2,1,0:T(8,128)(2,1)} %all-to-all-done.2.parts_ref), custom_call_target="tpu_custom_call" | custom-call | tf_op jit(solution)/shard_map/pallas_call | solution.py:290
  (54 shorter events, 7.5 us)
Async XLA Ops:
  0.6 0.9 copy-start.7
  1.5 0.9 copy-start.9
  2.5 12.9 %collective-permute-start.3 = (bf16[64,924]{1,0:T(8,128)(2,1)S(1)}, bf16[64,924]{1,0:T(8,128)(2,1)S(1)}, u32[]{:S(2)}, u32[]{:S(2)}) collective-permute-start(bf16[64,924]{1,0:T(8,128)(2,1)S(1)} %shard_map.103.x_ref), channel_id=1, source_target_pairs={{0,32},{32,0},{64,96},{96,64},{128,160},{160,128},{192,224},{224,1... | collective-permute-start | bytes 354824 | tf_op jit(solution)/shard_map/ppermute | solution.py:262
  6.4 12.3 %collective-permute-start = (bf16[32,1024]{1,0:T(8,128)(2,1)S(1)}, bf16[32,1024]{1,0:T(8,128)(2,1)S(1)}, u32[]{:S(2)}, u32[]{:S(2)}) collective-permute-start(bf16[32,1024]{1,0:T(8,128)(2,1)S(1)} %shard_map.102.x_ref), channel_id=1, source_target_pairs={{0,2},{1,3},{2,0},{3,1},{4,6},{5,7},{6,4},{7,5},{8,10},{9,11},{10,... | collective-permute-start | bytes 196616 | tf_op jit(solution)/shard_map/ppermute | solution.py:56
  7.3 12.7 %collective-permute-start.1 = (bf16[32,1024]{1,0:T(8,128)(2,1)S(1)}, bf16[32,1024]{1,0:T(8,128)(2,1)S(1)}, u32[]{:S(2)}, u32[]{:S(2)}) collective-permute-start(bf16[32,1024]{1,0:T(8,128)(2,1)S(1)} %shard_map.102.x_ref), channel_id=1, source_target_pairs={{0,16},{4,20},{8,24},{12,28},{16,0},{20,4},{24,8},{28,12},{1,17},{... | collective-permute-start | bytes 196616 | tf_op jit(solution)/shard_map/ppermute | solution.py:55
  14.5 11.1 %collective-permute-start.2 = (bf16[32,1024]{1,0:T(8,128)(2,1)S(1)}, bf16[32,1024]{1,0:T(8,128)(2,1)S(1)}, u32[]{:S(2)}, u32[]{:S(2)}) collective-permute-start(bf16[32,1024]{1,0:T(8,128)(2,1)S(1)} %shard_map.102.x_ref), channel_id=1, source_target_pairs={{0,18},{1,19},{2,16},{3,17},{4,22},{5,23},{6,20},{7,21},{8,26},{9,... | collective-permute-start | bytes 196616 | tf_op jit(solution)/shard_map/ppermute | solution.py:54
  15.4 23.5 %collective-permute-start.8 = (bf16[128,924]{1,0:T(8,128)(2,1)S(1)}, bf16[128,924]{1,0:T(8,128)(2,1)S(1)}, u32[]{:S(2)}, u32[]{:S(2)}) collective-permute-start(bf16[128,924]{1,0:T(8,128)(2,1)S(1)} %shard_map.104._.refs_0_), channel_id=1, source_target_pairs={{0,64},{32,96},{64,128},{96,160},{128,192},{160,224},{192,0},{224,... | collective-permute-start | bytes 709640 | tf_op jit(solution)/shard_map/ppermute | solution.py:267
  16.5 22.4 %collective-permute-start.9 = (bf16[128,924]{1,0:T(8,128)(2,1)S(1)}, bf16[128,924]{1,0:T(8,128)(2,1)S(1)}, u32[]{:S(2)}, u32[]{:S(2)}) collective-permute-start(bf16[128,924]{1,0:T(8,128)(2,1)S(1)} %shard_map.104._.refs_0_), channel_id=1, source_target_pairs={{0,192},{32,224},{64,0},{96,32},{128,64},{160,96},{192,128},{224,1... | collective-permute-start | bytes 709640 | tf_op jit(solution)/shard_map/ppermute | solution.py:267
  18.7 20.2 %collective-permute-start.10 = (bf16[128,924]{1,0:T(8,128)(2,1)S(1)}, bf16[128,924]{1,0:T(8,128)(2,1)S(1)}, u32[]{:S(2)}, u32[]{:S(2)}) collective-permute-start(bf16[128,924]{1,0:T(8,128)(2,1)S(1)} %shard_map.104._.refs_0_), channel_id=1, source_target_pairs={{0,128},{32,160},{64,192},{96,224},{128,0},{160,32},{192,64},{224,... | collective-permute-start | bytes 709640 | tf_op jit(solution)/shard_map/ppermute | solution.py:267
  25.6 6.6 %collective-permute-start.6 = (bf16[32,1024]{1,0:T(8,128)(2,1)S(1)}, bf16[32,1024]{1,0:T(8,128)(2,1)S(1)}, u32[]{:S(2)}, u32[]{:S(2)}) collective-permute-start(bf16[32,1024]{1,0:T(8,128)(2,1)S(1)} %get-tuple-element.13), channel_id=1, source_target_pairs={{0,8},{4,12},{8,16},{12,20},{16,24},{20,28},{24,0},{28,4},{1,9},{5... | collective-permute-start | bytes 196616 | tf_op jit(solution)/shard_map/ppermute | solution.py:62
  26.7 7.3 %collective-permute-start.7 = (bf16[32,1024]{1,0:T(8,128)(2,1)S(1)}, bf16[32,1024]{1,0:T(8,128)(2,1)S(1)}, u32[]{:S(2)}, u32[]{:S(2)}) collective-permute-start(bf16[32,1024]{1,0:T(8,128)(2,1)S(1)} %get-tuple-element.13), channel_id=1, source_target_pairs={{0,24},{4,28},{8,0},{12,4},{16,8},{20,12},{24,16},{28,20},{1,25},{... | collective-permute-start | bytes 196616 | tf_op jit(solution)/shard_map/ppermute | solution.py:63
  32.2 8.8 %copy-start.4 = (bf16[924,1024]{1,0:T(8,128)(2,1)S(1)}, bf16[924,1024]{1,0:T(8,128)(2,1)}, u32[]{:S(2)}) copy-start(bf16[924,1024]{1,0:T(8,128)(2,1)} %weight_ref.1) | copy-start | bytes 5677060
  32.2 6.2 %collective-permute-start.4 = (bf16[64,1024]{1,0:T(8,128)(2,1)S(1)}, bf16[64,1024]{1,0:T(8,128)(2,1)S(1)}, u32[]{:S(2)}, u32[]{:S(2)}) collective-permute-start(bf16[64,1024]{1,0:T(8,128)(2,1)S(1)} %get-tuple-element.12.four_ref), channel_id=1, source_target_pairs={{0,4},{4,8},{8,12},{12,16},{16,20},{20,24},{24,28},{28,0},{1,5},{5... | collective-permute-start | bytes 393224 | tf_op jit(solution)/shard_map/ppermute | solution.py:64
  33.9 5.0 %collective-permute-start.5 = (bf16[64,1024]{1,0:T(8,128)(2,1)S(1)}, bf16[64,1024]{1,0:T(8,128)(2,1)S(1)}, u32[]{:S(2)}, u32[]{:S(2)}) collective-permute-start(bf16[64,1024]{1,0:T(8,128)(2,1)S(1)} %get-tuple-element.12.four_ref), channel_id=1, source_target_pairs={{0,28},{4,0},{8,4},{12,8},{16,12},{20,16},{24,20},{28,24},{1,29},{... | collective-permute-start | bytes 393224 | tf_op jit(solution)/shard_map/ppermute | solution.py:65
  39.0 2.0 %collective-permute-start.11 = (bf16[256,1024]{1,0:T(8,128)(2,1)S(1)}, bf16[256,1024]{1,0:T(8,128)(2,1)S(1)}, u32[]{:S(2)}, u32[]{:S(2)}) collective-permute-start(bf16[256,1024]{1,0:T(8,128)(2,1)S(1)} %shard_map.106.mine_ref), channel_id=1, source_target_pairs={{0,1},{1,0},{2,3},{3,2},{4,5},{5,4},{6,7},{7,6},{8,9},{9,8},{10,11... | collective-permute-start | bytes 1572872 | tf_op jit(solution)/shard_map/ppermute | solution.py:70
  39.2 4.1 %copy-start = (bf16[512,924]{1,0:T(8,128)(2,1)}, bf16[512,924]{1,0:T(8,128)(2,1)S(1)}, u32[]{:S(2)}) copy-start(bf16[512,924]{1,0:T(8,128)(2,1)S(1)} %shard_map.107._) | copy-start | bytes 2838532
  43.3 1.0 copy-start.13
  44.3 22.0 %copy-start.8 = (bf16[64,924]{1,0:T(8,128)(2,1)S(1)}, bf16[64,924]{1,0:T(8,128)(2,1)}, u32[]{:S(2)}) copy-start(bf16[64,924]{1,0:T(8,128)(2,1)} %gate_ref.3) | copy-start | bytes 354820
  44.3 22.0 %copy-start.10 = (bf16[64,924]{1,0:T(8,128)(2,1)S(1)}, bf16[64,924]{1,0:T(8,128)(2,1)}, u32[]{:S(2)}) copy-start(bf16[64,924]{1,0:T(8,128)(2,1)} %up_ref.3) | copy-start | bytes 354820
  44.3 22.0 %all-to-all-start = ((bf16[8,64,924]{2,1,0:T(8,128)(2,1)}), bf16[8,64,924]{2,1,0:T(8,128)(2,1)S(1)}, u32[]{:S(2)}, u32[]{:S(2)}) async-start(bf16[8,64,924]{2,1,0:T(8,128)(2,1)} %get-tuple-element.14), calls=%async_computation | async-start | bytes 2097152 | tf_op jit(solution)/shard_map/all_to_all | solution.py:332
  51.4 10.8 %collective-permute-start.12 = (bf16[64,1024]{1,0:T(8,128)(2,1)S(1)}, bf16[64,1024]{1,0:T(8,128)(2,1)S(1)}, u32[]{:S(2)}, u32[]{:S(2)}) collective-permute-start(bf16[64,1024]{1,0:T(8,128)(2,1)S(1)} %get-tuple-element.15.four_ref), channel_id=1, source_target_pairs={{0,4},{4,8},{8,12},{12,16},{16,20},{20,24},{24,28},{28,0},{1,5},{5... | collective-permute-start | bytes 393224 | tf_op jit(solution)/shard_map/ppermute | solution.py:64
  51.5 10.7 %collective-permute-start.13 = (bf16[64,1024]{1,0:T(8,128)(2,1)S(1)}, bf16[64,1024]{1,0:T(8,128)(2,1)S(1)}, u32[]{:S(2)}, u32[]{:S(2)}) collective-permute-start(bf16[64,1024]{1,0:T(8,128)(2,1)S(1)} %get-tuple-element.15.four_ref), channel_id=1, source_target_pairs={{0,28},{4,0},{8,4},{12,8},{16,12},{20,16},{24,20},{28,24},{1,29},{... | collective-permute-start | bytes 393224 | tf_op jit(solution)/shard_map/ppermute | solution.py:65
  54.9 7.2 %collective-permute-start.14 = (bf16[32,1024]{1,0:T(8,128)(2,1)S(1)}, bf16[32,1024]{1,0:T(8,128)(2,1)S(1)}, u32[]{:S(2)}, u32[]{:S(2)}) collective-permute-start(bf16[32,1024]{1,0:T(8,128)(2,1)S(1)} %get-tuple-element.16), channel_id=1, source_target_pairs={{0,8},{4,12},{8,16},{12,20},{16,24},{20,28},{24,0},{28,4},{1,9},{5... | collective-permute-start | bytes 196616 | tf_op jit(solution)/shard_map/ppermute | solution.py:62
  55.0 7.2 %collective-permute-start.15 = (bf16[32,1024]{1,0:T(8,128)(2,1)S(1)}, bf16[32,1024]{1,0:T(8,128)(2,1)S(1)}, u32[]{:S(2)}, u32[]{:S(2)}) collective-permute-start(bf16[32,1024]{1,0:T(8,128)(2,1)S(1)} %get-tuple-element.16), channel_id=1, source_target_pairs={{0,24},{4,28},{8,0},{12,4},{16,8},{20,12},{24,16},{28,20},{1,25},{... | collective-permute-start | bytes 196616 | tf_op jit(solution)/shard_map/ppermute | solution.py:63
  66.6 29.6 %copy-start.2 = (bf16[1024,924]{0,1:T(8,128)(2,1)S(1)}, bf16[1024,924]{0,1:T(8,128)(2,1)}, u32[]{:S(2)}) copy-start(bf16[1024,924]{0,1:T(8,128)(2,1)} %param.11) | copy-start | bytes 5677060
  66.7 29.6 %copy-start.3 = (bf16[1024,924]{0,1:T(8,128)(2,1)S(1)}, bf16[1024,924]{0,1:T(8,128)(2,1)}, u32[]{:S(2)}) copy-start(bf16[1024,924]{0,1:T(8,128)(2,1)} %param.12) | copy-start | bytes 5677060
  98.6 4.6 %collective-permute-start.16 = (f32[256,1024]{1,0:T(8,128)S(1)}, f32[256,1024]{1,0:T(8,128)S(1)}, u32[]{:S(2)}, u32[]{:S(2)}) collective-permute-start(f32[256,1024]{1,0:T(8,128)S(1)} %get-tuple-element.18), channel_id=1, source_target_pairs={{0,1},{1,0},{2,3},{3,2},{4,5},{5,4},{6,7},{7,6},{8,9},{9,8},{10,11... | collective-permute-start | bytes 3145736 | tf_op jit(solution)/shard_map/ppermute | solution.py:70
  98.7 3.4 %collective-permute-start.17 = (bf16[256,1024]{1,0:T(8,128)(2,1)S(1)}, bf16[256,1024]{1,0:T(8,128)(2,1)S(1)}, u32[]{:S(2)}, u32[]{:S(2)}) collective-permute-start(bf16[256,1024]{1,0:T(8,128)(2,1)S(1)} %shard_map.109._.mine_ref), channel_id=1, source_target_pairs={{0,1},{1,0},{2,3},{3,2},{4,5},{5,4},{6,7},{7,6},{8,9},{9,8},{10,11... | collective-permute-start | bytes 1572872 | tf_op jit(solution)/shard_map/ppermute | solution.py:70
  102.2 1.0 copy-start.5
  103.2 5.9 %copy-start.1 = (bf16[512,924]{1,0:T(8,128)(2,1)S(1)}, bf16[512,924]{1,0:T(8,128)(2,1)}, u32[]{:S(2)}) copy-start(bf16[512,924]{1,0:T(8,128)(2,1)} %copy-done) | copy-start | bytes 2838532
  104.1 24.5 %all-to-all-start.2 = ((bf16[16,16,1024]{2,1,0:T(8,128)(2,1)}), bf16[16,16,1024]{2,1,0:T(8,128)(2,1)}, u32[]{:S(2)}, u32[]{:S(2)}) async-start(bf16[16,16,1024]{2,1,0:T(8,128)(2,1)} %bitcast.13), calls=%async_computation.2 | async-start | bytes 1048576 | tf_op jit(solution)/shard_map/all_to_all | solution.py:337
  112.8 1.2 copy-start.6
  (2 other events, 1.5 us)

commit v3 on v2

v3 whole, which is shorter than its diff:
```python
import functools

import jax
import jax.numpy as jnp
from jax import lax
from jax.experimental import pallas as pl
from jax.experimental.pallas import tpu as pltpu
from jax.sharding import PartitionSpec as P

F32 = jnp.float32
BF16 = jnp.bfloat16
BY_FEATURE = (((1,), (1,)), ((), ()))
BY_TOKEN = (((0,), (0,)), ((), ()))
ROWS = 16
NZ = 8

OWN = ((0, 0), (0, 1), (4, 0), (4, 1))
PREV = ((-1, 0), (-1, 1), (3, 0), (3, 1))
NEXT = ((1, 0), (1, 1), (5, 0), (5, 1))
PREV2 = ((-2, 0), (-2, 1))
NEXT2 = ((2, 0), (2, 1))
ORDER = OWN + PREV + NEXT + PREV2 + NEXT2


def gy_shift(step):
    return [(i, (i + step) % NZ) for i in range(NZ)]


def place_shift(step, flip):
    return [
        (z * 4 + g, ((z + step) % NZ) * 4 + (g ^ (2 * flip))) for z in range(NZ) for g in range(4)
    ]


OTHER_CORE = [(i, i ^ 1) for i in range(4)]
OTHER_Y = [(i, i ^ 2) for i in range(4)]
FAR_PLACES = [
    [(z + 4 * a) * 4 + 2 * y + core for a in range(2) for y in range(2)]
    for z in range(4)
    for core in range(2)
]
SAME_CORE = [[2 * k + core for k in range(16)] for core in range(2)]

ANY = pl.BlockSpec(memory_space=pl.ANY)
VMEM = pl.BlockSpec(memory_space=pltpu.VMEM)


def params(mib):
    return pltpu.CompilerParams(vmem_limit_bytes=mib * 2**20)


def row_of(there, second):
    z, y = lax.axis_index("gy"), lax.axis_index("gz") // 2
    step, flip = there
    block = second * 2 * NZ + lax.rem(z + step + NZ, NZ) * 2 + (y + flip - 2 * y * flip)
    return pl.multiple_of(block * ROWS, ROWS)


def near_places(near, four):
    return (
        lax.ppermute(near, "gy", gy_shift(2)),
        lax.ppermute(near, "gy", gy_shift(-2)),
        lax.ppermute(four, "gy", gy_shift(1)),
        lax.ppermute(four, "gy", gy_shift(-1)),
    )


def swap_core(x):
    return lax.ppermute(x, "gz", OTHER_CORE)


def pair_kernel(x_in, y_in, _, out_ref, held, sems):
    copies = [
        pltpu.make_async_copy(ref, held.at[pl.ds(k * ROWS, ROWS)], sems.at[k])
        for k, ref in enumerate((x_in, y_in))
    ]
    for copy in copies:
        copy.start()
    for copy in copies:
        copy.wait()
    for k in range(out_ref.shape[0]):
        out_ref[k] = held[...]


def pair_copies(x, y, earlier):
    rows, cols = x.shape
    return pl.pallas_call(
        pair_kernel,
        out_shape=jax.ShapeDtypeStruct((4, 2 * rows, cols), x.dtype),
        in_specs=[ANY] * 3,
        out_specs=VMEM,
        scratch_shapes=[pltpu.VMEM((2 * rows, cols), BF16), pltpu.SemaphoreType.DMA((2,))],
        compiler_params=params(58),
    )(x, y, earlier)


def far_places(x, y, earlier):
    return lax.all_to_all(
        pair_copies(x, y, earlier), ("gy", "gz"), 0, 0, axis_index_groups=FAR_PLACES
    )


def pack_kernel(far_ref, _, *outs):
    a, y = lax.axis_index("gy") // 4, lax.axis_index("gz") // 2
    for k, (far, flip) in enumerate(((0, 0), (0, 1), (1, 0), (1, 1))):
        there = (a + far - 2 * a * far) * 2 + (y + flip - 2 * y * flip)
        rows = pl.ds(k * ROWS, ROWS)
        for j in range(2):
            near_ref, four_ref = outs[2 * j : 2 * j + 2]
            block = far_ref[there, j * ROWS : (j + 1) * ROWS, :]
            four_ref[rows, :] = block
            if k < 2:
                near_ref[rows, :] = block


def pack(far, earlier):
    _, rows, cols = far.shape
    near = jax.ShapeDtypeStruct((rows, cols), far.dtype)
    four = jax.ShapeDtypeStruct((2 * rows, cols), far.dtype)
    return pl.pallas_call(
        pack_kernel,
        out_shape=(near, four, near, four),
        in_specs=[VMEM, ANY],
        out_specs=(VMEM,) * 4,
        compiler_params=params(4),
    )(far, earlier)


def merge_kernel(four_ref, prev_ref, next_ref, prev2_ref, next2_ref, *refs):
    out_ref = refs[-1]
    k = 0
    for ref in (four_ref, prev_ref, next_ref, prev2_ref, next2_ref):
        out_ref[pl.ds(k, ref.shape[0]), :] = ref[...]
        k += ref.shape[0]


def merge(four, got, earlier):
    prev2, next2, prev, following = got
    return pl.pallas_call(
        merge_kernel,
        out_shape=jax.ShapeDtypeStruct((16 * ROWS, four.shape[1]), four.dtype),
        in_specs=[VMEM] * 5 + [ANY] * len(earlier),
        out_specs=VMEM,
        compiler_params=params(4),
    )(four, prev, following, prev2, next2, *earlier)


def place_kernel(mine_ref, other_ref, out_ref):
    for k, there in enumerate(ORDER):
        rows = pl.ds(k * ROWS, ROWS)
        out_ref[pl.ds(row_of(there, 0), ROWS), :] = mine_ref[rows, :]
        out_ref[pl.ds(row_of(there, 1), ROWS), :] = other_ref[rows, :]


def place_rows(mine, other):
    rows, cols = mine.shape
    return pl.pallas_call(
        place_kernel,
        out_shape=jax.ShapeDtypeStruct((2 * rows, cols), mine.dtype),
        in_specs=[VMEM] * 2,
        out_specs=VMEM,
        compiler_params=params(8),
    )(mine, other)


def hidden_kernel(mine_ref, other_ref, weight_ref, *refs):
    cols_ref, out_ref = refs[-2:]
    place_kernel(mine_ref, other_ref, cols_ref)
    blocks, rows, units = out_ref.shape
    half = blocks * rows // 2
    for k in range(2):
        part = lax.dot_general(
            cols_ref[pl.ds(k * half, half), :],
            weight_ref[...],
            BY_FEATURE,
            preferred_element_type=F32,
        )
        out_ref[:, pl.ds(k * rows // 2, rows // 2), :] = part.astype(BF16).reshape(
            blocks, rows // 2, units
        )


def hidden_part(mine, other, weight, earlier):
    rows, cols = mine.shape
    return pl.pallas_call(
        hidden_kernel,
        out_shape=(
            jax.ShapeDtypeStruct((2 * rows, cols), BF16),
            jax.ShapeDtypeStruct((8, rows // 4, weight.shape[0]), BF16),
        ),
        in_specs=[VMEM] * 3 + [ANY] * len(earlier),
        out_specs=(VMEM, VMEM),
        compiler_params=params(16),
    )(mine, other, weight, *earlier)


def pre_kernel(gate_in, up_in, out_ref, held, sems):
    core = lax.axis_index("gz") % 2
    loads = [
        pltpu.make_async_copy(ref, held.at[k], sems.at[k]) for k, ref in enumerate((gate_in, up_in))
    ]
    for load in loads:
        load.start()
    for k, load in enumerate(loads):
        load.wait()
        blocks = [held[k, j * ROWS : (j + 1) * ROWS, :] for j in range(4)]
        for y in range(2):
            for second in range(2):
                out_ref[pl.ds((4 * k + 2 * second + y) * ROWS, ROWS), :] = jnp.where(
                    core == 0, blocks[2 * y + second], blocks[2 * y + 1 - second]
                )


def pack_pre(gate, up):
    rows, units = gate.shape
    return pl.pallas_call(
        pre_kernel,
        out_shape=jax.ShapeDtypeStruct((2 * rows, units), gate.dtype),
        in_specs=[ANY] * 2,
        out_specs=VMEM,
        scratch_shapes=[pltpu.VMEM((2, rows, units), BF16), pltpu.SemaphoreType.DMA((2,))],
        compiler_params=params(58),
    )(gate, up)


def sum_kernel(parts_ref, *refs):
    out_ref = refs[-1]
    total = parts_ref[0].astype(F32)
    for k in range(1, parts_ref.shape[0]):
        total = total + parts_ref[k].astype(F32)
    total = total.astype(BF16)
    for k in range(out_ref.shape[0]):
        out_ref[k] = total


def sum_copies(parts, earlier):
    return pl.pallas_call(
        sum_kernel,
        out_shape=jax.ShapeDtypeStruct(parts.shape, BF16),
        in_specs=[VMEM] + [ANY] * len(earlier),
        out_specs=VMEM,
        compiler_params=params(8),
    )(parts, *earlier)


def stack_kernel(x_ref, y_ref, out_ref):
    rows = x_ref.shape[0]
    out_ref[:rows, :] = x_ref[...]
    out_ref[rows:, :] = y_ref[...]


def stack(x, y):
    rows, cols = x.shape
    return pl.pallas_call(
        stack_kernel,
        out_shape=jax.ShapeDtypeStruct((2 * rows, cols), x.dtype),
        in_specs=[VMEM] * 2,
        out_specs=VMEM,
        compiler_params=params(4),
    )(x, y)


STEPS = (0, 2, 6, 4)


def blocks_of(pieces):
    me = lax.axis_index("gx")
    rows = pieces[0].shape[0] // 4
    for step, ref in zip(STEPS, pieces):
        block = lax.rem(me + 8 - step, 8)
        for k in range(2):
            yield block + k * (1 - 2 * lax.rem(block, 2)), ref, 2 * k * rows, rows


def hidden_rows_kernel(*refs):
    pieces, out_ref = refs[:4], refs[-1]
    for block, ref, first, rows in blocks_of(pieces):
        gate = ref[first : first + rows, :].astype(F32)
        up_value = ref[first + rows : first + 2 * rows, :].astype(F32)
        hidden = (gate * jax.nn.sigmoid(gate) * up_value).astype(BF16)
        for k in range(2):
            out_ref[k, block] = hidden[k * rows // 2 : (k + 1) * rows // 2, :]


def hidden_rows(pieces):
    rows, units = pieces[0].shape
    return pl.pallas_call(
        hidden_rows_kernel,
        out_shape=jax.ShapeDtypeStruct((2, 8, rows // 8, units), BF16),
        in_specs=[VMEM] * 4,
        out_specs=VMEM,
        compiler_params=params(12),
    )(*pieces)


def same_pair(x):
    return stack(x, lax.ppermute(x, "gx", [(i, i ^ 1) for i in range(8)]))


def along_x(pair):
    return [pair] + [
        lax.ppermute(pair, "gx", [(i, (i + step) % 8) for i in range(8)]) for step in (2, 6, 4)
    ]


def last_sum_kernel(parts_ref, out_ref):
    total = parts_ref[0].astype(F32)
    for k in range(1, parts_ref.shape[0]):
        total = total + parts_ref[k].astype(F32)
    out_ref[...] = total.astype(BF16)


def last_sum(parts):
    return pl.pallas_call(
        last_sum_kernel,
        out_shape=jax.ShapeDtypeStruct(parts.shape[1:], BF16),
        in_specs=[VMEM],
        out_specs=VMEM,
        compiler_params=params(4),
    )(parts)


def input_kernel(k, *refs):
    pieces, (hid_ref, gw_ref, uw_ref), refs = refs[:4], refs[4:7], refs[7:]
    part_ref, gg_ref, ug_ref = refs[-3:]
    half = hid_ref.shape[1] // 2
    gate_grads, up_grads, places = [], [], []
    for block, piece, first, rows in blocks_of(pieces):
        hidden_grad = hid_ref[block, k * half : (k + 1) * half, :].astype(F32)
        gate = piece[first + k * half : first + (k + 1) * half, :].astype(F32)
        first = first + rows
        up_value = piece[first + k * half : first + (k + 1) * half, :].astype(F32)
        sigmoid_gate = jax.nn.sigmoid(gate)
        gate_grad = hidden_grad * up_value * sigmoid_gate * (1.0 + gate * (1.0 - sigmoid_gate))
        gate_grads.append(gate_grad.astype(BF16))
        up_grads.append((hidden_grad * (gate * sigmoid_gate)).astype(BF16))
        places.append(block)
        gg_ref[k, block] = gate_grads[-1]
        ug_ref[k, block] = up_grads[-1]
    if len(refs) > 3:
        gg_ref[1 - k] = refs[0][1 - k]
        ug_ref[1 - k] = refs[1][1 - k]
    part = jnp.dot(
        jnp.concatenate(gate_grads, axis=0), gw_ref[...], preferred_element_type=F32
    ) + jnp.dot(jnp.concatenate(up_grads, axis=0), uw_ref[...], preferred_element_type=F32)
    for j, block in enumerate(places):
        part_ref[block] = part[j * half : (j + 1) * half, :]


def input_part(k, hidden_grad, pieces, gate_weight, up_weight, grads):
    blocks, rows, units = hidden_grad.shape
    half = jax.ShapeDtypeStruct((blocks, rows // 2, gate_weight.shape[1]), F32)
    grad = jax.ShapeDtypeStruct((2, blocks, rows // 2, units), BF16)
    return pl.pallas_call(
        functools.partial(input_kernel, k),
        out_shape=(half, grad, grad),
        in_specs=[VMEM] * (7 + len(grads)),
        out_specs=(VMEM,) * 3,
        compiler_params=params(12),
    )(*pieces, hidden_grad, gate_weight, up_weight, *grads)


def body(layer_input, out_grad, gate_pre, up_pre, gate_weight, up_weight, down_weight):
    pre = pack_pre(gate_pre, up_pre)
    far = far_places(out_grad, layer_input, pre)
    pre_pair = same_pair(pre)
    near, four, near_in, four_in = pack(far, pre_pair)
    pieces = along_x(pre_pair)
    mine = merge(four, near_places(near, four), pieces[1:])
    grad_cols, part = hidden_part(mine, swap_core(mine), down_weight, [])
    parts = lax.all_to_all(part, "gx", 0, 0)
    mine_in = merge(four_in, near_places(near_in, four_in), [])
    hidden_grad = lax.all_to_all(sum_copies(parts, [mine_in]), "gx", 0, 0)
    weights = (gate_weight.T, up_weight.T)
    send, gate_grad, up_grad = input_part(1, hidden_grad, pieces, *weights, [])
    keep, gate_grad, up_grad = input_part(
        0, hidden_grad, pieces, *weights, [gate_grad, up_grad]
    )
    total = (keep + swap_core(send)).astype(BF16).reshape(16, ROWS, -1)
    totals = lax.all_to_all(total, ("gy", "gz"), 0, 0, axis_index_groups=SAME_CORE)
    input_sum = last_sum(totals)
    hidden = hidden_rows(pieces)
    gate_grad, up_grad, hidden = (v.reshape(512, -1) for v in (gate_grad, up_grad, hidden))
    input_cols = place_rows(mine_in, swap_core(mine_in))
    gate_sum = lax.dot_general(input_cols, gate_grad, BY_TOKEN, preferred_element_type=F32)
    up_sum = lax.dot_general(input_cols, up_grad, BY_TOKEN, preferred_element_type=F32)
    down_sum = lax.dot_general(hidden, grad_cols, BY_TOKEN, preferred_element_type=F32)
    return (
        input_sum,
        gate_sum.astype(BF16),
        up_sum.astype(BF16),
        down_sum.astype(BF16),
    )


def solution(mesh):
    tokens = P(("gy", "gz"), "gx")
    hidden = P("gx", ("gy", "gz"))
    return jax.shard_map(
        body,
        mesh=mesh,
        in_specs=(tokens, tokens, hidden, hidden, hidden, hidden, tokens),
        out_specs=(tokens, hidden, hidden, tokens),
        check_vma=False,
    )
```

time: 131 us -> 124 us (0.947)
  blocking collectives: 29.6 us -> 18 us
  starting transfers between devices: 44.8 us -> 50.9 us
  Pallas kernels: 7.16 us -> 12.4 us
  local copies, waits for them, and re-layouts: 6.52 us -> 1.96 us
    all_to_all x1, blocking collectives: 29.6 us -> 18 us  [body(): hidden_grad = lax.all_to_all(sum_copies(parts, [mine_in]), 'gx', 0, 0)]
    ppermute x3 -> x0, starting transfers between devices: 8.99 us -> none  [the longest x1 7.19 us: far_places(): lax.ppermute(x, 'gy', gy_shift(4))]
    all_to_all x0 -> x1, starting transfers between devices: none -> 8.76 us  [far_places(): lax.all_to_all(pair_copies(x, y, earlier), ('gy', 'gz'), 0, 0, axis_index...]
    ppermute x3 -> x0, waiting for transfers between devices: 5.53 us -> none  [the longest x1 5.53 us: far_places(): lax.ppermute(x, ('gy', 'gz'), place_shift(4, 1))]
    pallas_call x5 -> x6, Pallas kernels: 2.9 us -> 8.2 us  [the longest x2 3.03 us: input_part(): pl.pallas_call(functools.partial(input_kernel, k), out_shape=(half, grad,...]
    all_to_all x0 -> x1, waiting for transfers between devices: none -> 4.78 us  [far_places(): lax.all_to_all(pair_copies(x, y, earlier), ('gy', 'gz'), 0, 0, axis_index...]
    unnamed x28 -> x20, local copies, waits for them, and re-layouts: 6.35 us -> 1.96 us
    all_to_all x1, starting transfers between devices: 4.99 us -> 8.85 us  [body(): lax.all_to_all(total, ('gy', 'gz'), 0, 0, axis_index_groups=SAME_CORE)]
  transfers between devices with their start and end apart: 20 -> 18, of which waited for: 9 -> 10; matrix products, arithmetic and copies ran while one was open for 7% -> 7% of each run, Pallas kernels for 0% -> 4%
where the time goes in v3:
time: 124 us
  starting transfers between devices  50.9 us (41%)
  waiting for transfers between devices  31.5 us (25%)
  blocking collectives  18 us (15%)
  Pallas kernels  12.4 us (10%)
  matrix products  7.34 us (6%)
  local copies, waits for them, and re-layouts  1.96 us (2%)
    all_to_all x1, blocking collectives, body(): hidden_grad = lax.all_to_all(sum_copies(parts, [mine_in]), 'gx', 0, 0)  18 us
    all_to_all x1, waiting for transfers between devices, body(): lax.all_to_all(total, ('gy', 'gz'), 0, 0, axis_index_groups=SAME_CORE)  10.4 us
    all_to_all x1, starting transfers between devices, body(): lax.all_to_all(total, ('gy', 'gz'), 0, 0, axis_index_groups=SAME_CORE)  8.85 us
    all_to_all x1, starting transfers between devices, far_places(): lax.all_to_all(pair_copies(x, y, earlier), ('gy', 'gz'), 0, 0, axis_index...  8.76 us
    ppermute x2, starting transfers between devices, near_places(): lax.ppermute(four, 'gy', gy_shift(-1))  6.29 us
    all_to_all x1, starting transfers between devices, body(): parts = lax.all_to_all(part, 'gx', 0, 0)  6 us
    ppermute x2, waiting for transfers between devices, near_places(): lax.ppermute(near, 'gy', gy_shift(2))  5.45 us
    ppermute x3, starting transfers between devices, along_x(): lax.ppermute(pair, 'gx', [(i, (i + step) % 8) for i in range(8)])  5.13 us
  transfers between devices with their start and end apart: 18, of which 10 were waited for; matrix products, arithmetic and copies ran while one was open for 7% of the time, Pallas kernels for 4%

profile of v3, /device:TPU:8, one launch (start us, length us, event | category | flops | bytes accessed | tf_op | source)
XLA Modules:
  0.0 123.9 jit_solution(11014204521587935346)
XLA Ops:
  0.6 1.7 %shard_map.102.x_ref._ = bf16[128,924]{1,0:T(8,128)(2,1)} custom-call(bf16[64,924]{1,0:T(8,128)(2,1)} %gate_in.1, bf16[64,924]{1,0:T(8,128)(2,1)} %up_in.1), custom_call_target="tpu_custom_call" | custom-call | tf_op jit(solution)/shard_map/pallas_call | solution.py:216
  2.3 2.3 %collective-permute-start = (bf16[128,924]{1,0:T(8,128)(2,1)}, bf16[128,924]{1,0:T(8,128)(2,1)S(1)}, u32[]{:S(2)}, u32[]{:S(2)}) collective-permute-start(bf16[128,924]{1,0:T(8,128)(2,1)} %shard_map.102.x_ref._), channel_id=1, source_target_pairs={{0,32},{32,0},{64,96},{96,64},{128,160},{160,128},{192,224},{224,1... | collective-permute-start | bytes 709640 | tf_op jit(solution)/shard_map/ppermute | solution.py:297
  4.6 1.5 %shard_map.104 = bf16[4,32,1024]{2,1,0:T(8,128)(2,1)} custom-call(bf16[16,1024]{1,0:T(8,128)(2,1)} %x_in.1, bf16[16,1024]{1,0:T(8,128)(2,1)} %y_in.1, bf16[128,924]{1,0:T(8,128)(2,1)} %shard_map.102.x_ref._), custom_call_target="tpu_custom_call" | custom-call | tf_op jit(solution)/shard_map/pallas_call | solution.py:87
  6.1 8.8 %all-to-all-start = ((bf16[4,32,1024]{2,1,0:T(8,128)(2,1)}), bf16[4,32,1024]{2,1,0:T(8,128)(2,1)S(1)}, u32[]{:S(2)}, u32[]{:S(2)}) async-start(bf16[4,32,1024]{2,1,0:T(8,128)(2,1)} %shard_map.104), calls=%async_computation | async-start | bytes 524288 | tf_op jit(solution)/shard_map/all_to_all | solution.py:98
  15.9 1.6 %collective-permute-start.1 = (bf16[256,924]{1,0:T(8,128)(2,1)S(1)}, bf16[256,924]{1,0:T(8,128)(2,1)S(1)}, u32[]{:S(2)}, u32[]{:S(2)}) collective-permute-start(bf16[256,924]{1,0:T(8,128)(2,1)S(1)} %shard_map.103._.refs_0_), channel_id=1, source_target_pairs={{0,64},{32,96},{64,128},{96,160},{128,192},{160,224},{192,0},{224,... | collective-permute-start | bytes 1419272 | tf_op jit(solution)/shard_map/ppermute | solution.py:302
  17.4 1.7 %collective-permute-start.2 = (bf16[256,924]{1,0:T(8,128)(2,1)S(1)}, bf16[256,924]{1,0:T(8,128)(2,1)S(1)}, u32[]{:S(2)}, u32[]{:S(2)}) collective-permute-start(bf16[256,924]{1,0:T(8,128)(2,1)S(1)} %shard_map.103._.refs_0_), channel_id=1, source_target_pairs={{0,192},{32,224},{64,0},{96,32},{128,64},{160,96},{192,128},{224,1... | collective-permute-start | bytes 1419272 | tf_op jit(solution)/shard_map/ppermute | solution.py:302
  19.2 1.8 %collective-permute-start.3 = (bf16[256,924]{1,0:T(8,128)(2,1)S(1)}, bf16[256,924]{1,0:T(8,128)(2,1)S(1)}, u32[]{:S(2)}, u32[]{:S(2)}) collective-permute-start(bf16[256,924]{1,0:T(8,128)(2,1)S(1)} %shard_map.103._.refs_0_), channel_id=1, source_target_pairs={{0,128},{32,160},{64,192},{96,224},{128,0},{160,32},{192,64},{224,... | collective-permute-start | bytes 1419272 | tf_op jit(solution)/shard_map/ppermute | solution.py:302
  21.0 4.8 %all-to-all-done.far_ref = bf16[4,32,1024]{2,1,0:T(8,128)(2,1)S(1)} async-done(((bf16[4,32,1024]{2,1,0:T(8,128)(2,1)}), bf16[4,32,1024]{2,1,0:T(8,128)(2,1)S(1)}, u32[]{:S(2)}, u32[]{:S(2)}) %all-to-all-start) | async-done | bytes 262176 | tf_op jit(solution)/shard_map/all_to_all | solution.py:98
  25.8 4.0 %collective-permute-start.6 = (bf16[32,1024]{1,0:T(8,128)(2,1)S(1)}, bf16[32,1024]{1,0:T(8,128)(2,1)S(1)}, u32[]{:S(2)}, u32[]{:S(2)}) collective-permute-start(bf16[32,1024]{1,0:T(8,128)(2,1)S(1)} %get-tuple-element.17), channel_id=1, source_target_pairs={{0,8},{4,12},{8,16},{12,20},{16,24},{20,28},{24,0},{28,4},{1,9},{5... | collective-permute-start | bytes 196616 | tf_op jit(solution)/shard_map/ppermute | solution.py:61
  30.0 2.7 %collective-permute-done.6.prev2_ref = bf16[32,1024]{1,0:T(8,128)(2,1)S(1)} collective-permute-done((bf16[32,1024]{1,0:T(8,128)(2,1)S(1)}, bf16[32,1024]{1,0:T(8,128)(2,1)S(1)}, u32[]{:S(2)}, u32[]{:S(2)}) %collective-permute-start.6) | collective-permute-done | bytes 65568 | tf_op jit(solution)/shard_map/ppermute | solution.py:61
  32.7 3.6 %collective-permute-start.4 = (bf16[64,1024]{1,0:T(8,128)(2,1)S(1)}, bf16[64,1024]{1,0:T(8,128)(2,1)S(1)}, u32[]{:S(2)}, u32[]{:S(2)}) collective-permute-start(bf16[64,1024]{1,0:T(8,128)(2,1)S(1)} %get-tuple-element.16.four_ref), channel_id=1, source_target_pairs={{0,4},{4,8},{8,12},{12,16},{16,20},{20,24},{24,28},{28,0},{1,5},{5... | collective-permute-start | bytes 393224 | tf_op jit(solution)/shard_map/ppermute | solution.py:63
  36.3 3.0 %collective-permute-start.5 = (bf16[64,1024]{1,0:T(8,128)(2,1)S(1)}, bf16[64,1024]{1,0:T(8,128)(2,1)S(1)}, u32[]{:S(2)}, u32[]{:S(2)}) collective-permute-start(bf16[64,1024]{1,0:T(8,128)(2,1)S(1)} %get-tuple-element.16.four_ref), channel_id=1, source_target_pairs={{0,28},{4,0},{8,4},{12,8},{16,12},{20,16},{24,20},{28,24},{1,29},{... | collective-permute-start | bytes 393224 | tf_op jit(solution)/shard_map/ppermute | solution.py:64
  39.3 2.5 %collective-permute-done.5.next_ref = bf16[64,1024]{1,0:T(8,128)(2,1)S(1)} collective-permute-done((bf16[64,1024]{1,0:T(8,128)(2,1)S(1)}, bf16[64,1024]{1,0:T(8,128)(2,1)S(1)}, u32[]{:S(2)}, u32[]{:S(2)}) %collective-permute-start.5) | collective-permute-done | bytes 131104 | tf_op jit(solution)/shard_map/ppermute | solution.py:64
  42.6 1.9 %collective-permute-done.8.other_ref = bf16[256,1024]{1,0:T(8,128)(2,1)S(1)} collective-permute-done((bf16[256,1024]{1,0:T(8,128)(2,1)S(1)}, bf16[256,1024]{1,0:T(8,128)(2,1)S(1)}, u32[]{:S(2)}, u32[]{:S(2)}) %collective-permute-start.8) | collective-permute-done | bytes 524320 | tf_op jit(solution)/shard_map/ppermute | solution.py:69
  44.5 2.3 %shard_map.107 = (bf16[512,1024]{1,0:T(8,128)(2,1)S(1)}, bf16[8,64,924]{2,1,0:T(8,128)(2,1)}) custom-call(bf16[256,1024]{1,0:T(8,128)(2,1)S(1)} %shard_map.106.mine_ref, bf16[256,1024]{1,0:T(8,128)(2,1)S(1)} %collective-permute-done.8.other_ref, bf16[924,1024]{1,0:T(8,128)(2,1)S(1)} %copy-done.3), custom_call_target="tpu_custom_call" | custom-call | tf_op jit(solution)/shard_map/pallas_call | solution.py:185
  47.8 6.0 %all-to-all-start.1 = ((bf16[8,64,924]{2,1,0:T(8,128)(2,1)}), bf16[8,64,924]{2,1,0:T(8,128)(2,1)}, u32[]{:S(2)}, u32[]{:S(2)}) async-start(bf16[8,64,924]{2,1,0:T(8,128)(2,1)} %get-tuple-element.18), calls=%async_computation.1 | async-start | bytes 2097152 | tf_op jit(solution)/shard_map/all_to_all | solution.py:371
  53.8 1.0 collective-permute-start.9
  54.8 3.3 %collective-permute-start.10 = (bf16[64,1024]{1,0:T(8,128)(2,1)S(1)}, bf16[64,1024]{1,0:T(8,128)(2,1)S(1)}, u32[]{:S(2)}, u32[]{:S(2)}) collective-permute-start(bf16[64,1024]{1,0:T(8,128)(2,1)S(1)} %get-tuple-element.19.four_ref), channel_id=1, source_target_pairs={{0,28},{4,0},{8,4},{12,8},{16,12},{20,16},{24,20},{28,24},{1,29},{... | collective-permute-start | bytes 393224 | tf_op jit(solution)/shard_map/ppermute | solution.py:64
  58.1 4.1 %collective-permute-start.12 = (bf16[32,1024]{1,0:T(8,128)(2,1)S(1)}, bf16[32,1024]{1,0:T(8,128)(2,1)S(1)}, u32[]{:S(2)}, u32[]{:S(2)}) collective-permute-start(bf16[32,1024]{1,0:T(8,128)(2,1)S(1)} %get-tuple-element.20), channel_id=1, source_target_pairs={{0,24},{4,28},{8,0},{12,4},{16,8},{20,12},{24,16},{28,20},{1,25},{... | collective-permute-start | bytes 196616 | tf_op jit(solution)/shard_map/ppermute | solution.py:62
  62.2 2.8 %collective-permute-done.11.prev2_ref = bf16[32,1024]{1,0:T(8,128)(2,1)S(1)} collective-permute-done((bf16[32,1024]{1,0:T(8,128)(2,1)S(1)}, bf16[32,1024]{1,0:T(8,128)(2,1)S(1)}, u32[]{:S(2)}, u32[]{:S(2)}) %collective-permute-start.11) | collective-permute-done | bytes 65568 | tf_op jit(solution)/shard_map/ppermute | solution.py:61
  65.9 3.9 %all-to-all-done.1.parts_ref = bf16[8,64,924]{2,1,0:T(8,128)(2,1)} async-done(((bf16[8,64,924]{2,1,0:T(8,128)(2,1)}), bf16[8,64,924]{2,1,0:T(8,128)(2,1)}, u32[]{:S(2)}, u32[]{:S(2)}) %all-to-all-start.1) | async-done | bytes 946208 | tf_op jit(solution)/shard_map/all_to_all | solution.py:371
  69.8 1.5 %shard_map.109 = bf16[8,64,924]{2,1,0:T(8,128)(2,1)S(1)} custom-call(bf16[8,64,924]{2,1,0:T(8,128)(2,1)} %all-to-all-done.1.parts_ref, bf16[256,1024]{1,0:T(8,128)(2,1)S(1)} %shard_map.108.refs_0_.mine_ref), custom_call_target="tpu_custom_call" | custom-call | tf_op jit(solution)/shard_map/pallas_call | solution.py:237
  71.3 18.0 %all_to_all.20.refs_4_ = bf16[8,64,924]{2,1,0:T(8,128)(2,1)S(1)} all-to-all(bf16[8,64,924]{2,1,0:T(8,128)(2,1)S(1)} %shard_map.109), channel_id=1, replica_groups=mesh['gx'=8,'gy'=8,'gz'=4] {'gx'}, dimensions={0} | all-to-all | bytes 1892352 | tf_op jit(solution)/shard_map/all_to_all | solution.py:373
  89.3 1.4 %shard_map.110 = (f32[8,32,1024]{2,1,0:T(8,128)S(1)}, bf16[2,8,32,924]{3,2,1,0:T(8,128)(2,1)S(1)}, bf16[2,8,32,924]{3,2,1,0:T(8,128)(2,1)S(1)}) custom-call(bf16[256,924]{1,0:T(8,128)(2,1)S(1)} %shard_map.103._.refs_0_, bf16[256,924]{1,0:T(8,128)(2,1)S(1)} %collective-permute-done.1.refs_0_.refs_1_, ...), custom_call_target="tpu_custom_call" | custom-call | tf_op jit(solution)/shard_map/pallas_call | solution.py:354
  91.4 1.6 %shard_map.111 = (f32[8,32,1024]{2,1,0:T(8,128)S(1)}, bf16[2,8,32,924]{3,2,1,0:T(8,128)(2,1)S(1)}, bf16[2,8,32,924]{3,2,1,0:T(8,128)(2,1)S(1)}) custom-call(bf16[256,924]{1,0:T(8,128)(2,1)S(1)} %shard_map.103._.refs_0_, bf16[256,924]{1,0:T(8,128)(2,1)S(1)} %collective-permute-done.1.refs_0_.refs_1_, ...), custom_call_target="tpu_custom_call" | custom-call | tf_op jit(solution)/shard_map/pallas_call | solution.py:354
  93.0 1.0 collective-permute-done.13
  95.0 8.9 %all-to-all-start.3 = ((bf16[16,16,1024]{2,1,0:T(8,128)(2,1)}), bf16[16,16,1024]{2,1,0:T(8,128)(2,1)S(1)}, u32[]{:S(2)}, u32[]{:S(2)}) async-start(bf16[16,16,1024]{2,1,0:T(8,128)(2,1)} %bitcast.19), calls=%async_computation.3 | async-start | bytes 1048576 | tf_op jit(solution)/shard_map/all_to_all | solution.py:380
  104.3 1.1 shard_map.113
  105.5 2.4 %convolution_convert_fusion = bf16[924,1024]{1,0:T(8,128)(2,1)} fusion(bf16[512,924]{1,0:T(8,128)(2,1)S(1)} %bitcast.16, bf16[512,1024]{1,0:T(8,128)(2,1)S(1)} %copy-done.5), kind=kOutput, calls=%fused_computation | convolution fusion | flops 969830400 | bytes 3887104 | tf_op jit(solution)/shard_map/dot_general | solution.py:387
  107.9 2.4 %convolution_convert_fusion.2 = bf16[1024,924]{0,1:T(8,128)(2,1)} fusion(bf16[512,1024]{1,0:T(8,128)(2,1)S(1)} %shard_map.113, bf16[512,924]{1,0:T(8,128)(2,1)S(1)} %bitcast.18), kind=kOutput, calls=%fused_computation.2 | convolution fusion | flops 969830400 | bytes 3887104 | tf_op jit(solution)/shard_map/dot_general | solution.py:385
  110.4 2.4 %convolution_convert_fusion.1 = bf16[1024,924]{0,1:T(8,128)(2,1)} fusion(bf16[512,1024]{1,0:T(8,128)(2,1)S(1)} %shard_map.113, bf16[512,924]{1,0:T(8,128)(2,1)S(1)} %bitcast.17), kind=kOutput, calls=%fused_computation.1 | convolution fusion | flops 969830400 | bytes 3887104 | tf_op jit(solution)/shard_map/dot_general | solution.py:386
  112.8 10.4 %all-to-all-done.3.parts_ref = bf16[16,16,1024]{2,1,0:T(8,128)(2,1)S(1)} async-done(((bf16[16,16,1024]{2,1,0:T(8,128)(2,1)}), bf16[16,16,1024]{2,1,0:T(8,128)(2,1)S(1)}, u32[]{:S(2)}, u32[]{:S(2)}) %all-to-all-start.3) | async-done | bytes 524320 | tf_op jit(solution)/shard_map/all_to_all | solution.py:380
  (42 shorter events, 6.7 us)
Async XLA Ops:
  2.3 12.6 %collective-permute-start = (bf16[128,924]{1,0:T(8,128)(2,1)}, bf16[128,924]{1,0:T(8,128)(2,1)S(1)}, u32[]{:S(2)}, u32[]{:S(2)}) collective-permute-start(bf16[128,924]{1,0:T(8,128)(2,1)} %shard_map.102.x_ref._), channel_id=1, source_target_pairs={{0,32},{32,0},{64,96},{96,64},{128,160},{160,128},{192,224},{224,1... | collective-permute-start | bytes 709640 | tf_op jit(solution)/shard_map/ppermute | solution.py:297
  6.1 19.7 %all-to-all-start = ((bf16[4,32,1024]{2,1,0:T(8,128)(2,1)}), bf16[4,32,1024]{2,1,0:T(8,128)(2,1)S(1)}, u32[]{:S(2)}, u32[]{:S(2)}) async-start(bf16[4,32,1024]{2,1,0:T(8,128)(2,1)} %shard_map.104), calls=%async_computation | async-start | bytes 524288 | tf_op jit(solution)/shard_map/all_to_all | solution.py:98
  14.9 1.0 copy-start.2
  15.9 26.0 %collective-permute-start.1 = (bf16[256,924]{1,0:T(8,128)(2,1)S(1)}, bf16[256,924]{1,0:T(8,128)(2,1)S(1)}, u32[]{:S(2)}, u32[]{:S(2)}) collective-permute-start(bf16[256,924]{1,0:T(8,128)(2,1)S(1)} %shard_map.103._.refs_0_), channel_id=1, source_target_pairs={{0,64},{32,96},{64,128},{96,160},{128,192},{160,224},{192,0},{224,... | collective-permute-start | bytes 1419272 | tf_op jit(solution)/shard_map/ppermute | solution.py:302
  17.4 24.4 %collective-permute-start.2 = (bf16[256,924]{1,0:T(8,128)(2,1)S(1)}, bf16[256,924]{1,0:T(8,128)(2,1)S(1)}, u32[]{:S(2)}, u32[]{:S(2)}) collective-permute-start(bf16[256,924]{1,0:T(8,128)(2,1)S(1)} %shard_map.103._.refs_0_), channel_id=1, source_target_pairs={{0,192},{32,224},{64,0},{96,32},{128,64},{160,96},{192,128},{224,1... | collective-permute-start | bytes 1419272 | tf_op jit(solution)/shard_map/ppermute | solution.py:302
  19.2 23.3 %collective-permute-start.3 = (bf16[256,924]{1,0:T(8,128)(2,1)S(1)}, bf16[256,924]{1,0:T(8,128)(2,1)S(1)}, u32[]{:S(2)}, u32[]{:S(2)}) collective-permute-start(bf16[256,924]{1,0:T(8,128)(2,1)S(1)} %shard_map.103._.refs_0_), channel_id=1, source_target_pairs={{0,128},{32,160},{64,192},{96,224},{128,0},{160,32},{192,64},{224,... | collective-permute-start | bytes 1419272 | tf_op jit(solution)/shard_map/ppermute | solution.py:302
  25.8 18.7 %copy-start.3 = (bf16[924,1024]{1,0:T(8,128)(2,1)S(1)}, bf16[924,1024]{1,0:T(8,128)(2,1)}, u32[]{:S(2)}) copy-start(bf16[924,1024]{1,0:T(8,128)(2,1)} %weight_ref.1) | copy-start | bytes 5677060
  25.8 6.9 %collective-permute-start.6 = (bf16[32,1024]{1,0:T(8,128)(2,1)S(1)}, bf16[32,1024]{1,0:T(8,128)(2,1)S(1)}, u32[]{:S(2)}, u32[]{:S(2)}) collective-permute-start(bf16[32,1024]{1,0:T(8,128)(2,1)S(1)} %get-tuple-element.17), channel_id=1, source_target_pairs={{0,8},{4,12},{8,16},{12,20},{16,24},{20,28},{24,0},{28,4},{1,9},{5... | collective-permute-start | bytes 196616 | tf_op jit(solution)/shard_map/ppermute | solution.py:61
  29.8 6.5 %collective-permute-start.7 = (bf16[32,1024]{1,0:T(8,128)(2,1)S(1)}, bf16[32,1024]{1,0:T(8,128)(2,1)S(1)}, u32[]{:S(2)}, u32[]{:S(2)}) collective-permute-start(bf16[32,1024]{1,0:T(8,128)(2,1)S(1)} %get-tuple-element.17), channel_id=1, source_target_pairs={{0,24},{4,28},{8,0},{12,4},{16,8},{20,12},{24,16},{28,20},{1,25},{... | collective-permute-start | bytes 196616 | tf_op jit(solution)/shard_map/ppermute | solution.py:62
  32.7 6.6 %collective-permute-start.4 = (bf16[64,1024]{1,0:T(8,128)(2,1)S(1)}, bf16[64,1024]{1,0:T(8,128)(2,1)S(1)}, u32[]{:S(2)}, u32[]{:S(2)}) collective-permute-start(bf16[64,1024]{1,0:T(8,128)(2,1)S(1)} %get-tuple-element.16.four_ref), channel_id=1, source_target_pairs={{0,4},{4,8},{8,12},{12,16},{16,20},{20,24},{24,28},{28,0},{1,5},{5... | collective-permute-start | bytes 393224 | tf_op jit(solution)/shard_map/ppermute | solution.py:63
  36.3 5.5 %collective-permute-start.5 = (bf16[64,1024]{1,0:T(8,128)(2,1)S(1)}, bf16[64,1024]{1,0:T(8,128)(2,1)S(1)}, u32[]{:S(2)}, u32[]{:S(2)}) collective-permute-start(bf16[64,1024]{1,0:T(8,128)(2,1)S(1)} %get-tuple-element.16.four_ref), channel_id=1, source_target_pairs={{0,28},{4,0},{8,4},{12,8},{16,12},{20,16},{24,20},{28,24},{1,29},{... | collective-permute-start | bytes 393224 | tf_op jit(solution)/shard_map/ppermute | solution.py:64
  42.5 2.0 %collective-permute-start.8 = (bf16[256,1024]{1,0:T(8,128)(2,1)S(1)}, bf16[256,1024]{1,0:T(8,128)(2,1)S(1)}, u32[]{:S(2)}, u32[]{:S(2)}) collective-permute-start(bf16[256,1024]{1,0:T(8,128)(2,1)S(1)} %shard_map.106.mine_ref), channel_id=1, source_target_pairs={{0,1},{1,0},{2,3},{3,2},{4,5},{5,4},{6,7},{7,6},{8,9},{9,8},{10,11... | collective-permute-start | bytes 1572872 | tf_op jit(solution)/shard_map/ppermute | solution.py:69
  46.8 1.0 copy-start.4
  47.8 22.0 %all-to-all-start.1 = ((bf16[8,64,924]{2,1,0:T(8,128)(2,1)}), bf16[8,64,924]{2,1,0:T(8,128)(2,1)}, u32[]{:S(2)}, u32[]{:S(2)}) async-start(bf16[8,64,924]{2,1,0:T(8,128)(2,1)} %get-tuple-element.18), calls=%async_computation.1 | async-start | bytes 2097152 | tf_op jit(solution)/shard_map/all_to_all | solution.py:371
  53.8 12.1 %collective-permute-start.9 = (bf16[64,1024]{1,0:T(8,128)(2,1)S(1)}, bf16[64,1024]{1,0:T(8,128)(2,1)S(1)}, u32[]{:S(2)}, u32[]{:S(2)}) collective-permute-start(bf16[64,1024]{1,0:T(8,128)(2,1)S(1)} %get-tuple-element.19.four_ref), channel_id=1, source_target_pairs={{0,4},{4,8},{8,12},{12,16},{16,20},{20,24},{24,28},{28,0},{1,5},{5... | collective-permute-start | bytes 393224 | tf_op jit(solution)/shard_map/ppermute | solution.py:63
  54.8 11.1 %collective-permute-start.10 = (bf16[64,1024]{1,0:T(8,128)(2,1)S(1)}, bf16[64,1024]{1,0:T(8,128)(2,1)S(1)}, u32[]{:S(2)}, u32[]{:S(2)}) collective-permute-start(bf16[64,1024]{1,0:T(8,128)(2,1)S(1)} %get-tuple-element.19.four_ref), channel_id=1, source_target_pairs={{0,28},{4,0},{8,4},{12,8},{16,12},{20,16},{24,20},{28,24},{1,29},{... | collective-permute-start | bytes 393224 | tf_op jit(solution)/shard_map/ppermute | solution.py:64
  58.1 6.9 %collective-permute-start.11 = (bf16[32,1024]{1,0:T(8,128)(2,1)S(1)}, bf16[32,1024]{1,0:T(8,128)(2,1)S(1)}, u32[]{:S(2)}, u32[]{:S(2)}) collective-permute-start(bf16[32,1024]{1,0:T(8,128)(2,1)S(1)} %get-tuple-element.20), channel_id=1, source_target_pairs={{0,8},{4,12},{8,16},{12,20},{16,24},{20,28},{24,0},{28,4},{1,9},{5... | collective-permute-start | bytes 196616 | tf_op jit(solution)/shard_map/ppermute | solution.py:61
  58.1 7.8 %collective-permute-start.12 = (bf16[32,1024]{1,0:T(8,128)(2,1)S(1)}, bf16[32,1024]{1,0:T(8,128)(2,1)S(1)}, u32[]{:S(2)}, u32[]{:S(2)}) collective-permute-start(bf16[32,1024]{1,0:T(8,128)(2,1)S(1)} %get-tuple-element.20), channel_id=1, source_target_pairs={{0,24},{4,28},{8,0},{12,4},{16,8},{20,12},{24,16},{28,20},{1,25},{... | collective-permute-start | bytes 196616 | tf_op jit(solution)/shard_map/ppermute | solution.py:62
  69.8 19.6 %copy-start = (bf16[1024,924]{0,1:T(8,128)(2,1)S(1)}, bf16[1024,924]{0,1:T(8,128)(2,1)}, u32[]{:S(2)}) copy-start(bf16[1024,924]{0,1:T(8,128)(2,1)} %param.11) | copy-start | bytes 5677060
  69.8 19.6 %copy-start.1 = (bf16[1024,924]{0,1:T(8,128)(2,1)S(1)}, bf16[1024,924]{0,1:T(8,128)(2,1)}, u32[]{:S(2)}) copy-start(bf16[1024,924]{0,1:T(8,128)(2,1)} %param.12) | copy-start | bytes 5677060
  90.8 3.2 %collective-permute-start.13 = (f32[8,32,1024]{2,1,0:T(8,128)S(1)}, f32[8,32,1024]{2,1,0:T(8,128)S(1)}, u32[]{:S(2)}, u32[]{:S(2)}) collective-permute-start(f32[8,32,1024]{2,1,0:T(8,128)S(1)} %get-tuple-element.24), channel_id=1, source_target_pairs={{0,1},{1,0},{2,3},{3,2},{4,5},{5,4},{6,7},{7,6},{8,9},{9,8},{10,11... | collective-permute-start | bytes 3145736 | tf_op jit(solution)/shard_map/ppermute | solution.py:69
  90.9 13.4 %collective-permute-start.14 = (bf16[256,1024]{1,0:T(8,128)(2,1)S(1)}, bf16[256,1024]{1,0:T(8,128)(2,1)}, u32[]{:S(2)}, u32[]{:S(2)}) collective-permute-start(bf16[256,1024]{1,0:T(8,128)(2,1)S(1)} %shard_map.108.refs_0_.mine_ref), channel_id=1, source_target_pairs={{0,1},{1,0},{2,3},{3,2},{4,5},{5,4},{6,7},{7,6},{8,9},{9,8},{10,11... | collective-permute-start | bytes 1572872 | tf_op jit(solution)/shard_map/ppermute | solution.py:69
  93.0 2.0 %copy-start.6 = (bf16[2,8,32,924]{3,2,1,0:T(8,128)(2,1)}, bf16[2,8,32,924]{3,2,1,0:T(8,128)(2,1)S(1)}, u32[]{:S(2)}) copy-start(bf16[2,8,32,924]{3,2,1,0:T(8,128)(2,1)S(1)} %get-tuple-element.26) | copy-start | bytes 2838532
  93.0 2.0 %copy-start.8 = (bf16[2,8,32,924]{3,2,1,0:T(8,128)(2,1)}, bf16[2,8,32,924]{3,2,1,0:T(8,128)(2,1)S(1)}, u32[]{:S(2)}) copy-start(bf16[2,8,32,924]{3,2,1,0:T(8,128)(2,1)S(1)} %get-tuple-element.25) | copy-start | bytes 2838532
  95.0 28.3 %all-to-all-start.3 = ((bf16[16,16,1024]{2,1,0:T(8,128)(2,1)}), bf16[16,16,1024]{2,1,0:T(8,128)(2,1)S(1)}, u32[]{:S(2)}, u32[]{:S(2)}) async-start(bf16[16,16,1024]{2,1,0:T(8,128)(2,1)} %bitcast.19), calls=%async_computation.3 | async-start | bytes 1048576 | tf_op jit(solution)/shard_map/all_to_all | solution.py:380
  103.8 1.6 %copy-start.5 = (bf16[512,1024]{1,0:T(8,128)(2,1)S(1)}, bf16[512,1024]{1,0:T(8,128)(2,1)}, u32[]{:S(2)}) copy-start(bf16[512,1024]{1,0:T(8,128)(2,1)} %copy-done.4) | copy-start | bytes 3145732
  105.5 2.5 %copy-start.9 = (bf16[2,8,32,924]{3,2,1,0:T(8,128)(2,1)S(1)}, bf16[2,8,32,924]{3,2,1,0:T(8,128)(2,1)}, u32[]{:S(2)}) copy-start(bf16[2,8,32,924]{3,2,1,0:T(8,128)(2,1)} %copy-done.8) | copy-start | bytes 2838532
  107.9 2.5 %copy-start.7 = (bf16[2,8,32,924]{3,2,1,0:T(8,128)(2,1)S(1)}, bf16[2,8,32,924]{3,2,1,0:T(8,128)(2,1)}, u32[]{:S(2)}) copy-start(bf16[2,8,32,924]{3,2,1,0:T(8,128)(2,1)} %copy-done.6) | copy-start | bytes 2838532

commit v4 on v3

--- a/solution.py
+++ b/solution.py
@@ -26,14 +26,7 @@
     return [(i, (i + step) % NZ) for i in range(NZ)]
 
 
-def place_shift(step, flip):
-    return [
-        (z * 4 + g, ((z + step) % NZ) * 4 + (g ^ (2 * flip))) for z in range(NZ) for g in range(4)
-    ]
-
-
 OTHER_CORE = [(i, i ^ 1) for i in range(4)]
-OTHER_Y = [(i, i ^ 2) for i in range(4)]
 FAR_PLACES = [
     [(z + 4 * a) * 4 + 2 * y + core for a in range(2) for y in range(2)]
     for z in range(4)
@@ -69,35 +62,45 @@
     return lax.ppermute(x, "gz", OTHER_CORE)
 
 
-def pair_kernel(x_in, y_in, _, out_ref, held, sems):
-    copies = [
-        pltpu.make_async_copy(ref, held.at[pl.ds(k * ROWS, ROWS)], sems.at[k])
-        for k, ref in enumerate((x_in, y_in))
+def front_kernel(*refs):
+    ins, (far_ref, pre_ref, tokens, held, sems) = refs[:4], refs[4:]
+    parts = (tokens.at[pl.ds(0, ROWS)], tokens.at[pl.ds(ROWS, ROWS)], held.at[0], held.at[1])
+    loads = [
+        pltpu.make_async_copy(src, dst, sems.at[k]) for k, (src, dst) in enumerate(zip(ins, parts))
     ]
-    for copy in copies:
-        copy.start()
-    for copy in copies:
-        copy.wait()
-    for k in range(out_ref.shape[0]):
-        out_ref[k] = held[...]
-
-
-def pair_copies(x, y, earlier):
-    rows, cols = x.shape
-    return pl.pallas_call(
-        pair_kernel,
-        out_shape=jax.ShapeDtypeStruct((4, 2 * rows, cols), x.dtype),
-        in_specs=[ANY] * 3,
-        out_specs=VMEM,
-        scratch_shapes=[pltpu.VMEM((2 * rows, cols), BF16), pltpu.SemaphoreType.DMA((2,))],
+    for load in loads:
+        load.start()
+    for load in loads:
+        load.wait()
+    core = lax.axis_index("gz") % 2
+    for k in range(2):
+        blocks = [held[k, j * ROWS : (j + 1) * ROWS, :] for j in range(4)]
+        for y in range(2):
+            for second in range(2):
+                pre_ref[pl.ds((4 * k + 2 * second + y) * ROWS, ROWS), :] = jnp.where(
+                    core == 0, blocks[2 * y + second], blocks[2 * y + 1 - second]
+                )
+    for k in range(far_ref.shape[0]):
+        far_ref[k] = tokens[...]
+
+
+def front(x, y, gate, up):
+    rows, units = gate.shape
+    return pl.pallas_call(
+        front_kernel,
+        out_shape=(
+            jax.ShapeDtypeStruct((4, 2 * ROWS, x.shape[1]), BF16),
+            jax.ShapeDtypeStruct((2 * rows, units), BF16),
+        ),
+        in_specs=[ANY] * 4,
+        out_specs=(VMEM, VMEM),
+        scratch_shapes=[
+            pltpu.VMEM((2 * ROWS, x.shape[1]), BF16),
+            pltpu.VMEM((2, rows, units), BF16),
+            pltpu.SemaphoreType.DMA((4,)),
+        ],
         compiler_params=params(58),
-    )(x, y, earlier)
-
-
-def far_places(x, y, earlier):
-    return lax.all_to_all(
-        pair_copies(x, y, earlier), ("gy", "gz"), 0, 0, axis_index_groups=FAR_PLACES
-    )
+    )(x, y, gate, up)
 
 
 def pack_kernel(far_ref, _, *outs):
@@ -192,35 +195,6 @@
         out_specs=(VMEM, VMEM),
         compiler_params=params(16),
     )(mine, other, weight, *earlier)
-
-
-def pre_kernel(gate_in, up_in, out_ref, held, sems):
-    core = lax.axis_index("gz") % 2
-    loads = [
-        pltpu.make_async_copy(ref, held.at[k], sems.at[k]) for k, ref in enumerate((gate_in, up_in))
-    ]
-    for load in loads:
-        load.start()
-    for k, load in enumerate(loads):
-        load.wait()
-        blocks = [held[k, j * ROWS : (j + 1) * ROWS, :] for j in range(4)]
-        for y in range(2):
-            for second in range(2):
-                out_ref[pl.ds((4 * k + 2 * second + y) * ROWS, ROWS), :] = jnp.where(
-                    core == 0, blocks[2 * y + second], blocks[2 * y + 1 - second]
-                )
-
-
-def pack_pre(gate, up):
-    rows, units = gate.shape
-    return pl.pallas_call(
-        pre_kernel,
-        out_shape=jax.ShapeDtypeStruct((2 * rows, units), gate.dtype),
-        in_specs=[ANY] * 2,
-        out_specs=VMEM,
-        scratch_shapes=[pltpu.VMEM((2, rows, units), BF16), pltpu.SemaphoreType.DMA((2,))],
-        compiler_params=params(58),
-    )(gate, up)
 
 
 def sum_kernel(parts_ref, *refs):
@@ -361,8 +335,8 @@
 
 
 def body(layer_input, out_grad, gate_pre, up_pre, gate_weight, up_weight, down_weight):
-    pre = pack_pre(gate_pre, up_pre)
-    far = far_places(out_grad, layer_input, pre)
+    copies, pre = front(out_grad, layer_input, gate_pre, up_pre)
+    far = lax.all_to_all(copies, ("gy", "gz"), 0, 0, axis_index_groups=FAR_PLACES)
     pre_pair = same_pair(pre)
     near, four, near_in, four_in = pack(far, pre_pair)
     pieces = along_x(pre_pair)

time: 124 us -> 123 us (level)
  Pallas kernels: 12.4 us -> 11.1 us
    pallas_call x2 -> x1, Pallas kernels: 3.2 us -> 1.85 us  [front(): pl.pallas_call(front_kernel, out_shape=(jax.ShapeDtypeStruct((4, 2 * ROWS...]
  transfers between devices with their start and end apart: 18 -> 18, of which waited for: 10 -> 10; matrix products, arithmetic and copies ran while one was open for 7% -> 7% of each run, Pallas kernels for 4% -> 3%
where the time goes in v4:
time: 123 us
  starting transfers between devices  50.9 us (41%)
  waiting for transfers between devices  31.5 us (26%)
  blocking collectives  18.1 us (15%)
  Pallas kernels  11.1 us (9%)
  matrix products  7.34 us (6%)
  local copies, waits for them, and re-layouts  1.96 us (2%)
    all_to_all x1, blocking collectives, body(): hidden_grad = lax.all_to_all(sum_copies(parts, [mine_in]), 'gx', 0, 0)  18.1 us
    all_to_all x1, waiting for transfers between devices, body(): lax.all_to_all(total, ('gy', 'gz'), 0, 0, axis_index_groups=SAME_CORE)  10.4 us
    all_to_all x1, starting transfers between devices, body(): lax.all_to_all(total, ('gy', 'gz'), 0, 0, axis_index_groups=SAME_CORE)  8.88 us
    all_to_all x1, starting transfers between devices, body(): lax.all_to_all(copies, ('gy', 'gz'), 0, 0, axis_index_groups=FAR_PLACES)  8.75 us
    ppermute x2, starting transfers between devices, near_places(): lax.ppermute(four, 'gy', gy_shift(-1))  6.29 us
    all_to_all x1, starting transfers between devices, body(): parts = lax.all_to_all(part, 'gx', 0, 0)  5.98 us
    ppermute x2, waiting for transfers between devices, near_places(): lax.ppermute(near, 'gy', gy_shift(2))  5.48 us
    ppermute x3, starting transfers between devices, along_x(): lax.ppermute(pair, 'gx', [(i, (i + step) % 8) for i in range(8)])  5.13 us
  transfers between devices with their start and end apart: 18, of which 10 were waited for; matrix products, arithmetic and copies ran while one was open for 7% of the time, Pallas kernels for 3%

profile of v4, /device:TPU:8, one launch (start us, length us, event | category | flops | bytes accessed | tf_op | source)
XLA Modules:
  0.0 122.5 jit_solution(11721963696732041616)
XLA Ops:
  0.6 1.9 %shard_map.102 = (bf16[4,32,1024]{2,1,0:T(8,128)(2,1)}, bf16[128,924]{1,0:T(8,128)(2,1)}) custom-call(bf16[16,1024]{1,0:T(8,128)(2,1)} %refs_0_.1, bf16[16,1024]{1,0:T(8,128)(2,1)} %refs_1_.1, bf16[64,924]{1,0:T(8,128)(2,1)} %refs_2_.1, bf16[64,924]{1,0:T(8,128)(2,1)} %refs_3_.1), custom_call_target="tpu_custom_call" | custom-call | tf_op jit(solution)/shard_map/pallas_call | solution.py:89
  2.5 2.3 %collective-permute-start = (bf16[128,924]{1,0:T(8,128)(2,1)}, bf16[128,924]{1,0:T(8,128)(2,1)S(1)}, u32[]{:S(2)}, u32[]{:S(2)}) collective-permute-start(bf16[128,924]{1,0:T(8,128)(2,1)} %get-tuple-element.18.x_ref), channel_id=1, source_target_pairs={{0,32},{32,0},{64,96},{96,64},{128,160},{160,128},{192,224},{224,1... | collective-permute-start | bytes 709640 | tf_op jit(solution)/shard_map/ppermute | solution.py:271
  4.8 8.7 %all-to-all-start = ((bf16[4,32,1024]{2,1,0:T(8,128)(2,1)}), bf16[4,32,1024]{2,1,0:T(8,128)(2,1)S(1)}, u32[]{:S(2)}, u32[]{:S(2)}) async-start(bf16[4,32,1024]{2,1,0:T(8,128)(2,1)} %get-tuple-element.19), calls=%async_computation | async-start | bytes 524288 | tf_op jit(solution)/shard_map/all_to_all | solution.py:339
  14.5 1.6 %collective-permute-start.1 = (bf16[256,924]{1,0:T(8,128)(2,1)S(1)}, bf16[256,924]{1,0:T(8,128)(2,1)S(1)}, u32[]{:S(2)}, u32[]{:S(2)}) collective-permute-start(bf16[256,924]{1,0:T(8,128)(2,1)S(1)} %shard_map.103._.refs_0_), channel_id=1, source_target_pairs={{0,64},{32,96},{64,128},{96,160},{128,192},{160,224},{192,0},{224,... | collective-permute-start | bytes 1419272 | tf_op jit(solution)/shard_map/ppermute | solution.py:276
  16.1 1.7 %collective-permute-start.2 = (bf16[256,924]{1,0:T(8,128)(2,1)S(1)}, bf16[256,924]{1,0:T(8,128)(2,1)S(1)}, u32[]{:S(2)}, u32[]{:S(2)}) collective-permute-start(bf16[256,924]{1,0:T(8,128)(2,1)S(1)} %shard_map.103._.refs_0_), channel_id=1, source_target_pairs={{0,192},{32,224},{64,0},{96,32},{128,64},{160,96},{192,128},{224,1... | collective-permute-start | bytes 1419272 | tf_op jit(solution)/shard_map/ppermute | solution.py:276
  17.8 1.8 %collective-permute-start.3 = (bf16[256,924]{1,0:T(8,128)(2,1)S(1)}, bf16[256,924]{1,0:T(8,128)(2,1)S(1)}, u32[]{:S(2)}, u32[]{:S(2)}) collective-permute-start(bf16[256,924]{1,0:T(8,128)(2,1)S(1)} %shard_map.103._.refs_0_), channel_id=1, source_target_pairs={{0,128},{32,160},{64,192},{96,224},{128,0},{160,32},{192,64},{224,... | collective-permute-start | bytes 1419272 | tf_op jit(solution)/shard_map/ppermute | solution.py:276
  19.6 4.8 %all-to-all-done.far_ref = bf16[4,32,1024]{2,1,0:T(8,128)(2,1)S(1)} async-done(((bf16[4,32,1024]{2,1,0:T(8,128)(2,1)}), bf16[4,32,1024]{2,1,0:T(8,128)(2,1)S(1)}, u32[]{:S(2)}, u32[]{:S(2)}) %all-to-all-start) | async-done | bytes 262176 | tf_op jit(solution)/shard_map/all_to_all | solution.py:339
  24.4 4.0 %collective-permute-start.6 = (bf16[32,1024]{1,0:T(8,128)(2,1)S(1)}, bf16[32,1024]{1,0:T(8,128)(2,1)S(1)}, u32[]{:S(2)}, u32[]{:S(2)}) collective-permute-start(bf16[32,1024]{1,0:T(8,128)(2,1)S(1)} %get-tuple-element.21), channel_id=1, source_target_pairs={{0,8},{4,12},{8,16},{12,20},{16,24},{20,28},{24,0},{28,4},{1,9},{5... | collective-permute-start | bytes 196616 | tf_op jit(solution)/shard_map/ppermute | solution.py:54
  28.7 2.7 %collective-permute-done.6.prev2_ref = bf16[32,1024]{1,0:T(8,128)(2,1)S(1)} collective-permute-done((bf16[32,1024]{1,0:T(8,128)(2,1)S(1)}, bf16[32,1024]{1,0:T(8,128)(2,1)S(1)}, u32[]{:S(2)}, u32[]{:S(2)}) %collective-permute-start.6) | collective-permute-done | bytes 65568 | tf_op jit(solution)/shard_map/ppermute | solution.py:54
  31.4 3.6 %collective-permute-start.4 = (bf16[64,1024]{1,0:T(8,128)(2,1)S(1)}, bf16[64,1024]{1,0:T(8,128)(2,1)S(1)}, u32[]{:S(2)}, u32[]{:S(2)}) collective-permute-start(bf16[64,1024]{1,0:T(8,128)(2,1)S(1)} %get-tuple-element.20.four_ref), channel_id=1, source_target_pairs={{0,4},{4,8},{8,12},{12,16},{16,20},{20,24},{24,28},{28,0},{1,5},{5... | collective-permute-start | bytes 393224 | tf_op jit(solution)/shard_map/ppermute | solution.py:56
  34.9 3.0 %collective-permute-start.5 = (bf16[64,1024]{1,0:T(8,128)(2,1)S(1)}, bf16[64,1024]{1,0:T(8,128)(2,1)S(1)}, u32[]{:S(2)}, u32[]{:S(2)}) collective-permute-start(bf16[64,1024]{1,0:T(8,128)(2,1)S(1)} %get-tuple-element.20.four_ref), channel_id=1, source_target_pairs={{0,28},{4,0},{8,4},{12,8},{16,12},{20,16},{24,20},{28,24},{1,29},{... | collective-permute-start | bytes 393224 | tf_op jit(solution)/shard_map/ppermute | solution.py:57
  37.9 2.5 %collective-permute-done.5.next_ref = bf16[64,1024]{1,0:T(8,128)(2,1)S(1)} collective-permute-done((bf16[64,1024]{1,0:T(8,128)(2,1)S(1)}, bf16[64,1024]{1,0:T(8,128)(2,1)S(1)}, u32[]{:S(2)}, u32[]{:S(2)}) %collective-permute-start.5) | collective-permute-done | bytes 131104 | tf_op jit(solution)/shard_map/ppermute | solution.py:57
  41.3 1.9 %collective-permute-done.8.other_ref = bf16[256,1024]{1,0:T(8,128)(2,1)S(1)} collective-permute-done((bf16[256,1024]{1,0:T(8,128)(2,1)S(1)}, bf16[256,1024]{1,0:T(8,128)(2,1)S(1)}, u32[]{:S(2)}, u32[]{:S(2)}) %collective-permute-start.8) | collective-permute-done | bytes 524320 | tf_op jit(solution)/shard_map/ppermute | solution.py:62
  43.2 2.3 %shard_map.106 = (bf16[512,1024]{1,0:T(8,128)(2,1)S(1)}, bf16[8,64,924]{2,1,0:T(8,128)(2,1)}) custom-call(bf16[256,1024]{1,0:T(8,128)(2,1)S(1)} %shard_map.105.mine_ref, bf16[256,1024]{1,0:T(8,128)(2,1)S(1)} %collective-permute-done.8.other_ref, bf16[924,1024]{1,0:T(8,128)(2,1)S(1)} %copy-done.2), custom_call_target="tpu_custom_call" | custom-call | tf_op jit(solution)/shard_map/pallas_call | solution.py:188
  45.5 1.0 copy-done.4
  46.4 6.0 %all-to-all-start.1 = ((bf16[8,64,924]{2,1,0:T(8,128)(2,1)}), bf16[8,64,924]{2,1,0:T(8,128)(2,1)}, u32[]{:S(2)}, u32[]{:S(2)}) async-start(bf16[8,64,924]{2,1,0:T(8,128)(2,1)} %get-tuple-element.22), calls=%async_computation.1 | async-start | bytes 2097152 | tf_op jit(solution)/shard_map/all_to_all | solution.py:345
  52.4 1.0 collective-permute-start.9
  53.4 3.3 %collective-permute-start.10 = (bf16[64,1024]{1,0:T(8,128)(2,1)S(1)}, bf16[64,1024]{1,0:T(8,128)(2,1)S(1)}, u32[]{:S(2)}, u32[]{:S(2)}) collective-permute-start(bf16[64,1024]{1,0:T(8,128)(2,1)S(1)} %get-tuple-element.23.four_ref), channel_id=1, source_target_pairs={{0,28},{4,0},{8,4},{12,8},{16,12},{20,16},{24,20},{28,24},{1,29},{... | collective-permute-start | bytes 393224 | tf_op jit(solution)/shard_map/ppermute | solution.py:57
  56.7 4.1 %collective-permute-start.12 = (bf16[32,1024]{1,0:T(8,128)(2,1)S(1)}, bf16[32,1024]{1,0:T(8,128)(2,1)S(1)}, u32[]{:S(2)}, u32[]{:S(2)}) collective-permute-start(bf16[32,1024]{1,0:T(8,128)(2,1)S(1)} %get-tuple-element.24), channel_id=1, source_target_pairs={{0,24},{4,28},{8,0},{12,4},{16,8},{20,12},{24,16},{28,20},{1,25},{... | collective-permute-start | bytes 196616 | tf_op jit(solution)/shard_map/ppermute | solution.py:55
  60.9 2.8 %collective-permute-done.11.prev2_ref = bf16[32,1024]{1,0:T(8,128)(2,1)S(1)} collective-permute-done((bf16[32,1024]{1,0:T(8,128)(2,1)S(1)}, bf16[32,1024]{1,0:T(8,128)(2,1)S(1)}, u32[]{:S(2)}, u32[]{:S(2)}) %collective-permute-start.11) | collective-permute-done | bytes 65568 | tf_op jit(solution)/shard_map/ppermute | solution.py:54
  64.5 3.8 %all-to-all-done.1.parts_ref = bf16[8,64,924]{2,1,0:T(8,128)(2,1)} async-done(((bf16[8,64,924]{2,1,0:T(8,128)(2,1)}), bf16[8,64,924]{2,1,0:T(8,128)(2,1)}, u32[]{:S(2)}, u32[]{:S(2)}) %all-to-all-start.1) | async-done | bytes 946208 | tf_op jit(solution)/shard_map/all_to_all | solution.py:345
  68.3 1.5 %shard_map.108 = bf16[8,64,924]{2,1,0:T(8,128)(2,1)S(1)} custom-call(bf16[8,64,924]{2,1,0:T(8,128)(2,1)} %all-to-all-done.1.parts_ref, bf16[256,1024]{1,0:T(8,128)(2,1)S(1)} %shard_map.107.refs_0_.mine_ref), custom_call_target="tpu_custom_call" | custom-call | tf_op jit(solution)/shard_map/pallas_call | solution.py:211
  69.8 18.1 %all_to_all.20.refs_4_ = bf16[8,64,924]{2,1,0:T(8,128)(2,1)S(1)} all-to-all(bf16[8,64,924]{2,1,0:T(8,128)(2,1)S(1)} %shard_map.108), channel_id=1, replica_groups=mesh['gx'=8,'gy'=8,'gz'=4] {'gx'}, dimensions={0} | all-to-all | bytes 1892352 | tf_op jit(solution)/shard_map/all_to_all | solution.py:347
  87.9 1.4 %shard_map.109 = (f32[8,32,1024]{2,1,0:T(8,128)S(1)}, bf16[2,8,32,924]{3,2,1,0:T(8,128)(2,1)S(1)}, bf16[2,8,32,924]{3,2,1,0:T(8,128)(2,1)S(1)}) custom-call(bf16[256,924]{1,0:T(8,128)(2,1)S(1)} %shard_map.103._.refs_0_, bf16[256,924]{1,0:T(8,128)(2,1)S(1)} %collective-permute-done.1.refs_0_.refs_1_, ...), custom_call_target="tpu_custom_call" | custom-call | tf_op jit(solution)/shard_map/pallas_call | solution.py:328
  90.0 1.6 %shard_map.110 = (f32[8,32,1024]{2,1,0:T(8,128)S(1)}, bf16[2,8,32,924]{3,2,1,0:T(8,128)(2,1)S(1)}, bf16[2,8,32,924]{3,2,1,0:T(8,128)(2,1)S(1)}) custom-call(bf16[256,924]{1,0:T(8,128)(2,1)S(1)} %shard_map.103._.refs_0_, bf16[256,924]{1,0:T(8,128)(2,1)S(1)} %collective-permute-done.1.refs_0_.refs_1_, ...), custom_call_target="tpu_custom_call" | custom-call | tf_op jit(solution)/shard_map/pallas_call | solution.py:328
  91.6 1.0 collective-permute-done.13
  93.5 8.9 %all-to-all-start.3 = ((bf16[16,16,1024]{2,1,0:T(8,128)(2,1)}), bf16[16,16,1024]{2,1,0:T(8,128)(2,1)S(1)}, u32[]{:S(2)}, u32[]{:S(2)}) async-start(bf16[16,16,1024]{2,1,0:T(8,128)(2,1)} %bitcast.19), calls=%async_computation.3 | async-start | bytes 1048576 | tf_op jit(solution)/shard_map/all_to_all | solution.py:354
  102.9 1.1 shard_map.112
  104.1 2.4 %convolution_convert_fusion = bf16[924,1024]{1,0:T(8,128)(2,1)} fusion(bf16[512,924]{1,0:T(8,128)(2,1)S(1)} %bitcast.16, bf16[512,1024]{1,0:T(8,128)(2,1)S(1)} %copy-done.5), kind=kOutput, calls=%fused_computation | convolution fusion | flops 969830400 | bytes 3887104 | tf_op jit(solution)/shard_map/dot_general | solution.py:361
  106.5 2.4 %convolution_convert_fusion.2 = bf16[1024,924]{0,1:T(8,128)(2,1)} fusion(bf16[512,1024]{1,0:T(8,128)(2,1)S(1)} %shard_map.112, bf16[512,924]{1,0:T(8,128)(2,1)S(1)} %bitcast.18), kind=kOutput, calls=%fused_computation.2 | convolution fusion | flops 969830400 | bytes 3887104 | tf_op jit(solution)/shard_map/dot_general | solution.py:359
  109.0 2.4 %convolution_convert_fusion.1 = bf16[1024,924]{0,1:T(8,128)(2,1)} fusion(bf16[512,1024]{1,0:T(8,128)(2,1)S(1)} %shard_map.112, bf16[512,924]{1,0:T(8,128)(2,1)S(1)} %bitcast.17), kind=kOutput, calls=%fused_computation.1 | convolution fusion | flops 969830400 | bytes 3887104 | tf_op jit(solution)/shard_map/dot_general | solution.py:360
  111.4 10.4 %all-to-all-done.3.parts_ref = bf16[16,16,1024]{2,1,0:T(8,128)(2,1)S(1)} async-done(((bf16[16,16,1024]{2,1,0:T(8,128)(2,1)}), bf16[16,16,1024]{2,1,0:T(8,128)(2,1)S(1)}, u32[]{:S(2)}, u32[]{:S(2)}) %all-to-all-start.3) | async-done | bytes 524320 | tf_op jit(solution)/shard_map/all_to_all | solution.py:354
  (41 shorter events, 5.7 us)
Async XLA Ops:
  2.5 11.0 %collective-permute-start = (bf16[128,924]{1,0:T(8,128)(2,1)}, bf16[128,924]{1,0:T(8,128)(2,1)S(1)}, u32[]{:S(2)}, u32[]{:S(2)}) collective-permute-start(bf16[128,924]{1,0:T(8,128)(2,1)} %get-tuple-element.18.x_ref), channel_id=1, source_target_pairs={{0,32},{32,0},{64,96},{96,64},{128,160},{160,128},{192,224},{224,1... | collective-permute-start | bytes 709640 | tf_op jit(solution)/shard_map/ppermute | solution.py:271
  4.8 19.6 %all-to-all-start = ((bf16[4,32,1024]{2,1,0:T(8,128)(2,1)}), bf16[4,32,1024]{2,1,0:T(8,128)(2,1)S(1)}, u32[]{:S(2)}, u32[]{:S(2)}) async-start(bf16[4,32,1024]{2,1,0:T(8,128)(2,1)} %get-tuple-element.19), calls=%async_computation | async-start | bytes 524288 | tf_op jit(solution)/shard_map/all_to_all | solution.py:339
  13.5 1.0 copy-start.3
  14.5 26.0 %collective-permute-start.1 = (bf16[256,924]{1,0:T(8,128)(2,1)S(1)}, bf16[256,924]{1,0:T(8,128)(2,1)S(1)}, u32[]{:S(2)}, u32[]{:S(2)}) collective-permute-start(bf16[256,924]{1,0:T(8,128)(2,1)S(1)} %shard_map.103._.refs_0_), channel_id=1, source_target_pairs={{0,64},{32,96},{64,128},{96,160},{128,192},{160,224},{192,0},{224,... | collective-permute-start | bytes 1419272 | tf_op jit(solution)/shard_map/ppermute | solution.py:276
  16.1 24.4 %collective-permute-start.2 = (bf16[256,924]{1,0:T(8,128)(2,1)S(1)}, bf16[256,924]{1,0:T(8,128)(2,1)S(1)}, u32[]{:S(2)}, u32[]{:S(2)}) collective-permute-start(bf16[256,924]{1,0:T(8,128)(2,1)S(1)} %shard_map.103._.refs_0_), channel_id=1, source_target_pairs={{0,192},{32,224},{64,0},{96,32},{128,64},{160,96},{192,128},{224,1... | collective-permute-start | bytes 1419272 | tf_op jit(solution)/shard_map/ppermute | solution.py:276
  17.8 23.3 %collective-permute-start.3 = (bf16[256,924]{1,0:T(8,128)(2,1)S(1)}, bf16[256,924]{1,0:T(8,128)(2,1)S(1)}, u32[]{:S(2)}, u32[]{:S(2)}) collective-permute-start(bf16[256,924]{1,0:T(8,128)(2,1)S(1)} %shard_map.103._.refs_0_), channel_id=1, source_target_pairs={{0,128},{32,160},{64,192},{96,224},{128,0},{160,32},{192,64},{224,... | collective-permute-start | bytes 1419272 | tf_op jit(solution)/shard_map/ppermute | solution.py:276
  24.4 18.7 %copy-start.2 = (bf16[924,1024]{1,0:T(8,128)(2,1)S(1)}, bf16[924,1024]{1,0:T(8,128)(2,1)}, u32[]{:S(2)}) copy-start(bf16[924,1024]{1,0:T(8,128)(2,1)} %weight_ref.1) | copy-start | bytes 5677060
  24.4 6.9 %collective-permute-start.6 = (bf16[32,1024]{1,0:T(8,128)(2,1)S(1)}, bf16[32,1024]{1,0:T(8,128)(2,1)S(1)}, u32[]{:S(2)}, u32[]{:S(2)}) collective-permute-start(bf16[32,1024]{1,0:T(8,128)(2,1)S(1)} %get-tuple-element.21), channel_id=1, source_target_pairs={{0,8},{4,12},{8,16},{12,20},{16,24},{20,28},{24,0},{28,4},{1,9},{5... | collective-permute-start | bytes 196616 | tf_op jit(solution)/shard_map/ppermute | solution.py:54
  28.4 6.5 %collective-permute-start.7 = (bf16[32,1024]{1,0:T(8,128)(2,1)S(1)}, bf16[32,1024]{1,0:T(8,128)(2,1)S(1)}, u32[]{:S(2)}, u32[]{:S(2)}) collective-permute-start(bf16[32,1024]{1,0:T(8,128)(2,1)S(1)} %get-tuple-element.21), channel_id=1, source_target_pairs={{0,24},{4,28},{8,0},{12,4},{16,8},{20,12},{24,16},{28,20},{1,25},{... | collective-permute-start | bytes 196616 | tf_op jit(solution)/shard_map/ppermute | solution.py:55
  31.4 6.6 %collective-permute-start.4 = (bf16[64,1024]{1,0:T(8,128)(2,1)S(1)}, bf16[64,1024]{1,0:T(8,128)(2,1)S(1)}, u32[]{:S(2)}, u32[]{:S(2)}) collective-permute-start(bf16[64,1024]{1,0:T(8,128)(2,1)S(1)} %get-tuple-element.20.four_ref), channel_id=1, source_target_pairs={{0,4},{4,8},{8,12},{12,16},{16,20},{20,24},{24,28},{28,0},{1,5},{5... | collective-permute-start | bytes 393224 | tf_op jit(solution)/shard_map/ppermute | solution.py:56
  34.9 5.5 %collective-permute-start.5 = (bf16[64,1024]{1,0:T(8,128)(2,1)S(1)}, bf16[64,1024]{1,0:T(8,128)(2,1)S(1)}, u32[]{:S(2)}, u32[]{:S(2)}) collective-permute-start(bf16[64,1024]{1,0:T(8,128)(2,1)S(1)} %get-tuple-element.20.four_ref), channel_id=1, source_target_pairs={{0,28},{4,0},{8,4},{12,8},{16,12},{20,16},{24,20},{28,24},{1,29},{... | collective-permute-start | bytes 393224 | tf_op jit(solution)/shard_map/ppermute | solution.py:57
  41.2 2.0 %collective-permute-start.8 = (bf16[256,1024]{1,0:T(8,128)(2,1)S(1)}, bf16[256,1024]{1,0:T(8,128)(2,1)S(1)}, u32[]{:S(2)}, u32[]{:S(2)}) collective-permute-start(bf16[256,1024]{1,0:T(8,128)(2,1)S(1)} %shard_map.105.mine_ref), channel_id=1, source_target_pairs={{0,1},{1,0},{2,3},{3,2},{4,5},{5,4},{6,7},{7,6},{8,9},{9,8},{10,11... | collective-permute-start | bytes 1572872 | tf_op jit(solution)/shard_map/ppermute | solution.py:62
  45.5 1.0 copy-start.4
  46.4 21.9 %all-to-all-start.1 = ((bf16[8,64,924]{2,1,0:T(8,128)(2,1)}), bf16[8,64,924]{2,1,0:T(8,128)(2,1)}, u32[]{:S(2)}, u32[]{:S(2)}) async-start(bf16[8,64,924]{2,1,0:T(8,128)(2,1)} %get-tuple-element.22), calls=%async_computation.1 | async-start | bytes 2097152 | tf_op jit(solution)/shard_map/all_to_all | solution.py:345
  52.4 12.1 %collective-permute-start.9 = (bf16[64,1024]{1,0:T(8,128)(2,1)S(1)}, bf16[64,1024]{1,0:T(8,128)(2,1)S(1)}, u32[]{:S(2)}, u32[]{:S(2)}) collective-permute-start(bf16[64,1024]{1,0:T(8,128)(2,1)S(1)} %get-tuple-element.23.four_ref), channel_id=1, source_target_pairs={{0,4},{4,8},{8,12},{12,16},{16,20},{20,24},{24,28},{28,0},{1,5},{5... | collective-permute-start | bytes 393224 | tf_op jit(solution)/shard_map/ppermute | solution.py:56
  53.4 11.1 %collective-permute-start.10 = (bf16[64,1024]{1,0:T(8,128)(2,1)S(1)}, bf16[64,1024]{1,0:T(8,128)(2,1)S(1)}, u32[]{:S(2)}, u32[]{:S(2)}) collective-permute-start(bf16[64,1024]{1,0:T(8,128)(2,1)S(1)} %get-tuple-element.23.four_ref), channel_id=1, source_target_pairs={{0,28},{4,0},{8,4},{12,8},{16,12},{20,16},{24,20},{28,24},{1,29},{... | collective-permute-start | bytes 393224 | tf_op jit(solution)/shard_map/ppermute | solution.py:57
  56.7 6.9 %collective-permute-start.11 = (bf16[32,1024]{1,0:T(8,128)(2,1)S(1)}, bf16[32,1024]{1,0:T(8,128)(2,1)S(1)}, u32[]{:S(2)}, u32[]{:S(2)}) collective-permute-start(bf16[32,1024]{1,0:T(8,128)(2,1)S(1)} %get-tuple-element.24), channel_id=1, source_target_pairs={{0,8},{4,12},{8,16},{12,20},{16,24},{20,28},{24,0},{28,4},{1,9},{5... | collective-permute-start | bytes 196616 | tf_op jit(solution)/shard_map/ppermute | solution.py:54
  56.7 7.8 %collective-permute-start.12 = (bf16[32,1024]{1,0:T(8,128)(2,1)S(1)}, bf16[32,1024]{1,0:T(8,128)(2,1)S(1)}, u32[]{:S(2)}, u32[]{:S(2)}) collective-permute-start(bf16[32,1024]{1,0:T(8,128)(2,1)S(1)} %get-tuple-element.24), channel_id=1, source_target_pairs={{0,24},{4,28},{8,0},{12,4},{16,8},{20,12},{24,16},{28,20},{1,25},{... | collective-permute-start | bytes 196616 | tf_op jit(solution)/shard_map/ppermute | solution.py:55
  68.3 19.6 %copy-start = (bf16[1024,924]{0,1:T(8,128)(2,1)S(1)}, bf16[1024,924]{0,1:T(8,128)(2,1)}, u32[]{:S(2)}) copy-start(bf16[1024,924]{0,1:T(8,128)(2,1)} %param.11) | copy-start | bytes 5677060
  68.3 19.6 %copy-start.1 = (bf16[1024,924]{0,1:T(8,128)(2,1)S(1)}, bf16[1024,924]{0,1:T(8,128)(2,1)}, u32[]{:S(2)}) copy-start(bf16[1024,924]{0,1:T(8,128)(2,1)} %param.12) | copy-start | bytes 5677060
  89.4 3.2 %collective-permute-start.13 = (f32[8,32,1024]{2,1,0:T(8,128)S(1)}, f32[8,32,1024]{2,1,0:T(8,128)S(1)}, u32[]{:S(2)}, u32[]{:S(2)}) collective-permute-start(f32[8,32,1024]{2,1,0:T(8,128)S(1)} %get-tuple-element.28), channel_id=1, source_target_pairs={{0,1},{1,0},{2,3},{3,2},{4,5},{5,4},{6,7},{7,6},{8,9},{9,8},{10,11... | collective-permute-start | bytes 3145736 | tf_op jit(solution)/shard_map/ppermute | solution.py:62
  89.5 13.4 %collective-permute-start.14 = (bf16[256,1024]{1,0:T(8,128)(2,1)S(1)}, bf16[256,1024]{1,0:T(8,128)(2,1)}, u32[]{:S(2)}, u32[]{:S(2)}) collective-permute-start(bf16[256,1024]{1,0:T(8,128)(2,1)S(1)} %shard_map.107.refs_0_.mine_ref), channel_id=1, source_target_pairs={{0,1},{1,0},{2,3},{3,2},{4,5},{5,4},{6,7},{7,6},{8,9},{9,8},{10,11... | collective-permute-start | bytes 1572872 | tf_op jit(solution)/shard_map/ppermute | solution.py:62
  91.5 2.0 %copy-start.6 = (bf16[2,8,32,924]{3,2,1,0:T(8,128)(2,1)}, bf16[2,8,32,924]{3,2,1,0:T(8,128)(2,1)S(1)}, u32[]{:S(2)}) copy-start(bf16[2,8,32,924]{3,2,1,0:T(8,128)(2,1)S(1)} %get-tuple-element.30) | copy-start | bytes 2838532
  91.6 2.0 %copy-start.8 = (bf16[2,8,32,924]{3,2,1,0:T(8,128)(2,1)}, bf16[2,8,32,924]{3,2,1,0:T(8,128)(2,1)S(1)}, u32[]{:S(2)}) copy-start(bf16[2,8,32,924]{3,2,1,0:T(8,128)(2,1)S(1)} %get-tuple-element.29) | copy-start | bytes 2838532
  93.5 28.3 %all-to-all-start.3 = ((bf16[16,16,1024]{2,1,0:T(8,128)(2,1)}), bf16[16,16,1024]{2,1,0:T(8,128)(2,1)S(1)}, u32[]{:S(2)}, u32[]{:S(2)}) async-start(bf16[16,16,1024]{2,1,0:T(8,128)(2,1)} %bitcast.19), calls=%async_computation.3 | async-start | bytes 1048576 | tf_op jit(solution)/shard_map/all_to_all | solution.py:354
  102.4 1.6 %copy-start.5 = (bf16[512,1024]{1,0:T(8,128)(2,1)S(1)}, bf16[512,1024]{1,0:T(8,128)(2,1)}, u32[]{:S(2)}) copy-start(bf16[512,1024]{1,0:T(8,128)(2,1)} %copy-done.4) | copy-start | bytes 3145732
  104.0 2.5 %copy-start.9 = (bf16[2,8,32,924]{3,2,1,0:T(8,128)(2,1)S(1)}, bf16[2,8,32,924]{3,2,1,0:T(8,128)(2,1)}, u32[]{:S(2)}) copy-start(bf16[2,8,32,924]{3,2,1,0:T(8,128)(2,1)} %copy-done.8) | copy-start | bytes 2838532
  106.5 2.5 %copy-start.7 = (bf16[2,8,32,924]{3,2,1,0:T(8,128)(2,1)S(1)}, bf16[2,8,32,924]{3,2,1,0:T(8,128)(2,1)}, u32[]{:S(2)}) copy-start(bf16[2,8,32,924]{3,2,1,0:T(8,128)(2,1)} %copy-done.6) | copy-start | bytes 2838532

commit v5 on v4

--- a/solution.py
+++ b/solution.py
@@ -318,12 +318,12 @@
         jnp.concatenate(gate_grads, axis=0), gw_ref[...], preferred_element_type=F32
     ) + jnp.dot(jnp.concatenate(up_grads, axis=0), uw_ref[...], preferred_element_type=F32)
     for j, block in enumerate(places):
-        part_ref[block] = part[j * half : (j + 1) * half, :]
+        part_ref[block] = part[j * half : (j + 1) * half, :].astype(part_ref.dtype)
 
 
 def input_part(k, hidden_grad, pieces, gate_weight, up_weight, grads):
     blocks, rows, units = hidden_grad.shape
-    half = jax.ShapeDtypeStruct((blocks, rows // 2, gate_weight.shape[1]), F32)
+    half = jax.ShapeDtypeStruct((blocks, rows // 2, gate_weight.shape[1]), BF16 if k else F32)
     grad = jax.ShapeDtypeStruct((2, blocks, rows // 2, units), BF16)
     return pl.pallas_call(
         functools.partial(input_kernel, k),
@@ -350,7 +350,7 @@
     keep, gate_grad, up_grad = input_part(
         0, hidden_grad, pieces, *weights, [gate_grad, up_grad]
     )
-    total = (keep + swap_core(send)).astype(BF16).reshape(16, ROWS, -1)
+    total = (keep + swap_core(send).astype(F32)).astype(BF16).reshape(16, ROWS, -1)
     totals = lax.all_to_all(total, ("gy", "gz"), 0, 0, axis_index_groups=SAME_CORE)
     input_sum = last_sum(totals)
     hidden = hidden_rows(pieces)

time: 123 us -> 122 us (level)
  transfers between devices with their start and end apart: 18 -> 18, of which waited for: 10 -> 9; matrix products, arithmetic and copies ran while one was open for 7% -> 7% of each run, Pallas kernels for 3% -> 3%
where the time goes in v5:
time: 122 us
  starting transfers between devices  50.9 us (42%)
  waiting for transfers between devices  30.4 us (25%)
  blocking collectives  18.1 us (15%)
  Pallas kernels  11.1 us (9%)
  matrix products  7.34 us (6%)
  local copies, waits for them, and re-layouts  2.27 us (2%)
    all_to_all x1, blocking collectives, body(): hidden_grad = lax.all_to_all(sum_copies(parts, [mine_in]), 'gx', 0, 0)  18.1 us
    all_to_all x1, waiting for transfers between devices, body(): lax.all_to_all(total, ('gy', 'gz'), 0, 0, axis_index_groups=SAME_CORE)  10.4 us
    all_to_all x1, starting transfers between devices, body(): lax.all_to_all(total, ('gy', 'gz'), 0, 0, axis_index_groups=SAME_CORE)  8.88 us
    all_to_all x1, starting transfers between devices, body(): lax.all_to_all(copies, ('gy', 'gz'), 0, 0, axis_index_groups=FAR_PLACES)  8.75 us
    ppermute x2, starting transfers between devices, near_places(): lax.ppermute(four, 'gy', gy_shift(-1))  6.29 us
    all_to_all x1, starting transfers between devices, body(): parts = lax.all_to_all(part, 'gx', 0, 0)  5.98 us
    ppermute x2, waiting for transfers between devices, near_places(): lax.ppermute(near, 'gy', gy_shift(2))  5.48 us
    ppermute x3, starting transfers between devices, along_x(): lax.ppermute(pair, 'gx', [(i, (i + step) % 8) for i in range(8)])  5.13 us
  transfers between devices with their start and end apart: 18, of which 9 were waited for; matrix products, arithmetic and copies ran while one was open for 7% of the time, Pallas kernels for 3%

profile of v5, /device:TPU:8, one launch (start us, length us, event | category | flops | bytes accessed | tf_op | source)
XLA Modules:
  0.0 122.0 jit_solution(8857305074611007690)
XLA Ops:
  0.6 1.9 %shard_map.102 = (bf16[4,32,1024]{2,1,0:T(8,128)(2,1)}, bf16[128,924]{1,0:T(8,128)(2,1)}) custom-call(bf16[16,1024]{1,0:T(8,128)(2,1)} %refs_0_.1, bf16[16,1024]{1,0:T(8,128)(2,1)} %refs_1_.1, bf16[64,924]{1,0:T(8,128)(2,1)} %refs_2_.1, bf16[64,924]{1,0:T(8,128)(2,1)} %refs_3_.1), custom_call_target="tpu_custom_call" | custom-call | tf_op jit(solution)/shard_map/pallas_call | solution.py:89
  2.5 2.3 %collective-permute-start = (bf16[128,924]{1,0:T(8,128)(2,1)}, bf16[128,924]{1,0:T(8,128)(2,1)S(1)}, u32[]{:S(2)}, u32[]{:S(2)}) collective-permute-start(bf16[128,924]{1,0:T(8,128)(2,1)} %get-tuple-element.18.x_ref), channel_id=1, source_target_pairs={{0,32},{32,0},{64,96},{96,64},{128,160},{160,128},{192,224},{224,1... | collective-permute-start | bytes 709640 | tf_op jit(solution)/shard_map/ppermute | solution.py:271
  4.8 8.7 %all-to-all-start = ((bf16[4,32,1024]{2,1,0:T(8,128)(2,1)}), bf16[4,32,1024]{2,1,0:T(8,128)(2,1)S(1)}, u32[]{:S(2)}, u32[]{:S(2)}) async-start(bf16[4,32,1024]{2,1,0:T(8,128)(2,1)} %get-tuple-element.19), calls=%async_computation | async-start | bytes 524288 | tf_op jit(solution)/shard_map/all_to_all | solution.py:339
  14.5 1.6 %collective-permute-start.1 = (bf16[256,924]{1,0:T(8,128)(2,1)S(1)}, bf16[256,924]{1,0:T(8,128)(2,1)S(1)}, u32[]{:S(2)}, u32[]{:S(2)}) collective-permute-start(bf16[256,924]{1,0:T(8,128)(2,1)S(1)} %shard_map.103._.refs_0_), channel_id=1, source_target_pairs={{0,64},{32,96},{64,128},{96,160},{128,192},{160,224},{192,0},{224,... | collective-permute-start | bytes 1419272 | tf_op jit(solution)/shard_map/ppermute | solution.py:276
  16.1 1.7 %collective-permute-start.2 = (bf16[256,924]{1,0:T(8,128)(2,1)S(1)}, bf16[256,924]{1,0:T(8,128)(2,1)S(1)}, u32[]{:S(2)}, u32[]{:S(2)}) collective-permute-start(bf16[256,924]{1,0:T(8,128)(2,1)S(1)} %shard_map.103._.refs_0_), channel_id=1, source_target_pairs={{0,192},{32,224},{64,0},{96,32},{128,64},{160,96},{192,128},{224,1... | collective-permute-start | bytes 1419272 | tf_op jit(solution)/shard_map/ppermute | solution.py:276
  17.8 1.8 %collective-permute-start.3 = (bf16[256,924]{1,0:T(8,128)(2,1)S(1)}, bf16[256,924]{1,0:T(8,128)(2,1)S(1)}, u32[]{:S(2)}, u32[]{:S(2)}) collective-permute-start(bf16[256,924]{1,0:T(8,128)(2,1)S(1)} %shard_map.103._.refs_0_), channel_id=1, source_target_pairs={{0,128},{32,160},{64,192},{96,224},{128,0},{160,32},{192,64},{224,... | collective-permute-start | bytes 1419272 | tf_op jit(solution)/shard_map/ppermute | solution.py:276
  19.6 4.8 %all-to-all-done.far_ref = bf16[4,32,1024]{2,1,0:T(8,128)(2,1)S(1)} async-done(((bf16[4,32,1024]{2,1,0:T(8,128)(2,1)}), bf16[4,32,1024]{2,1,0:T(8,128)(2,1)S(1)}, u32[]{:S(2)}, u32[]{:S(2)}) %all-to-all-start) | async-done | bytes 262176 | tf_op jit(solution)/shard_map/all_to_all | solution.py:339
  24.4 4.0 %collective-permute-start.6 = (bf16[32,1024]{1,0:T(8,128)(2,1)S(1)}, bf16[32,1024]{1,0:T(8,128)(2,1)S(1)}, u32[]{:S(2)}, u32[]{:S(2)}) collective-permute-start(bf16[32,1024]{1,0:T(8,128)(2,1)S(1)} %get-tuple-element.21), channel_id=1, source_target_pairs={{0,8},{4,12},{8,16},{12,20},{16,24},{20,28},{24,0},{28,4},{1,9},{5... | collective-permute-start | bytes 196616 | tf_op jit(solution)/shard_map/ppermute | solution.py:54
  28.7 2.7 %collective-permute-done.6.prev2_ref = bf16[32,1024]{1,0:T(8,128)(2,1)S(1)} collective-permute-done((bf16[32,1024]{1,0:T(8,128)(2,1)S(1)}, bf16[32,1024]{1,0:T(8,128)(2,1)S(1)}, u32[]{:S(2)}, u32[]{:S(2)}) %collective-permute-start.6) | collective-permute-done | bytes 65568 | tf_op jit(solution)/shard_map/ppermute | solution.py:54
  31.4 3.6 %collective-permute-start.4 = (bf16[64,1024]{1,0:T(8,128)(2,1)S(1)}, bf16[64,1024]{1,0:T(8,128)(2,1)S(1)}, u32[]{:S(2)}, u32[]{:S(2)}) collective-permute-start(bf16[64,1024]{1,0:T(8,128)(2,1)S(1)} %get-tuple-element.20.four_ref), channel_id=1, source_target_pairs={{0,4},{4,8},{8,12},{12,16},{16,20},{20,24},{24,28},{28,0},{1,5},{5... | collective-permute-start | bytes 393224 | tf_op jit(solution)/shard_map/ppermute | solution.py:56
  34.9 3.0 %collective-permute-start.5 = (bf16[64,1024]{1,0:T(8,128)(2,1)S(1)}, bf16[64,1024]{1,0:T(8,128)(2,1)S(1)}, u32[]{:S(2)}, u32[]{:S(2)}) collective-permute-start(bf16[64,1024]{1,0:T(8,128)(2,1)S(1)} %get-tuple-element.20.four_ref), channel_id=1, source_target_pairs={{0,28},{4,0},{8,4},{12,8},{16,12},{20,16},{24,20},{28,24},{1,29},{... | collective-permute-start | bytes 393224 | tf_op jit(solution)/shard_map/ppermute | solution.py:57
  37.9 2.5 %collective-permute-done.5.next_ref = bf16[64,1024]{1,0:T(8,128)(2,1)S(1)} collective-permute-done((bf16[64,1024]{1,0:T(8,128)(2,1)S(1)}, bf16[64,1024]{1,0:T(8,128)(2,1)S(1)}, u32[]{:S(2)}, u32[]{:S(2)}) %collective-permute-start.5) | collective-permute-done | bytes 131104 | tf_op jit(solution)/shard_map/ppermute | solution.py:57
  41.3 1.9 %collective-permute-done.8.other_ref = bf16[256,1024]{1,0:T(8,128)(2,1)S(1)} collective-permute-done((bf16[256,1024]{1,0:T(8,128)(2,1)S(1)}, bf16[256,1024]{1,0:T(8,128)(2,1)S(1)}, u32[]{:S(2)}, u32[]{:S(2)}) %collective-permute-start.8) | collective-permute-done | bytes 524320 | tf_op jit(solution)/shard_map/ppermute | solution.py:62
  43.2 2.3 %shard_map.106 = (bf16[512,1024]{1,0:T(8,128)(2,1)S(1)}, bf16[8,64,924]{2,1,0:T(8,128)(2,1)}) custom-call(bf16[256,1024]{1,0:T(8,128)(2,1)S(1)} %shard_map.105.mine_ref, bf16[256,1024]{1,0:T(8,128)(2,1)S(1)} %collective-permute-done.8.other_ref, bf16[924,1024]{1,0:T(8,128)(2,1)S(1)} %copy-done.2), custom_call_target="tpu_custom_call" | custom-call | tf_op jit(solution)/shard_map/pallas_call | solution.py:188
  45.5 1.0 copy-done.4
  46.4 6.0 %all-to-all-start.1 = ((bf16[8,64,924]{2,1,0:T(8,128)(2,1)}), bf16[8,64,924]{2,1,0:T(8,128)(2,1)}, u32[]{:S(2)}, u32[]{:S(2)}) async-start(bf16[8,64,924]{2,1,0:T(8,128)(2,1)} %get-tuple-element.22), calls=%async_computation.1 | async-start | bytes 2097152 | tf_op jit(solution)/shard_map/all_to_all | solution.py:345
  52.4 1.0 collective-permute-start.9
  53.4 3.3 %collective-permute-start.10 = (bf16[64,1024]{1,0:T(8,128)(2,1)S(1)}, bf16[64,1024]{1,0:T(8,128)(2,1)S(1)}, u32[]{:S(2)}, u32[]{:S(2)}) collective-permute-start(bf16[64,1024]{1,0:T(8,128)(2,1)S(1)} %get-tuple-element.23.four_ref), channel_id=1, source_target_pairs={{0,28},{4,0},{8,4},{12,8},{16,12},{20,16},{24,20},{28,24},{1,29},{... | collective-permute-start | bytes 393224 | tf_op jit(solution)/shard_map/ppermute | solution.py:57
  56.7 4.1 %collective-permute-start.12 = (bf16[32,1024]{1,0:T(8,128)(2,1)S(1)}, bf16[32,1024]{1,0:T(8,128)(2,1)S(1)}, u32[]{:S(2)}, u32[]{:S(2)}) collective-permute-start(bf16[32,1024]{1,0:T(8,128)(2,1)S(1)} %get-tuple-element.24), channel_id=1, source_target_pairs={{0,24},{4,28},{8,0},{12,4},{16,8},{20,12},{24,16},{28,20},{1,25},{... | collective-permute-start | bytes 196616 | tf_op jit(solution)/shard_map/ppermute | solution.py:55
  60.9 2.8 %collective-permute-done.11.prev2_ref = bf16[32,1024]{1,0:T(8,128)(2,1)S(1)} collective-permute-done((bf16[32,1024]{1,0:T(8,128)(2,1)S(1)}, bf16[32,1024]{1,0:T(8,128)(2,1)S(1)}, u32[]{:S(2)}, u32[]{:S(2)}) %collective-permute-start.11) | collective-permute-done | bytes 65568 | tf_op jit(solution)/shard_map/ppermute | solution.py:54
  64.5 3.8 %all-to-all-done.1.parts_ref = bf16[8,64,924]{2,1,0:T(8,128)(2,1)} async-done(((bf16[8,64,924]{2,1,0:T(8,128)(2,1)}), bf16[8,64,924]{2,1,0:T(8,128)(2,1)}, u32[]{:S(2)}, u32[]{:S(2)}) %all-to-all-start.1) | async-done | bytes 946208 | tf_op jit(solution)/shard_map/all_to_all | solution.py:345
  68.3 1.5 %shard_map.108 = bf16[8,64,924]{2,1,0:T(8,128)(2,1)S(1)} custom-call(bf16[8,64,924]{2,1,0:T(8,128)(2,1)} %all-to-all-done.1.parts_ref, bf16[256,1024]{1,0:T(8,128)(2,1)S(1)} %shard_map.107.refs_0_.mine_ref), custom_call_target="tpu_custom_call" | custom-call | tf_op jit(solution)/shard_map/pallas_call | solution.py:211
  69.8 18.1 %all_to_all.20.refs_4_ = bf16[8,64,924]{2,1,0:T(8,128)(2,1)S(1)} all-to-all(bf16[8,64,924]{2,1,0:T(8,128)(2,1)S(1)} %shard_map.108), channel_id=1, replica_groups=mesh['gx'=8,'gy'=8,'gz'=4] {'gx'}, dimensions={0} | all-to-all | bytes 1892352 | tf_op jit(solution)/shard_map/all_to_all | solution.py:347
  87.9 1.5 %shard_map.109 = (bf16[8,32,1024]{2,1,0:T(8,128)(2,1)S(1)}, bf16[2,8,32,924]{3,2,1,0:T(8,128)(2,1)S(1)}, bf16[2,8,32,924]{3,2,1,0:T(8,128)(2,1)S(1)}) custom-call(bf16[256,924]{1,0:T(8,128)(2,1)S(1)} %shard_map.103._.refs_0_, bf16[256,924]{1,0:T(8,128)(2,1)S(1)} %collective-permute-done.1.refs_0_.refs_1_, ...), custom_call_target="tpu_custom_call" | custom-call | tf_op jit(solution)/shard_map/pallas_call | solution.py:328
  90.0 1.6 %shard_map.110 = (f32[8,32,1024]{2,1,0:T(8,128)S(1)}, bf16[2,8,32,924]{3,2,1,0:T(8,128)(2,1)S(1)}, bf16[2,8,32,924]{3,2,1,0:T(8,128)(2,1)S(1)}) custom-call(bf16[256,924]{1,0:T(8,128)(2,1)S(1)} %shard_map.103._.refs_0_, bf16[256,924]{1,0:T(8,128)(2,1)S(1)} %collective-permute-done.1.refs_0_.refs_1_, ...), custom_call_target="tpu_custom_call" | custom-call | tf_op jit(solution)/shard_map/pallas_call | solution.py:328
  91.6 1.1 add_convert_fusion
  93.1 8.9 %all-to-all-start.3 = ((bf16[16,16,1024]{2,1,0:T(8,128)(2,1)}), bf16[16,16,1024]{2,1,0:T(8,128)(2,1)S(1)}, u32[]{:S(2)}, u32[]{:S(2)}) async-start(bf16[16,16,1024]{2,1,0:T(8,128)(2,1)} %bitcast.19), calls=%async_computation.3 | async-start | bytes 1048576 | tf_op jit(solution)/shard_map/all_to_all | solution.py:354
  102.4 1.1 shard_map.112
  103.6 2.4 %convolution_convert_fusion = bf16[924,1024]{1,0:T(8,128)(2,1)} fusion(bf16[512,924]{1,0:T(8,128)(2,1)S(1)} %bitcast.16, bf16[512,1024]{1,0:T(8,128)(2,1)S(1)} %copy-done.5), kind=kOutput, calls=%fused_computation | convolution fusion | flops 969830400 | bytes 3887104 | tf_op jit(solution)/shard_map/dot_general | solution.py:361
  106.0 2.4 %convolution_convert_fusion.2 = bf16[1024,924]{0,1:T(8,128)(2,1)} fusion(bf16[512,1024]{1,0:T(8,128)(2,1)S(1)} %shard_map.112, bf16[512,924]{1,0:T(8,128)(2,1)S(1)} %bitcast.18), kind=kOutput, calls=%fused_computation.2 | convolution fusion | flops 969830400 | bytes 3887104 | tf_op jit(solution)/shard_map/dot_general | solution.py:359
  108.5 2.4 %convolution_convert_fusion.1 = bf16[1024,924]{0,1:T(8,128)(2,1)} fusion(bf16[512,1024]{1,0:T(8,128)(2,1)S(1)} %shard_map.112, bf16[512,924]{1,0:T(8,128)(2,1)S(1)} %bitcast.17), kind=kOutput, calls=%fused_computation.1 | convolution fusion | flops 969830400 | bytes 3887104 | tf_op jit(solution)/shard_map/dot_general | solution.py:360
  110.9 10.4 %all-to-all-done.3.parts_ref = bf16[16,16,1024]{2,1,0:T(8,128)(2,1)S(1)} async-done(((bf16[16,16,1024]{2,1,0:T(8,128)(2,1)}), bf16[16,16,1024]{2,1,0:T(8,128)(2,1)S(1)}, u32[]{:S(2)}, u32[]{:S(2)}) %all-to-all-start.3) | async-done | bytes 524320 | tf_op jit(solution)/shard_map/all_to_all | solution.py:354
  (41 shorter events, 5.1 us)
Async XLA Ops:
  2.5 11.0 %collective-permute-start = (bf16[128,924]{1,0:T(8,128)(2,1)}, bf16[128,924]{1,0:T(8,128)(2,1)S(1)}, u32[]{:S(2)}, u32[]{:S(2)}) collective-permute-start(bf16[128,924]{1,0:T(8,128)(2,1)} %get-tuple-element.18.x_ref), channel_id=1, source_target_pairs={{0,32},{32,0},{64,96},{96,64},{128,160},{160,128},{192,224},{224,1... | collective-permute-start | bytes 709640 | tf_op jit(solution)/shard_map/ppermute | solution.py:271
  4.8 19.6 %all-to-all-start = ((bf16[4,32,1024]{2,1,0:T(8,128)(2,1)}), bf16[4,32,1024]{2,1,0:T(8,128)(2,1)S(1)}, u32[]{:S(2)}, u32[]{:S(2)}) async-start(bf16[4,32,1024]{2,1,0:T(8,128)(2,1)} %get-tuple-element.19), calls=%async_computation | async-start | bytes 524288 | tf_op jit(solution)/shard_map/all_to_all | solution.py:339
  13.5 1.0 copy-start.3
  14.5 26.0 %collective-permute-start.1 = (bf16[256,924]{1,0:T(8,128)(2,1)S(1)}, bf16[256,924]{1,0:T(8,128)(2,1)S(1)}, u32[]{:S(2)}, u32[]{:S(2)}) collective-permute-start(bf16[256,924]{1,0:T(8,128)(2,1)S(1)} %shard_map.103._.refs_0_), channel_id=1, source_target_pairs={{0,64},{32,96},{64,128},{96,160},{128,192},{160,224},{192,0},{224,... | collective-permute-start | bytes 1419272 | tf_op jit(solution)/shard_map/ppermute | solution.py:276
  16.1 24.4 %collective-permute-start.2 = (bf16[256,924]{1,0:T(8,128)(2,1)S(1)}, bf16[256,924]{1,0:T(8,128)(2,1)S(1)}, u32[]{:S(2)}, u32[]{:S(2)}) collective-permute-start(bf16[256,924]{1,0:T(8,128)(2,1)S(1)} %shard_map.103._.refs_0_), channel_id=1, source_target_pairs={{0,192},{32,224},{64,0},{96,32},{128,64},{160,96},{192,128},{224,1... | collective-permute-start | bytes 1419272 | tf_op jit(solution)/shard_map/ppermute | solution.py:276
  17.8 23.3 %collective-permute-start.3 = (bf16[256,924]{1,0:T(8,128)(2,1)S(1)}, bf16[256,924]{1,0:T(8,128)(2,1)S(1)}, u32[]{:S(2)}, u32[]{:S(2)}) collective-permute-start(bf16[256,924]{1,0:T(8,128)(2,1)S(1)} %shard_map.103._.refs_0_), channel_id=1, source_target_pairs={{0,128},{32,160},{64,192},{96,224},{128,0},{160,32},{192,64},{224,... | collective-permute-start | bytes 1419272 | tf_op jit(solution)/shard_map/ppermute | solution.py:276
  24.4 18.7 %copy-start.2 = (bf16[924,1024]{1,0:T(8,128)(2,1)S(1)}, bf16[924,1024]{1,0:T(8,128)(2,1)}, u32[]{:S(2)}) copy-start(bf16[924,1024]{1,0:T(8,128)(2,1)} %weight_ref.1) | copy-start | bytes 5677060
  24.4 6.9 %collective-permute-start.6 = (bf16[32,1024]{1,0:T(8,128)(2,1)S(1)}, bf16[32,1024]{1,0:T(8,128)(2,1)S(1)}, u32[]{:S(2)}, u32[]{:S(2)}) collective-permute-start(bf16[32,1024]{1,0:T(8,128)(2,1)S(1)} %get-tuple-element.21), channel_id=1, source_target_pairs={{0,8},{4,12},{8,16},{12,20},{16,24},{20,28},{24,0},{28,4},{1,9},{5... | collective-permute-start | bytes 196616 | tf_op jit(solution)/shard_map/ppermute | solution.py:54
  28.4 6.5 %collective-permute-start.7 = (bf16[32,1024]{1,0:T(8,128)(2,1)S(1)}, bf16[32,1024]{1,0:T(8,128)(2,1)S(1)}, u32[]{:S(2)}, u32[]{:S(2)}) collective-permute-start(bf16[32,1024]{1,0:T(8,128)(2,1)S(1)} %get-tuple-element.21), channel_id=1, source_target_pairs={{0,24},{4,28},{8,0},{12,4},{16,8},{20,12},{24,16},{28,20},{1,25},{... | collective-permute-start | bytes 196616 | tf_op jit(solution)/shard_map/ppermute | solution.py:55
  31.4 6.6 %collective-permute-start.4 = (bf16[64,1024]{1,0:T(8,128)(2,1)S(1)}, bf16[64,1024]{1,0:T(8,128)(2,1)S(1)}, u32[]{:S(2)}, u32[]{:S(2)}) collective-permute-start(bf16[64,1024]{1,0:T(8,128)(2,1)S(1)} %get-tuple-element.20.four_ref), channel_id=1, source_target_pairs={{0,4},{4,8},{8,12},{12,16},{16,20},{20,24},{24,28},{28,0},{1,5},{5... | collective-permute-start | bytes 393224 | tf_op jit(solution)/shard_map/ppermute | solution.py:56
  34.9 5.5 %collective-permute-start.5 = (bf16[64,1024]{1,0:T(8,128)(2,1)S(1)}, bf16[64,1024]{1,0:T(8,128)(2,1)S(1)}, u32[]{:S(2)}, u32[]{:S(2)}) collective-permute-start(bf16[64,1024]{1,0:T(8,128)(2,1)S(1)} %get-tuple-element.20.four_ref), channel_id=1, source_target_pairs={{0,28},{4,0},{8,4},{12,8},{16,12},{20,16},{24,20},{28,24},{1,29},{... | collective-permute-start | bytes 393224 | tf_op jit(solution)/shard_map/ppermute | solution.py:57
  41.2 2.0 %collective-permute-start.8 = (bf16[256,1024]{1,0:T(8,128)(2,1)S(1)}, bf16[256,1024]{1,0:T(8,128)(2,1)S(1)}, u32[]{:S(2)}, u32[]{:S(2)}) collective-permute-start(bf16[256,1024]{1,0:T(8,128)(2,1)S(1)} %shard_map.105.mine_ref), channel_id=1, source_target_pairs={{0,1},{1,0},{2,3},{3,2},{4,5},{5,4},{6,7},{7,6},{8,9},{9,8},{10,11... | collective-permute-start | bytes 1572872 | tf_op jit(solution)/shard_map/ppermute | solution.py:62
  45.5 1.0 copy-start.4
  46.4 21.9 %all-to-all-start.1 = ((bf16[8,64,924]{2,1,0:T(8,128)(2,1)}), bf16[8,64,924]{2,1,0:T(8,128)(2,1)}, u32[]{:S(2)}, u32[]{:S(2)}) async-start(bf16[8,64,924]{2,1,0:T(8,128)(2,1)} %get-tuple-element.22), calls=%async_computation.1 | async-start | bytes 2097152 | tf_op jit(solution)/shard_map/all_to_all | solution.py:345
  52.4 12.1 %collective-permute-start.9 = (bf16[64,1024]{1,0:T(8,128)(2,1)S(1)}, bf16[64,1024]{1,0:T(8,128)(2,1)S(1)}, u32[]{:S(2)}, u32[]{:S(2)}) collective-permute-start(bf16[64,1024]{1,0:T(8,128)(2,1)S(1)} %get-tuple-element.23.four_ref), channel_id=1, source_target_pairs={{0,4},{4,8},{8,12},{12,16},{16,20},{20,24},{24,28},{28,0},{1,5},{5... | collective-permute-start | bytes 393224 | tf_op jit(solution)/shard_map/ppermute | solution.py:56
  53.4 11.1 %collective-permute-start.10 = (bf16[64,1024]{1,0:T(8,128)(2,1)S(1)}, bf16[64,1024]{1,0:T(8,128)(2,1)S(1)}, u32[]{:S(2)}, u32[]{:S(2)}) collective-permute-start(bf16[64,1024]{1,0:T(8,128)(2,1)S(1)} %get-tuple-element.23.four_ref), channel_id=1, source_target_pairs={{0,28},{4,0},{8,4},{12,8},{16,12},{20,16},{24,20},{28,24},{1,29},{... | collective-permute-start | bytes 393224 | tf_op jit(solution)/shard_map/ppermute | solution.py:57
  56.7 6.9 %collective-permute-start.11 = (bf16[32,1024]{1,0:T(8,128)(2,1)S(1)}, bf16[32,1024]{1,0:T(8,128)(2,1)S(1)}, u32[]{:S(2)}, u32[]{:S(2)}) collective-permute-start(bf16[32,1024]{1,0:T(8,128)(2,1)S(1)} %get-tuple-element.24), channel_id=1, source_target_pairs={{0,8},{4,12},{8,16},{12,20},{16,24},{20,28},{24,0},{28,4},{1,9},{5... | collective-permute-start | bytes 196616 | tf_op jit(solution)/shard_map/ppermute | solution.py:54
  56.7 7.8 %collective-permute-start.12 = (bf16[32,1024]{1,0:T(8,128)(2,1)S(1)}, bf16[32,1024]{1,0:T(8,128)(2,1)S(1)}, u32[]{:S(2)}, u32[]{:S(2)}) collective-permute-start(bf16[32,1024]{1,0:T(8,128)(2,1)S(1)} %get-tuple-element.24), channel_id=1, source_target_pairs={{0,24},{4,28},{8,0},{12,4},{16,8},{20,12},{24,16},{28,20},{1,25},{... | collective-permute-start | bytes 196616 | tf_op jit(solution)/shard_map/ppermute | solution.py:55
  68.3 19.6 %copy-start = (bf16[1024,924]{0,1:T(8,128)(2,1)S(1)}, bf16[1024,924]{0,1:T(8,128)(2,1)}, u32[]{:S(2)}) copy-start(bf16[1024,924]{0,1:T(8,128)(2,1)} %param.11) | copy-start | bytes 5677060
  68.3 19.6 %copy-start.1 = (bf16[1024,924]{0,1:T(8,128)(2,1)S(1)}, bf16[1024,924]{0,1:T(8,128)(2,1)}, u32[]{:S(2)}) copy-start(bf16[1024,924]{0,1:T(8,128)(2,1)} %param.12) | copy-start | bytes 5677060
  89.4 2.2 %collective-permute-start.13 = (bf16[8,32,1024]{2,1,0:T(8,128)(2,1)S(1)}, bf16[8,32,1024]{2,1,0:T(8,128)(2,1)S(1)}, u32[]{:S(2)}, u32[]{:S(2)}) collective-permute-start(bf16[8,32,1024]{2,1,0:T(8,128)(2,1)S(1)} %get-tuple-element.28), channel_id=1, source_target_pairs={{0,1},{1,0},{2,3},{3,2},{4,5},{5,4},{6,7},{7,6},{8,9},{9,8},{10,11... | collective-permute-start | bytes 1572872 | tf_op jit(solution)/shard_map/ppermute | solution.py:62
  89.5 12.9 %collective-permute-start.14 = (bf16[256,1024]{1,0:T(8,128)(2,1)S(1)}, bf16[256,1024]{1,0:T(8,128)(2,1)}, u32[]{:S(2)}, u32[]{:S(2)}) collective-permute-start(bf16[256,1024]{1,0:T(8,128)(2,1)S(1)} %shard_map.107.refs_0_.mine_ref), channel_id=1, source_target_pairs={{0,1},{1,0},{2,3},{3,2},{4,5},{5,4},{6,7},{7,6},{8,9},{9,8},{10,11... | collective-permute-start | bytes 1572872 | tf_op jit(solution)/shard_map/ppermute | solution.py:62
  91.6 1.2 copy-start.6
  91.6 1.5 %copy-start.8 = (bf16[2,8,32,924]{3,2,1,0:T(8,128)(2,1)}, bf16[2,8,32,924]{3,2,1,0:T(8,128)(2,1)S(1)}, u32[]{:S(2)}) copy-start(bf16[2,8,32,924]{3,2,1,0:T(8,128)(2,1)S(1)} %get-tuple-element.29) | copy-start | bytes 2838532
  93.1 28.3 %all-to-all-start.3 = ((bf16[16,16,1024]{2,1,0:T(8,128)(2,1)}), bf16[16,16,1024]{2,1,0:T(8,128)(2,1)S(1)}, u32[]{:S(2)}, u32[]{:S(2)}) async-start(bf16[16,16,1024]{2,1,0:T(8,128)(2,1)} %bitcast.19), calls=%async_computation.3 | async-start | bytes 1048576 | tf_op jit(solution)/shard_map/all_to_all | solution.py:354
  102.0 1.6 %copy-start.5 = (bf16[512,1024]{1,0:T(8,128)(2,1)S(1)}, bf16[512,1024]{1,0:T(8,128)(2,1)}, u32[]{:S(2)}) copy-start(bf16[512,1024]{1,0:T(8,128)(2,1)} %copy-done.4) | copy-start | bytes 3145732
  103.6 2.5 %copy-start.9 = (bf16[2,8,32,924]{3,2,1,0:T(8,128)(2,1)S(1)}, bf16[2,8,32,924]{3,2,1,0:T(8,128)(2,1)}, u32[]{:S(2)}) copy-start(bf16[2,8,32,924]{3,2,1,0:T(8,128)(2,1)} %copy-done.8) | copy-start | bytes 2838532
  106.0 2.5 %copy-start.7 = (bf16[2,8,32,924]{3,2,1,0:T(8,128)(2,1)S(1)}, bf16[2,8,32,924]{3,2,1,0:T(8,128)(2,1)}, u32[]{:S(2)}) copy-start(bf16[2,8,32,924]{3,2,1,0:T(8,128)(2,1)} %copy-done.6) | copy-start | bytes 2838532
